TPU v7x, 256 devices: a whole 4x4x8 slice. The times are simulated.
256 devices in a mesh: row: 16 (over y, x), col: 16 (over z, core).
Axes of the slice: x: 4, y: 4, z: 8, core: 2. Of those that a mesh axis runs over, the one named last changes fastest.
Arguments:
- panel: float32 [32768, 512], P('row', 'col'), may hold values from -6 to 6
- trailing: float32 [32768, 8192], P('row', 'col'), may hold values from -6 to 6
Outputs:
- r_factor: float32 [512, 512], P(None, 'col')
- top_rows: float32 [512, 8192], P(None, 'col')
- projected: float32 [32768, 8192], P('row', 'col')
All inputs are finite; a program needn't handle non-finite values.
Results may differ from a plain program's by a relative error of at most 0.0003.
Values sent between devices are 32-bit elements; how exact they have to be, the bound alone decides.
No kernel may reach another device: no remote copies, remote signals or barrier semaphores. Data moves between devices by JAX's collectives and lax.ppermute only.
A program may use at most 64 MiB of HBM per device.

v0:
```python
import jax
import jax.numpy as jnp
from jax import lax
from jax.sharding import PartitionSpec as P


def contract_rows(left, right):
    return lax.dot_general(left, right, (((0,), (0,)), ((), ())), precision=lax.Precision.HIGHEST)


def lower_solve(factor_low, right_side):
    return jax.scipy.linalg.solve_triangular(factor_low, right_side, lower=True)


def on_device(panel, trailing):
    highest = lax.Precision.HIGHEST
    gathered = lax.all_gather(panel, "col", axis=1, tiled=True)
    width = gathered.shape[1]
    local_gram = contract_rows(gathered, gathered)
    gram = lax.psum(local_gram, "row")
    factor_low = jnp.linalg.cholesky(gram)
    orth_rows = lower_solve(factor_low, gathered.T)
    top_rows = lax.psum(jnp.dot(orth_rows, trailing, precision=highest), "row")
    projected = trailing - contract_rows(orth_rows, top_rows)
    r_whole = factor_low.T
    col_width = width // lax.axis_size("col")
    col_index = lax.axis_index("col")
    r_factor = lax.dynamic_slice_in_dim(r_whole, col_index * col_width, col_width, 1)
    return (r_factor, top_rows, projected)


def solution(mesh):
    placed = (P("row", "col"), P("row", "col"))
    return jax.shard_map(
        on_device,
        mesh=mesh,
        in_specs=placed,
        out_specs=(P(None, "col"), P(None, "col"), P("row", "col")),
        check_vma=False,
    )
```

profile of v0, /device:TPU:1, one launch (start us, length us, event | category | flops | bytes accessed | tf_op | source)
XLA Modules:
  0.0 435.3 jit_solution(18013870793459214362)
XLA Ops:
  7.2 0.7 all-gather.2.cloned.1.call-update
  7.9 48.2 %all-gather.2.cloned.1.call-done = f32[2048,512]{0,1:T(8,128)} async-done(((f32[2048,32]{0,1:T(8,128)}), f32[2048,512]{0,1:T(8,128)}) %all-gather.2.cloned.1.call-update) | async-done | bytes 4194320 | tf_op jit(solution)/shard_map/all_gather | solution.py:17
  56.2 10.2 %fusion.39 = f32[512,512]{0,1:T(8,128)} fusion(f32[2048,512]{0,1:T(8,128)} %all-gather.2.cloned.1.call-done), kind=kOutput, calls=%fused_computation.74 | convolution fusion | flops 6442450944 | bytes 5242880 | tf_op jit(solution)/shard_map/dot_general | solution.py:8
  66.4 0.2 all-reduce.6.cloned.1.call-start
  66.7 93.8 %all-reduce.4.cloned.1.call-done = f32[512,512]{0,1:T(8,128)} async-done(((f32[512,512]{0,1:T(8,128)}), f32[512,512]{0,1:T(8,128)}) %all-reduce.4.cloned.1.call-update) | async-done | bytes 1048592 | tf_op jit(solution)/shard_map/psum | solution.py:20
  160.4 1.6 copy.6
  162.0 1.4 fusion.15
  163.5 11.7 %cholesky.104 = f32[128,128]{1,0:T(8,128)S(1)} custom-call(f32[128,128]{1,0:T(8,128)S(1)} %cholesky.266), custom_call_target="Cholesky" | custom-call | tf_op jit(solution)/shard_map/jit(cholesky)/cholesky | solution.py:21
  175.2 9.8 %custom-call.31 = f32[1,128,128]{1,2,0:T(8,128)S(1)} custom-call(f32[1,128,128]{2,1,0:T(8,128)S(1)} %get-tuple-element.32), custom_call_target="InvertDiagBlocksLowerTriangular" | custom-call | tf_op jit(solution)/shard_map/jit(cholesky)/cholesky | solution.py:21
  185.0 0.1 cholesky.224
  185.2 0.3 constant_dynamic-update-slice_fusion.3
  185.5 0.3 convolution_subtract_fusion.3
  185.8 11.7 %cholesky.217 = f32[128,128]{1,0:T(8,128)S(1)} custom-call(f32[128,128]{1,0:T(8,128)S(1)} %cholesky.270), custom_call_target="Cholesky" | custom-call | tf_op jit(solution)/shard_map/jit(cholesky)/cholesky | solution.py:21
  197.6 10.2 %custom-call.32 = f32[1,128,128]{1,2,0:T(8,128)S(1)} custom-call(f32[1,128,128]{2,1,0:T(8,128)S(1)} %get-tuple-element.29), custom_call_target="InvertDiagBlocksLowerTriangular" | custom-call | tf_op jit(solution)/shard_map/jit(cholesky)/cholesky | solution.py:21
  207.8 0.3 convolution_dynamic-update-slice_fusion
  208.0 0.4 convolution_subtract_fusion.4
  208.4 11.7 %cholesky.238 = f32[128,128]{1,0:T(8,128)S(1)} custom-call(f32[128,128]{1,0:T(8,128)S(1)} %cholesky.275), custom_call_target="Cholesky" | custom-call | tf_op jit(solution)/shard_map/jit(cholesky)/cholesky | solution.py:21
  220.2 0.6 compare_reduce_fusion.1
  220.8 9.8 %custom-call.33 = f32[1,128,128]{1,2,0:T(8,128)S(1)} custom-call(f32[1,128,128]{2,1,0:T(8,128)S(1)} %get-tuple-element.26), custom_call_target="InvertDiagBlocksLowerTriangular" | custom-call | tf_op jit(solution)/shard_map/jit(cholesky)/cholesky | solution.py:21
  230.7 0.2 convolution_dynamic-update-slice_fusion.1
  230.9 0.4 convolution_subtract_fusion.5
  231.3 11.7 %cholesky.255 = f32[128,128]{1,0:T(8,128)S(1)} custom-call(f32[128,128]{1,0:T(8,128)S(1)} %convolution_subtract_fusion.5), custom_call_target="Cholesky" | custom-call | tf_op jit(solution)/shard_map/jit(cholesky)/cholesky | solution.py:21
  243.0 0.7 compare_reduce_fusion
  243.6 0.6 compare_reduce_fusion.2
  246.9 1.4 fusion.16
  248.2 10.4 %while.1 = (s32[]{:T(128)}, f32[512,512]{1,0:T(8,128)S(1)}, s32[4,2]{0,1:T(2,128)S(1)}, f32[4,128,128]{2,1,0:T(8,128)}, s32[]{:T(128)}) while((s32[]{:T(128)}, f32[512,512]{1,0:T(8,128)S(1)}, s32[4,2]{0,1:T(2,128)S(1)}, f32[4,128,128]{2,1,0:T(8,128)}, s32[]{:T(128)}) %tuple.32), condition=%wide.while_cond, body=%wide.while_body.sunk | while | flops 2 | bytes 132205 | solution.py:12
  248.3 0.5 fusion.50
  248.8 2.0 bitcast_dynamic-update-slice_fusion.2
  250.9 0.5 fusion.50
  251.4 2.0 bitcast_dynamic-update-slice_fusion.2
  253.5 0.5 fusion.50
  254.0 2.0 bitcast_dynamic-update-slice_fusion.2
  256.1 0.5 fusion.50
  256.6 2.0 bitcast_dynamic-update-slice_fusion.2
  258.6 40.2 %custom-call.34 = f32[4,128,128]{1,2,0:T(8,128)S(1)} custom-call(f32[4,128,128]{2,1,0:T(8,128)} %get-tuple-element.10), custom_call_target="InvertDiagBlocksLowerTriangular" | custom-call | tf_op jit(solution)/shard_map/jit(_solve_triangular)/triangular_solve | solution.py:12
  298.8 2.4 fusion.13
  301.2 2.2 convolution_subtract_fusion.2
  303.5 1.1 fusion.28
  304.6 1.3 convolution_subtract_fusion.1
  305.8 1.1 fusion.26
  306.9 3.1 fusion.6
  310.0 1.1 fusion.25
  311.1 1.0 copy-done.2
  312.1 8.1 %fusion.9 = f32[512,512]{1,0:T(8,128)} fusion(f32[2048,512]{1,0:T(8,128)S(1)} %copy-done.1, f32[128,2048]{1,0:T(8,128)S(1)} %fusion.25, f32[128,2048]{1,0:T(8,128)S(1)} %fusion.26, f32[128,2048]{1,0:T(8,128)S(1)} %fusion.28, f32[128,2048]{1,0:T(8,128)S(1)} %fusion.13), kind=kOutput, calls=%fused_computation.13 | convolution fusion | flops 6445596672 | bytes 9437184 | tf_op jit(solution)/shard_map/dot_general | solution.py:23
  320.2 1.5 dynamic-slice_bitcast_fusion
  321.7 95.1 %all-reduce.6.cloned.1.call-done = f32[512,512]{1,0:T(8,128)} async-done(((f32[512,512]{1,0:T(8,128)}), f32[512,512]{1,0:T(8,128)}) %all-reduce.6.cloned.1.call-update) | async-done | bytes 1048592 | tf_op jit(solution)/shard_map/psum | solution.py:23
  416.8 10.8 %convolution_subtract_fusion = f32[2048,512]{1,0:T(8,128)} fusion(f32[2048,512]{1,0:T(8,128)} %param.3, f32[512,512]{1,0:T(8,128)} %all-reduce.6.cloned.1.call-done, f32[128,2048]{1,0:T(8,128)} %copy-done.2, f32[128,2048]{1,0:T(8,128)S(1)} %fusion.26, f32[128,2048]{1,0:T(8,128)S(1)} %fusion.28, f32[128,2048]{1,0:T(8,128)S(1)} %fusion.13), kind=kOutput, calls=%fused_computation.3 | convolution fusion | flops 6446645248 | bytes 13631488 | tf_op jit(solution)/shard_map/dot_general | solution.py:8
  427.6 1.0 copy.23
  (27 shorter events, 0.6 us)
Async XLA Ops:
  7.2 49.0 %all-gather.2.cloned.1.call-start = ((), (), s32[]{:S(2)}) async-start(), calls=%async_computation | async-start | bytes 4456448 | tf_op jit(solution)/shard_map/all_gather | solution.py:17
  7.9 152.5 %all-reduce.4.cloned.1.call-start = ((), (), s32[]{:S(2)}) async-start(), calls=%async_computation.1 | async-start | bytes 2097152 | tf_op jit(solution)/shard_map/psum | solution.py:20
  66.4 350.4 %all-reduce.6.cloned.1.call-start = ((), (), s32[]{:S(2)}) async-start(), calls=%async_computation.2 | async-start | bytes 2097152 | tf_op jit(solution)/shard_map/psum | solution.py:23
  258.6 45.9 %copy-start.4 = (f32[512,512]{1,0:T(8,128)}, f32[512,512]{1,0:T(8,128)S(1)}, u32[]{:S(2)}) copy-start(f32[512,512]{1,0:T(8,128)S(1)} %get-tuple-element.92) | copy-start | bytes 3145732
  298.8 5.7 %copy-start = (f32[2048,512]{0,1:T(8,128)S(1)}, f32[2048,512]{0,1:T(8,128)}, u32[]{:S(2)}) copy-start(f32[2048,512]{0,1:T(8,128)} %all-gather.2.cloned.1.call-done) | copy-start | bytes 12582916
  306.9 5.2 %copy-start.1 = (f32[2048,512]{1,0:T(8,128)S(1)}, f32[2048,512]{1,0:T(8,128)}, u32[]{:S(2)}) copy-start(f32[2048,512]{1,0:T(8,128)} %param.3) | copy-start | bytes 12582916
  311.1 1.0 copy-start.2
  416.8 10.8 %copy-start.3 = (f32[512,512]{1,0:T(8,128)S(1)}, f32[512,512]{1,0:T(8,128)}, u32[]{:S(2)}) copy-start(f32[512,512]{1,0:T(8,128)} %all-reduce.6.cloned.1.call-done) | copy-start | bytes 3145732
Sparse Core Ops, SparseCore 0:
  9.8 46.3 all-gather.1
  66.5 93.8 all-reduce.3
  320.3 96.4 all-reduce.5
where the time goes:
time: 439 us; the launch traced here: 435 us
  waiting for transfers between devices  238 us (54%)
  other arithmetic  122 us (28%)
  matrix products  43.1 us (10%)
  between operations  16.8 us (4%)
  local copies, waits for them, and re-layouts  15.6 us (4%)
    psum x1, waiting for transfers between devices, on_device(): top_rows = lax.psum(jnp.dot(orth_rows, trailing, precision=highest), 'row')  95.1 us
    psum x1, waiting for transfers between devices, on_device(): gram = lax.psum(local_gram, 'row')  93.8 us
    another operation x14, other arithmetic, on_device(): factor_low = jnp.linalg.cholesky(gram)  78.7 us
    all_gather x1, waiting for transfers between devices, on_device(): gathered = lax.all_gather(panel, 'col', axis=1, tiled=True)  48.2 us
    another operation x3, other arithmetic, lower_solve(): return jax.scipy.linalg.solve_triangular(factor_low, right_side, lower=True)  41.6 us
    dot_general x2, matrix products, contract_rows(): lax.dot_general(left, right, (((0,), (0,)), ((), ())), precision=lax.Prec...  21 us
    another operation x7, matrix products, lower_solve(): return jax.scipy.linalg.solve_triangular(factor_low, right_side, lower=True)  12.2 us
    another operation x12, local copies, waits for them, and re-layouts  10.4 us
  transfers between devices with their start and end apart: 3, of which 3 were waited for; matrix products, arithmetic and copies ran while one was open for 0% of the time, Pallas kernels for 0%

commit v1 on v0

v1 whole, which is shorter than its diff:
```python
import functools

import jax
import jax.numpy as jnp
from jax import lax
from jax.experimental import pallas as pl
from jax.experimental.pallas import tpu as pltpu
from jax.sharding import PartitionSpec as P

HIGHEST = lax.Precision.HIGHEST
HIGH = lax.Precision.HIGH
BLOCK = 128
SIDE = 4


def matmul(left, right, left_dim, right_dim, precision):
    return lax.dot_general(
        left, right, (((left_dim,), (right_dim,)), ((), ())),
        precision=precision, preferred_element_type=jnp.float32,
    )


def factor_block(rows):
    count = len(rows)
    lane = lax.broadcasted_iota(jnp.int32, (8, BLOCK), 1)
    sub = lax.broadcasted_iota(jnp.int32, (8, BLOCK), 0)
    extra = [jnp.where(lane == sub + 8 * g, 1.0, 0.0).astype(jnp.float32) for g in range(count)]
    upper, inverse = [], []
    for p in range(count):
        first = 8 * p
        top, ext = rows[p], extra[p]
        cols = [jnp.broadcast_to(top[:, first + m : first + m + 1], (8, BLOCK)) for m in range(8)]
        for j in range(8):
            pivot = jnp.broadcast_to(cols[j][j : j + 1, :], (8, BLOCK))
            factor = jnp.where(sub > j, cols[j] * (1.0 / pivot), 0.0)
            for m in range(j + 1, 8):
                cols[m] = cols[m] - factor * jnp.broadcast_to(cols[m][j : j + 1, :], (8, BLOCK))
            if j < 7:
                top = top - factor * jnp.broadcast_to(top[j : j + 1, :], (8, BLOCK))
                ext = ext - factor * jnp.broadcast_to(ext[j : j + 1, :], (8, BLOCK))
        pivots = cols[0]
        for j in range(1, 8):
            pivots = jnp.where(sub == j, cols[j], pivots)
        scale = lax.rsqrt(pivots)
        top = jnp.where(lane >= sub + first, top * scale, 0.0)
        ext = ext * scale
        upper.append(top)
        inverse.append(ext)
        if p + 1 < count:
            turned = top.T
            for g in range(p + 1, count):
                for i in range(8):
                    weight = jnp.broadcast_to(turned[8 * g : 8 * g + 8, i : i + 1], (8, BLOCK))
                    rows[g] = rows[g] - weight * jnp.broadcast_to(top[i : i + 1, :], (8, BLOCK))
                    extra[g] = extra[g] - weight * jnp.broadcast_to(ext[i : i + 1, :], (8, BLOCK))
    return jnp.concatenate(upper, 0), jnp.concatenate(inverse, 0)


def eliminate(k, size, work, upper):
    start = pl.multiple_of(k * BLOCK, BLOCK)
    here = pl.ds(start, BLOCK)
    groups = [work[pl.ds(pl.multiple_of(start + 8 * g, 8), 8), here] for g in range(BLOCK // 8)]
    diag, diag_inv = factor_block(groups)
    solved = matmul(diag_inv, work[here, :], 1, 0, HIGHEST)
    lane = lax.broadcasted_iota(jnp.int32, (BLOCK, size), 1)
    upper[here, :] = jnp.where(lane >= start + BLOCK, solved, 0.0)
    work[here, :] = jnp.where(lane < start, solved, 0.0)
    work[here, here] = diag_inv

    @pl.when(k < size // BLOCK - 1)
    def _():
        weights = upper[here, :]
        change = matmul(weights, jnp.where(lane >= start + BLOCK, solved, work[here, :]), 0, 0, HIGHEST)
        row = lax.broadcasted_iota(jnp.int32, (size, size), 0)
        col = lax.broadcasted_iota(jnp.int32, (size, size), 1)
        old = work[...]
        base = jnp.where((col >= start) & (col < start + BLOCK), 0.0, old)
        work[...] = jnp.where(row >= start + BLOCK, base - change, old)

    upper[here, here] = diag


def first_kernel(steps, gram_ref, work_ref, upper_ref):
    size = work_ref.shape[0]
    count = size // BLOCK
    work_ref[...] = jnp.zeros_like(work_ref)
    upper_ref[...] = jnp.zeros_like(upper_ref)
    for g in range(count):
        here = slice(g * BLOCK, (g + 1) * BLOCK)
        for t in range(count - 1):
            j = g + t
            part = gram_ref[here, t * BLOCK : (t + 1) * BLOCK]
            if j < count:
                work_ref[here, j * BLOCK : (j + 1) * BLOCK] = part
            elif (j - count, g) == (0, count - 1):
                work_ref[0:BLOCK, here] = part.T

    def step(k, carry):
        eliminate(k, size, work_ref, upper_ref)
        return carry

    lax.fori_loop(0, steps, step, 0)


def second_kernel(begin, work_in, upper_in, work_ref, upper_ref):
    size = work_ref.shape[0]
    work_ref[...] = work_in[...]
    upper_ref[...] = upper_in[...]

    def step(k, carry):
        eliminate(k, size, work_ref, upper_ref)
        return carry

    lax.fori_loop(begin, size // BLOCK, step, 0)


def in_vmem(kernel, operands, size, name):
    vmem = pl.BlockSpec(memory_space=pltpu.VMEM)
    return pl.pallas_call(
        kernel,
        out_shape=[jax.ShapeDtypeStruct((size, size), jnp.float32)] * 2,
        in_specs=[vmem] * len(operands),
        out_specs=[vmem] * 2,
        compiler_params=pltpu.CompilerParams(vmem_limit_bytes=24 << 20),
        cost_estimate=pl.CostEstimate(flops=20_000_000_000, bytes_accessed=4 << 20, transcendentals=0),
        name=name,
    )(*operands)


def shifted(dy, dx):
    return [(y * SIDE + x, (y + dy) % SIDE * SIDE + (x + dx) % SIDE) for y in range(SIDE) for x in range(SIDE)]


def sum_along(value, along_y):
    total = value
    for k in range(1, SIDE):
        total = total + lax.ppermute(value, "row", shifted(k, 0) if along_y else shifted(0, k))
    return total


LINES = [[y * SIDE + x for x in range(SIDE)] for y in range(SIDE)]


def on_device(panel, trailing):
    own = panel.T
    width = own.shape[0] * lax.axis_size("col")
    rows_t = lax.all_gather(own, "col", axis=0, tiled=True)
    part = matmul(own, rows_t, 1, 1, HIGHEST)
    group = lax.axis_index("col") * own.shape[0] // BLOCK
    part = lax.dynamic_slice_in_dim(jnp.concatenate([part, part], 1), group * BLOCK, width - BLOCK, 1)
    part = sum_along(sum_along(part, False), True)
    gram = lax.all_gather(part, "col", axis=0, tiled=True)

    mixed = matmul(rows_t, trailing, 1, 0, HIGH)
    mixed = lax.psum_scatter(mixed, "row", scatter_dimension=0, tiled=True, axis_index_groups=LINES)
    mixed = sum_along(mixed, True)

    work, upper = in_vmem(functools.partial(first_kernel, 2), (gram,), width, "factor_first")
    mixed = lax.all_gather(mixed, "row", axis=0, tiled=True, axis_index_groups=LINES)
    inverse_t, upper = in_vmem(functools.partial(second_kernel, 2), (work, upper), width, "factor_second")

    top_rows = matmul(inverse_t, mixed, 1, 0, HIGH)
    coefs = matmul(inverse_t, top_rows, 0, 0, HIGH)
    projected = trailing - matmul(rows_t, coefs, 0, 0, HIGH)
    r_factor = lax.dynamic_slice_in_dim(upper, lax.axis_index("col") * own.shape[0], own.shape[0], 1)
    return (r_factor, top_rows, projected)


def solution(mesh):
    placed = (P("row", "col"), P("row", "col"))
    return jax.shard_map(
        on_device,
        mesh=mesh,
        in_specs=placed,
        out_specs=(P(None, "col"), P(None, "col"), P("row", "col")),
        check_vma=False,
    )
```

time: 439 us -> 174 us (0.40)
  waiting for transfers between devices: 238 us -> 63.5 us
  other arithmetic: 122 us -> 0.85 us
  Pallas kernels: 0 us -> 27.8 us
  blocking collectives: 0 us -> 19.3 us
  matrix products: 43.1 us -> 24.1 us
  starting transfers between devices: 0.3 us -> 12.6 us
    psum x2 -> x0, waiting for transfers between devices: 189 us -> none  [the longest x1 95.1 us: on_device(): top_rows = lax.psum(jnp.dot(orth_rows, trailing, precision=highest), 'row')]
    another operation x17 -> x0, other arithmetic: 120 us -> none  [the longest x14 78.7 us: on_device(): factor_low = jnp.linalg.cholesky(gram)]
    pallas_call x0 -> x2, Pallas kernels: none -> 27.8 us  [in_vmem(): pl.pallas_call(kernel, out_shape=[jax.ShapeDtypeStruct((size, size), jnp....]
    all_gather x0 -> x1, blocking collectives: none -> 19.3 us  [on_device(): gram = lax.all_gather(part, 'col', axis=0, tiled=True)]
    another operation x13 -> x0, matrix products: 14 us -> none  [the longest x7 12.2 us: lower_solve(): return jax.scipy.linalg.solve_triangular(factor_low, right_side, lower=True)]
    ppermute x0 -> x9, starting transfers between devices: none -> 12.4 us  [sum_along(): lax.ppermute(value, 'row', shifted(k, 0) if along_y else shifted(0, k))]
    all_gather x1 -> x2, waiting for transfers between devices: 48.2 us -> 59.6 us  [the longest x1 48.2 us: on_device(): rows_t = lax.all_gather(own, 'col', axis=0, tiled=True)]
    another operation x17 -> x0, local copies, waits for them, and re-layouts: 10.5 us -> none
  transfers between devices with their start and end apart: 3 -> 12, of which waited for: 3 -> 3; matrix products, arithmetic and copies ran while one was open for 0% -> 7% of each run, Pallas kernels for 0% -> 16%
where the time goes in v1:
time: 174 us
  waiting for transfers between devices  63.5 us (36%)
  Pallas kernels  27.8 us (16%)
  matrix products  24.1 us (14%)
  blocking collectives  19.3 us (11%)
  between operations  13.9 us (8%)
  starting transfers between devices  12.6 us (7%)
  local copies, waits for them, and re-layouts  11.6 us (7%)
    all_gather x1, waiting for transfers between devices, on_device(): rows_t = lax.all_gather(own, 'col', axis=0, tiled=True)  48.2 us
    pallas_call x2, Pallas kernels, in_vmem(): pl.pallas_call(kernel, out_shape=[jax.ShapeDtypeStruct((size, size), jnp....  27.8 us
    dot_general x5, matrix products, matmul(): lax.dot_general(left, right, (((left_dim,), (right_dim,)), ((), ())), pre...  24.1 us
    all_gather x1, blocking collectives, on_device(): gram = lax.all_gather(part, 'col', axis=0, tiled=True)  19.3 us
    ppermute x9, starting transfers between devices, sum_along(): lax.ppermute(value, 'row', shifted(k, 0) if along_y else shifted(0, k))  12.4 us
    unnamed x11, local copies, waits for them, and re-layouts  11.5 us
    all_gather x1, waiting for transfers between devices, on_device(): lax.all_gather(mixed, 'row', axis=0, tiled=True, axis_index_groups=LINES)  11.3 us
  transfers between devices with their start and end apart: 12, of which 3 were waited for; matrix products, arithmetic and copies ran while one was open for 7% of the time, Pallas kernels for 16%

profile of v1, /device:TPU:1, one launch (start us, length us, event | category | flops | bytes accessed | tf_op | source)
XLA Modules:
  0.0 173.6 jit_solution(3057314513841867804)
XLA Ops:
  7.2 0.0 all-gather.3.cloned.1.call-start
  7.2 0.7 all-gather.3.cloned.1.call-update
  7.9 0.0 copy-start.2
  7.9 0.0 reduce-scatter.2.cloned.1.call-start
  8.0 48.2 %all-gather.3.cloned.1.call-done = f32[512,2048]{1,0:T(8,128)} async-done(((f32[32,2048]{1,0:T(8,128)}), f32[512,2048]{1,0:T(8,128)}) %all-gather.3.cloned.1.call-update) | async-done | bytes 4194320 | tf_op jit(solution)/shard_map/all_gather | solution.py:147
  56.2 7.9 %fusion.2 = f32[512,512]{1,0:T(8,128)} fusion(f32[512,2048]{1,0:T(8,128)} %all-gather.3.cloned.1.call-done, f32[2048,512]{1,0:T(8,128)} %param.3), kind=kOutput, calls=%fused_computation.9 | convolution fusion | flops 3221225472 | bytes 9437184 | tf_op jit(solution)/shard_map/dot_general | solution.py:17
  64.1 0.0 reduce-scatter.2.cloned.1.call-update
  64.1 0.0 all-gather.5.cloned.1.call-start
  64.2 0.0 copy-done.2
  64.2 6.0 %fusion.1 = f32[32,512]{1,0:T(8,128)S(1)} fusion(f32[2048,32]{0,1:T(8,128)S(1)} %copy-done.2, f32[512,2048]{1,0:T(8,128)} %all-gather.3.cloned.1.call-done), kind=kOutput, calls=%fused_computation.8 | convolution fusion | flops 402653184 | bytes 4521984 | tf_op jit(solution)/shard_map/dot_general | solution.py:17
  70.3 2.8 %collective-permute-start.1 = (f32[32,384]{1,0:T(8,128)S(1)}, f32[32,384]{1,0:T(8,128)S(1)}, u32[]{:S(2)}, u32[]{:S(2)}) collective-permute-start(f32[32,384]{1,0:T(8,128)S(1)} %fusion), channel_id=1, source_target_pairs={{0,32},{16,48},{32,0},{48,16},{64,96},{80,112},{96,64},{112,80},{1... | collective-permute-start | bytes 147464 | tf_op jit(solution)/shard_map/ppermute | solution.py:137
  73.1 0.3 collective-permute-start
  73.4 2.4 %collective-permute-start.2 = (f32[32,384]{1,0:T(8,128)S(1)}, f32[32,384]{1,0:T(8,128)S(1)}, u32[]{:S(2)}, u32[]{:S(2)}) collective-permute-start(f32[32,384]{1,0:T(8,128)S(1)} %fusion), channel_id=1, source_target_pairs={{0,48},{16,0},{32,16},{48,32},{64,112},{80,64},{96,80},{112,96},{1... | collective-permute-start | bytes 147464 | tf_op jit(solution)/shard_map/ppermute | solution.py:137
  75.7 0.0 collective-permute-done.1
  75.7 3.2 %collective-permute-done = f32[32,384]{1,0:T(8,128)S(1)} collective-permute-done((f32[32,384]{1,0:T(8,128)S(1)}, f32[32,384]{1,0:T(8,128)S(1)}, u32[]{:S(2)}, u32[]{:S(2)}) %collective-permute-start) | collective-permute-done | bytes 49184 | tf_op jit(solution)/shard_map/ppermute | solution.py:137
  79.0 0.0 collective-permute-done.2
  79.0 2.5 %collective-permute-start.5 = (f32[32,384]{1,0:T(8,128)S(1)}, f32[32,384]{1,0:T(8,128)S(1)}, u32[]{:S(2)}, u32[]{:S(2)}) collective-permute-start(f32[32,384]{1,0:T(8,128)S(1)} %add_add_fusion.2), channel_id=1, source_target_pairs={{0,192},{16,208},{32,224},{48,240},{64,0},{80,16},{96,32},{112,48}... | collective-permute-start | bytes 147464 | tf_op jit(solution)/shard_map/ppermute | solution.py:137
  81.6 0.5 collective-permute-start.4
  82.1 0.6 collective-permute-start.3
  82.7 5.4 %copy.5 = f32[2048,512]{0,1:T(8,128)} copy(f32[2048,512]{1,0:T(8,128)} %param.3) | data formatting | bytes 8388608 | tf_op args[1]
  88.1 0.0 collective-permute-done.5
  88.1 0.0 collective-permute-done.4
  88.1 0.0 collective-permute-done.3
  88.1 19.3 %all_gather.10.gram_ref = f32[512,384]{1,0:T(8,128)S(1)} all-gather(f32[32,384]{1,0:T(8,128)S(1)} %add_add_fusion.1), channel_id=1, replica_groups=mesh['row'=16,'col'=16] {'col'}, dimensions={0}, use_global_device_ids=true | all-gather | bytes 835584 | tf_op jit(solution)/shard_map/all_gather | solution.py:152
  107.4 0.0 reduce-scatter.2.cloned.1.call-done
  107.4 0.0 copy-start.3
  107.4 2.1 %collective-permute-start.8 = (f32[128,512]{1,0:T(8,128)}, f32[128,512]{1,0:T(8,128)S(1)}, u32[]{:S(2)}, u32[]{:S(2)}) collective-permute-start(f32[128,512]{1,0:T(8,128)} %reduce-scatter.2.cloned.1.call-done), channel_id=1, source_target_pairs={{0,192},{16,208},{32,224},{48,240},{64,0},{80,16},{96,32},{112,48}... | collective-permute-start | bytes 786440 | tf_op jit(solution)/shard_map/ppermute | solution.py:137
  109.5 1.2 collective-permute-start.7
  110.7 0.0 collective-permute-start.6
  110.7 14.5 %factor_first.1 = (f32[512,512]{1,0:T(8,128)S(1)}, f32[512,512]{1,0:T(8,128)S(1)}) custom-call(f32[512,384]{1,0:T(8,128)S(1)} %all_gather.10.gram_ref), custom_call_target="tpu_custom_call" | custom-call | flops 20000000000 | bytes 4194304 | tf_op jit(solution)/shard_map/factor_first/pallas_call | solution.py:119
  125.2 0.0 collective-permute-done.8
  125.2 0.0 collective-permute-done.7
  125.2 0.0 collective-permute-done.6
  125.2 0.0 copy-done.3
  125.2 0.8 add_add_fusion
  126.0 0.0 all-gather.5.cloned.1.call-update
  126.0 13.3 %factor_second.1 = (f32[512,512]{1,0:T(8,128)S(1)}, f32[512,512]{1,0:T(8,128)S(1)}) custom-call(f32[512,512]{1,0:T(8,128)S(1)} %get-tuple-element.7.work_in, f32[512,512]{1,0:T(8,128)S(1)} %get-tuple-element.8.upper_in), custom_call_target="tpu_custom_call" | custom-call | flops 20000000000 | bytes 4194304 | tf_op jit(solution)/shard_map/factor_second/pallas_call | solution.py:119
  139.4 0.1 constant_dynamic-slice_fusion
  139.5 0.7 copy.6
  140.3 11.3 %all-gather.5.cloned.1.call-done = f32[512,512]{1,0:T(8,128)} async-done(((f32[128,512]{1,0:T(8,128)}), f32[512,512]{1,0:T(8,128)}) %all-gather.5.cloned.1.call-update) | async-done | bytes 1048592 | tf_op jit(solution)/shard_map/all_gather | solution.py:159
  151.6 0.0 copy-start
  151.6 2.4 %fusion.3 = f32[512,512]{1,0:T(8,128)S(1)} fusion(f32[512,512]{1,0:T(8,128)S(1)} %get-tuple-element.10, f32[512,512]{1,0:T(8,128)} %all-gather.5.cloned.1.call-done), kind=kOutput, calls=%fused_computation.10 | convolution fusion | flops 805306368 | bytes 3145728 | tf_op jit(solution)/shard_map/dot_general | solution.py:17
  154.0 0.0 copy-start.1
  154.0 1.0 fusion.4
  155.0 0.0 copy-done
  155.0 6.7 %bitcast_subtract_fusion = f32[2048,512]{0,1:T(8,128)} fusion(f32[2048,512]{0,1:T(8,128)} %copy.5, f32[512,512]{1,0:T(8,128)S(1)} %fusion.4, f32[512,2048]{1,0:T(8,128)S(1)} %copy-done), kind=kOutput, calls=%fused_computation | convolution fusion | flops 3222274048 | bytes 13631488 | tf_op jit(solution)/shard_map/dot_general | solution.py:17
  161.8 0.0 copy-done.1
  161.8 5.3 %copy.7 = f32[2048,512]{1,0:T(8,128)} copy(f32[2048,512]{0,1:T(8,128)} %bitcast_subtract_fusion) | data formatting | bytes 8388608
  (3 shorter events, 0.1 us)
Async XLA Ops:
  7.2 49.0 %all-gather.3.cloned.1.call-start = ((), (), s32[]{:S(2)}) async-start(), calls=%async_computation.1 | async-start | bytes 4456448 | tf_op jit(solution)/shard_map/all_gather | solution.py:147
  7.9 56.3 %copy-start.2 = (f32[2048,32]{0,1:T(8,128)S(1)}, f32[2048,32]{0,1:T(8,128)}, u32[]{:S(2)}) copy-start(f32[2048,32]{0,1:T(8,128)} %param.2) | copy-start | bytes 786436
  7.9 99.5 %reduce-scatter.2.cloned.1.call-start = ((), (), s32[]{:S(2)}) async-start(), calls=%async_computation.2 | async-start | bytes 1310720 | tf_op jit(solution)/shard_map/reduce_scatter | solution.py:155
  64.1 87.5 %all-gather.5.cloned.1.call-start = ((), (), s32[]{:S(2)}) async-start(), calls=%async_computation.3 | async-start | bytes 1310720 | tf_op jit(solution)/shard_map/all_gather | solution.py:159
  70.3 5.5 %collective-permute-start.1 = (f32[32,384]{1,0:T(8,128)S(1)}, f32[32,384]{1,0:T(8,128)S(1)}, u32[]{:S(2)}, u32[]{:S(2)}) collective-permute-start(f32[32,384]{1,0:T(8,128)S(1)} %fusion), channel_id=1, source_target_pairs={{0,32},{16,48},{32,0},{48,16},{64,96},{80,112},{96,64},{112,80},{1... | collective-permute-start | bytes 147464 | tf_op jit(solution)/shard_map/ppermute | solution.py:137
  73.1 5.9 %collective-permute-start = (f32[32,384]{1,0:T(8,128)S(1)}, f32[32,384]{1,0:T(8,128)S(1)}, u32[]{:S(2)}, u32[]{:S(2)}) collective-permute-start(f32[32,384]{1,0:T(8,128)S(1)} %fusion), channel_id=1, source_target_pairs={{0,16},{16,32},{32,48},{48,0},{64,80},{80,96},{96,112},{112,64},{1... | collective-permute-start | bytes 147464 | tf_op jit(solution)/shard_map/ppermute | solution.py:137
  73.4 5.6 %collective-permute-start.2 = (f32[32,384]{1,0:T(8,128)S(1)}, f32[32,384]{1,0:T(8,128)S(1)}, u32[]{:S(2)}, u32[]{:S(2)}) collective-permute-start(f32[32,384]{1,0:T(8,128)S(1)} %fusion), channel_id=1, source_target_pairs={{0,48},{16,0},{32,16},{48,32},{64,112},{80,64},{96,80},{112,96},{1... | collective-permute-start | bytes 147464 | tf_op jit(solution)/shard_map/ppermute | solution.py:137
  79.0 9.1 %collective-permute-start.5 = (f32[32,384]{1,0:T(8,128)S(1)}, f32[32,384]{1,0:T(8,128)S(1)}, u32[]{:S(2)}, u32[]{:S(2)}) collective-permute-start(f32[32,384]{1,0:T(8,128)S(1)} %add_add_fusion.2), channel_id=1, source_target_pairs={{0,192},{16,208},{32,224},{48,240},{64,0},{80,16},{96,32},{112,48}... | collective-permute-start | bytes 147464 | tf_op jit(solution)/shard_map/ppermute | solution.py:137
  81.6 6.5 %collective-permute-start.4 = (f32[32,384]{1,0:T(8,128)S(1)}, f32[32,384]{1,0:T(8,128)S(1)}, u32[]{:S(2)}, u32[]{:S(2)}) collective-permute-start(f32[32,384]{1,0:T(8,128)S(1)} %add_add_fusion.2), channel_id=1, source_target_pairs={{0,128},{16,144},{32,160},{48,176},{64,192},{80,208},{96,224},{112... | collective-permute-start | bytes 147464 | tf_op jit(solution)/shard_map/ppermute | solution.py:137
  82.1 6.0 %collective-permute-start.3 = (f32[32,384]{1,0:T(8,128)S(1)}, f32[32,384]{1,0:T(8,128)S(1)}, u32[]{:S(2)}, u32[]{:S(2)}) collective-permute-start(f32[32,384]{1,0:T(8,128)S(1)} %add_add_fusion.2), channel_id=1, source_target_pairs={{0,64},{16,80},{32,96},{48,112},{64,128},{80,144},{96,160},{112,17... | collective-permute-start | bytes 147464 | tf_op jit(solution)/shard_map/ppermute | solution.py:137
  107.4 17.8 %copy-start.3 = (f32[128,512]{1,0:T(8,128)S(1)}, f32[128,512]{1,0:T(8,128)}, u32[]{:S(2)}) copy-start(f32[128,512]{1,0:T(8,128)} %reduce-scatter.2.cloned.1.call-done) | copy-start | bytes 786436
  107.4 17.8 %collective-permute-start.8 = (f32[128,512]{1,0:T(8,128)}, f32[128,512]{1,0:T(8,128)S(1)}, u32[]{:S(2)}, u32[]{:S(2)}) collective-permute-start(f32[128,512]{1,0:T(8,128)} %reduce-scatter.2.cloned.1.call-done), channel_id=1, source_target_pairs={{0,192},{16,208},{32,224},{48,240},{64,0},{80,16},{96,32},{112,48}... | collective-permute-start | bytes 786440 | tf_op jit(solution)/shard_map/ppermute | solution.py:137
  109.5 15.7 %collective-permute-start.7 = (f32[128,512]{1,0:T(8,128)}, f32[128,512]{1,0:T(8,128)S(1)}, u32[]{:S(2)}, u32[]{:S(2)}) collective-permute-start(f32[128,512]{1,0:T(8,128)} %reduce-scatter.2.cloned.1.call-done), channel_id=1, source_target_pairs={{0,128},{16,144},{32,160},{48,176},{64,192},{80,208},{96,224},{112... | collective-permute-start | bytes 786440 | tf_op jit(solution)/shard_map/ppermute | solution.py:137
  110.7 14.5 %collective-permute-start.6 = (f32[128,512]{1,0:T(8,128)}, f32[128,512]{1,0:T(8,128)S(1)}, u32[]{:S(2)}, u32[]{:S(2)}) collective-permute-start(f32[128,512]{1,0:T(8,128)} %reduce-scatter.2.cloned.1.call-done), channel_id=1, source_target_pairs={{0,64},{16,80},{32,96},{48,112},{64,128},{80,144},{96,160},{112,17... | collective-permute-start | bytes 786440 | tf_op jit(solution)/shard_map/ppermute | solution.py:137
  151.6 3.4 %copy-start = (f32[512,2048]{1,0:T(8,128)S(1)}, f32[512,2048]{1,0:T(8,128)}, u32[]{:S(2)}) copy-start(f32[512,2048]{1,0:T(8,128)} %all-gather.3.cloned.1.call-done) | copy-start | bytes 12582916
  154.0 7.8 %copy-start.1 = (f32[512,512]{1,0:T(8,128)}, f32[512,512]{1,0:T(8,128)S(1)}, u32[]{:S(2)}) copy-start(f32[512,512]{1,0:T(8,128)S(1)} %fusion.3) | copy-start | bytes 3145732
Sparse Core Ops, SparseCore 0:
  9.8 46.3 all-gather.2
  64.3 24.1 reduce-scatter.1
  126.1 25.4 all-gather.4

commit v2 on v0

v2 whole, which is shorter than its diff:
```python
import functools

import jax
import jax.numpy as jnp
from jax import lax
from jax.experimental import pallas as pl
from jax.experimental.pallas import tpu as pltpu
from jax.sharding import PartitionSpec as P

BLOCK = 128
SIDE = 4
NARROW = 32


def three_parts(value):
    high = value.astype(jnp.bfloat16)
    rest = value - high.astype(jnp.float32)
    middle = rest.astype(jnp.bfloat16)
    return high, middle, (rest - middle.astype(jnp.float32)).astype(jnp.bfloat16)


def exact_product(left, right, left_dim, right_dim):
    a, b = three_parts(left), three_parts(right)
    return lax.dot_general(
        jnp.concatenate([a[0], a[0], a[1], a[1], a[0], a[2]], left_dim),
        jnp.concatenate([b[0], b[1], b[0], b[1], b[2], b[0]], right_dim),
        (((left_dim,), (right_dim,)), ((), ())),
        preferred_element_type=jnp.float32,
    )


def one_row(value, j):
    return jnp.broadcast_to(value[j : j + 1, :], value.shape)


def factor_block(rows):
    count, wide, step = len(rows), 4, 2
    lane = lax.broadcasted_iota(jnp.int32, (8, BLOCK), 1)
    sub = lax.broadcasted_iota(jnp.int32, (8, BLOCK), 0)
    extra = [jnp.where(lane == sub + 8 * g, 1.0, 0.0).astype(jnp.float32) for g in range(count)]
    for p in range(0, count, wide):
        for q in range(p, p + wide, step):
            live = range(q, p + wide)
            cols = {
                g: [jnp.broadcast_to(rows[g][:, 8 * q + m : 8 * q + m + 1], (8, BLOCK)) for m in range(8 * step)]
                for g in live
            }
            pivots = {}
            for j in range(8 * step):
                group, at = q + j // 8, j % 8
                scale = 1.0 / one_row(cols[group][j], at)
                top, ext = one_row(rows[group], at), one_row(extra[group], at)
                entries = {m: one_row(cols[group][m], at) for m in range(j + 1, 8 * step)}
                for g in live:
                    if g < group:
                        continue
                    factor = cols[g][j] * scale
                    if g == group:
                        factor = jnp.where(sub > at, factor, 0.0)
                    for m in range(j + 1, 8 * step):
                        cols[g][m] = cols[g][m] - factor * entries[m]
                    rows[g] = rows[g] - factor * top
                    extra[g] = extra[g] - factor * ext
                pivots[group] = cols[group][j] if at == 0 else jnp.where(sub == at, cols[group][j], pivots[group])
            for g in range(q, q + step):
                scale = lax.rsqrt(pivots[g])
                rows[g] = jnp.where(lane >= sub + 8 * g, rows[g] * scale, 0.0)
                extra[g] = extra[g] * scale
        if p + wide < count:
            solved = jnp.concatenate(rows[p : p + wide], 0)
            both = jnp.concatenate([solved, jnp.concatenate(extra[p : p + wide], 0)], 1)
            change = exact_product(solved, both, 0, 0)
            for g in range(p + wide, count):
                rows[g] = rows[g] - change[8 * g : 8 * g + 8, :BLOCK]
                extra[g] = extra[g] - change[8 * g : 8 * g + 8, BLOCK:]
    return jnp.concatenate(rows, 0), jnp.concatenate(extra, 0)


def eliminate(begin, end, work, upper):
    size = work.shape[0]

    def step(k, carry):
        start = pl.multiple_of(k * BLOCK, BLOCK)
        groups = [work[pl.ds(pl.multiple_of(start + 8 * g, 8), 8), pl.ds(start, BLOCK)] for g in range(BLOCK // 8)]
        diag, diag_inv = factor_block(groups)
        for i in range(begin, end):

            @pl.when(k == i)
            def _(first=i * BLOCK, last=(i + 1) * BLOCK):
                here = slice(first, last)
                solved = exact_product(diag_inv, work[here, :], 1, 0)
                pieces = [diag_inv]
                if first:
                    work[here, :first] = solved[:, :first]
                    pieces = [solved[:, :first], diag_inv]
                work[here, here] = diag_inv
                upper[here, here] = diag
                if last < size:
                    right = solved[:, last:]
                    work[here, last:] = jnp.zeros_like(right)
                    upper[here, last:] = right
                    change = exact_product(right, jnp.concatenate(pieces + [right], 1), 0, 0)
                    if first:
                        work[last:, :first] = work[last:, :first] - change[:, :first]
                    work[last:, here] = -change[:, here]
                    work[last:, last:] = work[last:, last:] - change[:, last:]

        return carry

    lax.fori_loop(begin, end, step, 0)


def first_kernel(steps, part_ref, work_ref, upper_ref):
    size = work_ref.shape[0]
    chips = size // (2 * NARROW)
    upper_ref[...] = jnp.zeros_like(upper_ref)
    pair = 2 * NARROW
    tall = part_ref.shape[0] // (2 * chips)
    far = chips // 2

    def columns_of(z, c, s):
        first = (2 * z + c) * tall
        return part_ref[first : first + pair, s * NARROW : (s + 1) * NARROW]

    for z in range(chips):
        here = slice(z * pair, (z + 1) * pair)
        for s in range(far):
            lower = (z - s) % chips
            block = jnp.concatenate([columns_of(z, 0, s), columns_of(lower, 1, s)], 1)
            if lower <= z:
                work_ref[lower * pair : (lower + 1) * pair, here] = block
            else:
                work_ref[here, lower * pair : (lower + 1) * pair] = block.T
        if z >= far:
            for c in range(2):
                first = (2 * z + c) * tall + pair
                row = (2 * (z - far) + c) * NARROW
                work_ref[row : row + NARROW, here] = part_ref[first : first + NARROW, 0:pair]

    eliminate(0, steps, work_ref, upper_ref)


def second_kernel(begin, place_ref, work_in, upper_in, work_ref, upper_ref, own_ref, turned_ref):
    size = work_ref.shape[0]

    eliminate(begin, size // BLOCK, work_ref, upper_ref)
    first = place_ref[0] * NARROW
    group = pl.multiple_of(first // BLOCK * BLOCK, BLOCK)
    turned_ref[...] = upper_ref[:, pl.ds(group, BLOCK)].T
    own_ref[...] = turned_ref[pl.ds(pl.multiple_of(lax.rem(first, BLOCK), NARROW), NARROW), :]


VMEM = pl.BlockSpec(memory_space=pltpu.VMEM)
SMEM = pl.BlockSpec(memory_space=pltpu.SMEM)
HBM = pl.BlockSpec(memory_space=pltpu.HBM)


def cost(flops):
    return pl.CostEstimate(flops=flops, bytes_accessed=1 << 20, transcendentals=0)


def in_vmem(value):
    return pltpu.with_memory_space_constraint(value, pltpu.VMEM)


def scalar(value):
    return jnp.asarray(value, jnp.int32).reshape(1)


def factor_first(parts, size, steps):
    return pl.pallas_call(
        functools.partial(first_kernel, steps),
        out_shape=[jax.ShapeDtypeStruct((size, size), jnp.float32)] * 2,
        in_specs=[VMEM],
        out_specs=[VMEM] * 2,
        compiler_params=pltpu.CompilerParams(vmem_limit_bytes=16 << 20),
        cost_estimate=cost(10_000_000_000),
        name="factor_first",
    )(parts)


def factor_second(work, upper, begin):
    size = work.shape[0]
    return pl.pallas_call(
        functools.partial(second_kernel, begin),
        out_shape=[jax.ShapeDtypeStruct((size, size), jnp.float32)] * 2 + [jax.ShapeDtypeStruct((NARROW, size), jnp.float32)],
        in_specs=[SMEM, VMEM, VMEM],
        out_specs=[VMEM] * 3,
        scratch_shapes=[pltpu.VMEM((BLOCK, size), jnp.float32)],
        input_output_aliases={1: 0, 2: 1},
        compiler_params=pltpu.CompilerParams(vmem_limit_bytes=16 << 20),
        cost_estimate=cost(8_000_000_000),
        name="factor_second",
    )(scalar(lax.axis_index("col")), work, upper)


def shifted(dy, dx):
    return [(y * SIDE + x, (y + dy) % SIDE * SIDE + (x + dx) % SIDE) for y in range(SIDE) for x in range(SIDE)]


def sent_along(value, along_y):
    return [lax.ppermute(value, "row", shifted(k, 0) if along_y else shifted(0, k)) for k in range(1, SIDE)]


def sum_along(value, along_y):
    return sum(sent_along(value, along_y), value)


LINES = [[y * SIDE + x for x in range(SIDE)] for y in range(SIDE)]


def split(value):
    high = value.astype(jnp.bfloat16)
    return high, (value - high.astype(jnp.float32)).astype(jnp.bfloat16)


def three_products(left, right, left_dim, right_dim):
    def one(a, b):
        return lax.dot_general(a, b, (((left_dim,), (right_dim,)), ((), ())), preferred_element_type=jnp.float32)

    return one(left[0], right[0]) + (one(left[0], right[1]) + one(left[1], right[0]))


def part_kernel(core_ref, own_ref, other_ref, *refs):
    part_ref, own, sem = refs[-3:]
    refs = refs[:-2]
    load = pltpu.make_async_copy(own_ref, own, sem)
    load.start()
    load.wait()
    own_ref = own
    narrow = own_ref.shape[0]
    even = core_ref[0] == 0
    blocks = jnp.concatenate([own_ref[...], other_ref[...]] + [ref[...] for ref in refs[:-1]], 0)
    count, pair = blocks.shape[0], 2 * narrow
    left = three_parts(blocks)
    right = jnp.concatenate([part[:pair] for part in left], 0)
    products = lax.dot_general(
        jnp.concatenate(left, 0), right, (((1,), (1,)), ((), ())), preferred_element_type=jnp.float32
    )

    def piece(i, j):
        return products[i * count : (i + 1) * count, j * pair : (j + 1) * pair]

    total = piece(0, 0) + ((piece(0, 1) + piece(1, 0)) + (piece(1, 1) + (piece(0, 2) + piece(2, 0))))
    columns = [jnp.concatenate([jnp.where(even, total[:narrow, :narrow], total[narrow:pair, :narrow]),
                                jnp.where(even, total[narrow:pair, :narrow], total[:narrow, :narrow])], 0)]
    for first in range(pair, count - narrow, pair):
        turned = total[first : first + narrow].T
        swapped = jnp.concatenate([turned[narrow:], turned[:narrow]], 0)
        columns.append(jnp.where(even, total[first : first + pair, :narrow], swapped))
    tail = total[count - narrow :]
    tail = jnp.where(even, tail, jnp.concatenate([tail[:, narrow:], tail[:, :narrow]], 1))
    tail = jnp.concatenate([tail, jnp.zeros((narrow, (len(columns) - 2) * narrow), jnp.float32)], 1)
    part_ref[...] = jnp.concatenate([jnp.concatenate(columns, 1), tail], 0)


def gram_part(own, other, blocks):
    return pl.pallas_call(
        part_kernel,
        out_shape=jax.ShapeDtypeStruct((3 * NARROW, 4 * NARROW), jnp.float32),
        in_specs=[SMEM, HBM] + [VMEM] * (1 + len(blocks)),
        out_specs=VMEM,
        scratch_shapes=[pltpu.VMEM(own.shape, jnp.float32), pltpu.SemaphoreType.DMA],
        compiler_params=pltpu.CompilerParams(vmem_limit_bytes=16 << 20),
        cost_estimate=cost(2_000_000_000),
        name="gram_part",
    )(scalar(lax.rem(lax.axis_index("col"), 2)), pltpu.with_memory_space_constraint(own, pltpu.HBM), in_vmem(other), *[in_vmem(block) for block in blocks])


def turn_kernel(tile, *refs):
    own_ref, *blocks, high_ref, low_ref, own, high, low, sems = refs
    load = pltpu.make_async_copy(own_ref, own, sems.at[0])
    load.start()
    load.wait()
    stores = []
    for t in range(high.shape[0]):
        rows = jnp.concatenate([ref[:, t * tile : (t + 1) * tile] for ref in [own] + blocks], 0)
        here = pl.ds(t * tile, tile)
        for value, kept, out, i in zip(split(rows.T), (high, low), (high_ref, low_ref), range(2)):
            kept[t] = value
            stores.append(pltpu.make_async_copy(kept.at[t], out.at[here, :], sems.at[1 + 2 * t + i]))
            stores[-1].start()
    for store in stores:
        store.wait()


def turn(blocks, tile):
    count = sum(block.shape[0] for block in blocks)
    depth = blocks[0].shape[1]
    tiles = depth // tile
    return pl.pallas_call(
        functools.partial(turn_kernel, tile),
        out_shape=[pltpu.HBM((depth, count), jnp.bfloat16)] * 2,
        in_specs=[HBM] + [VMEM] * (len(blocks) - 1),
        out_specs=[HBM, HBM],
        scratch_shapes=[pltpu.VMEM(blocks[0].shape, jnp.float32)]
        + [pltpu.VMEM((tiles, tile, count), jnp.bfloat16)] * 2
        + [pltpu.SemaphoreType.DMA((2 * tiles + 1,))],
        compiler_params=pltpu.CompilerParams(vmem_limit_bytes=16 << 20),
        cost_estimate=cost(3_000_000_000),
        name="turn",
    )(pltpu.with_memory_space_constraint(blocks[0], pltpu.HBM), *[in_vmem(block) for block in blocks[1:]])


def mixed_kernel(tile, turned, place_ref, *refs):
    own_ref, *blocks = refs[: -(10 + SIDE)]
    trailing_ref, *quarter_refs = refs[-(10 + SIDE) : -9]
    high_ref, low_ref, own, taken, high, low, loads_sem, stores_sem, whole = refs[-9:]
    tiles = taken.shape[0]
    here = [pl.ds(t * tile, tile) for t in range(tiles)]
    load_own = pltpu.make_async_copy(own_ref, own, loads_sem.at[tiles])
    load_own.start()
    loads = [pltpu.make_async_copy(trailing_ref.at[here[t], :], taken.at[t], loads_sem.at[t]) for t in range(tiles)]
    for load in loads:
        load.start()
    load_own.wait()
    blocks = [own] + blocks
    stores = []
    for t in range(tiles):
        rows = split(jnp.concatenate([ref[:, t * tile : (t + 1) * tile] for ref in blocks], 0))
        loads[t].wait()
        product = three_products(rows, split(taken[t]), 1, 0)
        whole[...] = product if t == 0 else whole[...] + product
        for value, kept, out, i in ((rows[0], high, high_ref, 0), (rows[1], low, low_ref, 1)):
            kept[t] = value[-turned:].T
            stores.append(pltpu.make_async_copy(kept.at[t], out.at[here[t], :], stores_sem.at[2 * t + i]))
            stores[-1].start()
    size = whole.shape[0] // SIDE
    for k in range(SIDE):
        quarter_refs[k][...] = whole[pl.ds(pl.multiple_of(lax.rem(place_ref[0] + k, SIDE) * size, size), size), :]
    for store in stores:
        store.wait()


def mix(early, late, trailing, tile):
    depth, across = trailing.shape
    tiles = depth // tile
    blocks = early + late
    width = sum(block.shape[0] for block in blocks)
    turned = sum(block.shape[0] for block in late)
    return pl.pallas_call(
        functools.partial(mixed_kernel, tile, turned),
        out_shape=[jax.ShapeDtypeStruct((width // SIDE, across), jnp.float32)] * SIDE
        + [pltpu.HBM((depth, turned), jnp.bfloat16)] * 2,
        in_specs=[SMEM, HBM] + [VMEM] * (len(blocks) - 1) + [HBM],
        out_specs=[VMEM] * SIDE + [HBM, HBM],
        scratch_shapes=[
            pltpu.VMEM(blocks[0].shape, jnp.float32),
            pltpu.VMEM((tiles, tile, across), jnp.float32),
            pltpu.VMEM((tiles, tile, turned), jnp.bfloat16),
            pltpu.VMEM((tiles, tile, turned), jnp.bfloat16),
            pltpu.SemaphoreType.DMA((tiles + 1,)),
            pltpu.SemaphoreType.DMA((2 * tiles,)),
            pltpu.VMEM((width, across), jnp.float32),
        ],
        compiler_params=pltpu.CompilerParams(vmem_limit_bytes=20 << 20),
        cost_estimate=cost(5_000_000_000),
        name="mixed",
    )(
        scalar(lax.rem(lax.axis_index("row"), SIDE)),
        pltpu.with_memory_space_constraint(blocks[0], pltpu.HBM),
        *[in_vmem(block) for block in blocks[1:]],
        pltpu.with_memory_space_constraint(trailing, pltpu.HBM),
    )


def last_kernel(tile, place_ref, inverse_ref, *refs):
    pieces, refs = refs[:SIDE], refs[SIDE:]
    highs, lows, refs = refs[:2], refs[2:4], refs[4:]
    trailing_ref, top_ref, out_ref, rows, tiles, sems = refs
    width = inverse_ref.shape[0]
    count = width // NARROW
    quarter = count // SIDE

    def placed(i):
        return pl.ds(pl.multiple_of(place_ref[i] * NARROW, NARROW), NARROW)

    for k in range(SIDE):
        for j in range(quarter):
            at = placed(lax.rem(place_ref[count] - k + SIDE, SIDE) * quarter + j)
            rows[at, :] = pieces[k][j * NARROW : (j + 1) * NARROW, :]
    inverse = split(inverse_ref[...])
    top = three_products(inverse, split(rows[...]), 1, 0)
    top_ref[...] = top
    rows[...] = three_products(inverse, split(top), 0, 0)
    weights = split(jnp.concatenate([rows[placed(i), :] for i in range(count)], 0))
    copies = []
    for t in range(trailing_ref.shape[0] // tile):
        here = slice(t * tile, (t + 1) * tile)
        left = [jnp.concatenate([a[here, :], b[here, :]], 1) for a, b in (highs, lows)]
        tiles[t] = trailing_ref[here, :] - three_products(left, weights, 1, 0)
        copies.append(pltpu.make_async_copy(tiles.at[t], out_ref.at[pl.ds(t * tile, tile), :], sems.at[t]))
        copies[-1].start()
    for copy in copies:
        copy.wait()


def finish(places, inverse_t, pieces, highs, lows, trailing, tile):
    depth, across = trailing.shape
    width = inverse_t.shape[0]
    return pl.pallas_call(
        functools.partial(last_kernel, tile),
        out_shape=[
            jax.ShapeDtypeStruct((width, across), jnp.float32),
            jax.ShapeDtypeStruct((depth, across), jnp.float32),
        ],
        in_specs=[SMEM] + [VMEM] * (2 + SIDE + 2 * len(highs)),
        out_specs=[VMEM, pl.BlockSpec(memory_space=pl.ANY)],
        scratch_shapes=[pltpu.VMEM((width, across), jnp.float32)]
        + [pltpu.VMEM((depth // tile, tile, across), jnp.float32), pltpu.SemaphoreType.DMA((depth // tile,))],
        compiler_params=pltpu.CompilerParams(vmem_limit_bytes=24 << 20),
        cost_estimate=cost(8_000_000_000),
        name="finish",
    )(places, inverse_t, *pieces, *highs, *lows, trailing)


def round_z(chips):
    return [(2 * z + c, 2 * ((z + 1 - 2 * c) % chips) + c) for z in range(chips) for c in range(2)]


def on_device(panel, trailing):
    own = panel.T
    narrow = own.shape[0]
    devices = lax.axis_size("col")
    chips = devices // 2
    width = narrow * devices
    far = chips // 2
    ring = round_z(chips)
    swap = [(i, i ^ 1) for i in range(devices)]

    def send(value):
        return lax.ppermute(value, "col", ring)

    def exchange(value):
        return lax.ppermute(value, "col", swap)

    first, second = [own], [exchange(own)]
    blocks = [own, second[0]]
    for s in range(1, far):
        first.append(send(first[-1]))
        second.append(send(second[-1]))
        blocks += [first[s], second[s], exchange(second[s]), exchange(first[s])]
    first.append(send(first[-1]))
    early = blocks[: 4 * far - 4]
    high, low = turn(early, 512)
    first[far], high = lax.optimization_barrier((first[far], high))

    received = [first[s] if core == 0 else second[s] for s in range(1, far) for core in range(2)] + [first[far]]
    part = gram_part(own, second[0], received)
    pieces = sent_along(part, False)
    late = blocks[4 * far - 4 :] + [first[far], exchange(first[far])]
    late[0], pieces[0] = lax.optimization_barrier((late[0], pieces[0]))
    *quarters, late_high, late_low = mix(early, late, trailing, 512)
    part = sum(pieces, part)
    quarters[1:] = [lax.ppermute(quarter, "row", shifted(0, k + 1)) for k, quarter in enumerate(quarters[1:])]
    part, quarters[0] = lax.optimization_barrier((sum_along(part, True), quarters[0]))
    mixed = sum(quarters[1:], quarters[0])
    mixed = sum_along(mixed, True)
    parts = lax.all_gather(part, "col", axis=0, tiled=True)

    work, upper = factor_first(parts, width, 2)
    quarters = [mixed] + sent_along(mixed, False)
    inverse_t, upper, own_factor = factor_second(work, upper, 2)

    row, col = lax.axis_index("row"), lax.axis_index("col")
    z, c = lax.div(col, 2), lax.rem(col, 2)
    places = [2 * z + c, 2 * z + 1 - c]
    for s in range(1, far):
        for chip in (z + s * (2 * c - 1), z - s * (2 * c - 1)):
            chip = lax.rem(chip + chips, chips)
            places += [2 * chip + c, 2 * chip + 1 - c]
    chip = lax.rem(z + far, chips)
    places += [2 * chip + c, 2 * chip + 1 - c, lax.rem(row, SIDE)]
    places = jnp.stack(places).astype(jnp.int32)
    top_rows, projected = finish(places, inverse_t, quarters, [high, late_high], [low, late_low], trailing, 512)
    return (own_factor.T, top_rows, projected)


def solution(mesh):
    placed = (P("row", "col"), P("row", "col"))
    return jax.shard_map(
        on_device,
        mesh=mesh,
        in_specs=placed,
        out_specs=(P(None, "col"), P(None, "col"), P("row", "col")),
        check_vma=False,
    )
```

time: 439 us -> 122 us (0.28)
  waiting for transfers between devices: 238 us -> 17.6 us
  other arithmetic: 122 us -> 1.03 us
  starting transfers between devices: 0.3 us -> 44.7 us
  matrix products: 43.1 us -> 0 us
  Pallas kernels: 0 us -> 37.8 us
  blocking collectives: 0 us -> 19.9 us
  between operations: 16.8 us -> 0.99 us
  local copies, waits for them, and re-layouts: 15.6 us -> 0.11 us
    psum x2 -> x0, waiting for transfers between devices: 189 us -> none  [the longest x1 95.1 us: on_device(): top_rows = lax.psum(jnp.dot(orth_rows, trailing, precision=highest), 'row')]
    another operation x17 -> x0, other arithmetic: 120 us -> none  [the longest x14 78.7 us: on_device(): factor_low = jnp.linalg.cholesky(gram)]
    all_gather x1 -> x0, waiting for transfers between devices: 48.2 us -> none  [on_device(): gathered = lax.all_gather(panel, 'col', axis=1, tiled=True)]
    ppermute x0 -> x30, starting transfers between devices: none -> 44.7 us  [the longest x12 14.2 us: sent_along(): lax.ppermute(value, 'row', shifted(k, 0) if along_y else shifted(0, k))]
    pallas_call x0 -> x6, Pallas kernels: none -> 37.8 us  [the longest x1 9.46 us: factor_first(): pl.pallas_call(functools.partial(first_kernel, steps), out_shape=[jax.Sha...]
    dot_general x3 -> x0, matrix products: 29.1 us -> none  [the longest x2 21 us: contract_rows(): lax.dot_general(left, right, (((0,), (0,)), ((), ())), precision=lax.Prec...]
    all_gather x0 -> x1, blocking collectives: none -> 19.9 us  [on_device(): parts = lax.all_gather(part, 'col', axis=0, tiled=True)]
    ppermute x0 -> x30, waiting for transfers between devices: none -> 17.6 us  [the longest x12 11.3 us: sent_along(): lax.ppermute(value, 'row', shifted(k, 0) if along_y else shifted(0, k))]
  transfers between devices with their start and end apart: 3 -> 30, of which waited for: 3 -> 7; matrix products, arithmetic and copies ran while one was open for 0% -> 1% of each run, Pallas kernels for 0% -> 24%
where the time goes in v2:
time: 122 us
  starting transfers between devices  44.7 us (37%)
  Pallas kernels  37.8 us (31%)
  blocking collectives  19.9 us (16%)
  waiting for transfers between devices  17.6 us (14%)
    all_gather x1, blocking collectives, on_device(): parts = lax.all_gather(part, 'col', axis=0, tiled=True)  19.9 us
    ppermute x12, starting transfers between devices, sent_along(): lax.ppermute(value, 'row', shifted(k, 0) if along_y else shifted(0, k))  14.2 us
    ppermute x7, starting transfers between devices, send(): return lax.ppermute(value, 'col', ring)  13.6 us
    ppermute x8, starting transfers between devices, exchange(): return lax.ppermute(value, 'col', swap)  13.2 us
    ppermute x12, waiting for transfers between devices, sent_along(): lax.ppermute(value, 'row', shifted(k, 0) if along_y else shifted(0, k))  11.3 us
    pallas_call x1, Pallas kernels, factor_first(): pl.pallas_call(functools.partial(first_kernel, steps), out_shape=[jax.Sha...  9.46 us
    pallas_call x1, Pallas kernels, finish(): pl.pallas_call(functools.partial(last_kernel, tile), out_shape=[jax.Shape...  7.95 us
    pallas_call x1, Pallas kernels, factor_second(): pl.pallas_call(functools.partial(second_kernel, begin), out_shape=[jax.Sh...  7.79 us
  transfers between devices with their start and end apart: 30, of which 7 were waited for; matrix products, arithmetic and copies ran while one was open for 1% of the time, Pallas kernels for 24%

profile of v2, /device:TPU:1, one launch (start us, length us, event | category | flops | bytes accessed | tf_op | source)
XLA Modules:
  0.0 122.1 jit_solution(13802925114477278450)
XLA Ops:
  0.6 3.3 %collective-permute-start = (f32[32,2048]{1,0:T(8,128)}, f32[32,2048]{1,0:T(8,128)S(1)}, u32[]{:S(2)}, u32[]{:S(2)}) collective-permute-start(f32[32,2048]{1,0:T(8,128)} %bitcast.21), channel_id=1, source_target_pairs={{0,1},{1,0},{2,3},{3,2},{4,5},{5,4},{6,7},{7,6},{8,9},{9,8},{10,11... | collective-permute-start | bytes 786440 | tf_op jit(solution)/shard_map/ppermute | solution.py:435
  4.0 3.8 %collective-permute-start.1 = (f32[32,2048]{1,0:T(8,128)}, f32[32,2048]{1,0:T(8,128)S(1)}, u32[]{:S(2)}, u32[]{:S(2)}) collective-permute-start(f32[32,2048]{1,0:T(8,128)} %bitcast.22), channel_id=1, source_target_pairs={{0,2},{1,15},{2,4},{3,1},{4,6},{5,3},{6,8},{7,5},{8,10},{9,7},{10,... | collective-permute-start | bytes 786440 | tf_op jit(solution)/shard_map/ppermute | solution.py:432
  7.8 1.4 %collective-permute-start.2 = (f32[32,2048]{1,0:T(8,128)S(1)}, f32[32,2048]{1,0:T(8,128)S(1)}, u32[]{:S(2)}, u32[]{:S(2)}) collective-permute-start(f32[32,2048]{1,0:T(8,128)S(1)} %collective-permute-done.refs_1_.other_ref), channel_id=1, source_target_pairs={{0,2},{1,15},{2,4},{3,1},{4,6},{5,3},{6,8},{7,5},{8,10},{9,7},{10,... | collective-permute-start | bytes 786440 | tf_op jit(solution)/shard_map/ppermute | solution.py:432
  9.2 2.3 %collective-permute-done.1.refs_2_.refs_0_ = f32[32,2048]{1,0:T(8,128)S(1)} collective-permute-done((f32[32,2048]{1,0:T(8,128)}, f32[32,2048]{1,0:T(8,128)S(1)}, u32[]{:S(2)}, u32[]{:S(2)}) %collective-permute-start.1) | collective-permute-done | bytes 262176 | tf_op jit(solution)/shard_map/ppermute | solution.py:432
  11.4 3.0 %collective-permute-start.3 = (f32[32,2048]{1,0:T(8,128)S(1)}, f32[32,2048]{1,0:T(8,128)S(1)}, u32[]{:S(2)}, u32[]{:S(2)}) collective-permute-start(f32[32,2048]{1,0:T(8,128)S(1)} %collective-permute-done.1.refs_2_.refs_0_), channel_id=1, source_target_pairs={{0,2},{1,15},{2,4},{3,1},{4,6},{5,3},{6,8},{7,5},{8,10},{9,7},{10,... | collective-permute-start | bytes 786440 | tf_op jit(solution)/shard_map/ppermute | solution.py:432
  14.4 0.0 collective-permute-done.2.refs_3_.refs_1_
  14.4 2.8 %collective-permute-start.4 = (f32[32,2048]{1,0:T(8,128)S(1)}, f32[32,2048]{1,0:T(8,128)S(1)}, u32[]{:S(2)}, u32[]{:S(2)}) collective-permute-start(f32[32,2048]{1,0:T(8,128)S(1)} %collective-permute-done.2.refs_3_.refs_1_), channel_id=1, source_target_pairs={{0,2},{1,15},{2,4},{3,1},{4,6},{5,3},{6,8},{7,5},{8,10},{9,7},{10,... | collective-permute-start | bytes 786440 | tf_op jit(solution)/shard_map/ppermute | solution.py:432
  17.3 0.5 collective-permute-done.3.refs_6_.refs_2_
  17.8 2.6 %collective-permute-start.11 = (f32[32,2048]{1,0:T(8,128)S(1)}, f32[32,2048]{1,0:T(8,128)S(1)}, u32[]{:S(2)}, u32[]{:S(2)}) collective-permute-start(f32[32,2048]{1,0:T(8,128)S(1)} %collective-permute-done.3.refs_6_.refs_2_), channel_id=1, source_target_pairs={{0,1},{1,0},{2,3},{3,2},{4,5},{5,4},{6,7},{7,6},{8,9},{9,8},{10,11... | collective-permute-start | bytes 786440 | tf_op jit(solution)/shard_map/ppermute | solution.py:435
  20.3 0.6 collective-permute-start.5
  20.9 2.2 %collective-permute-start.10 = (f32[32,2048]{1,0:T(8,128)S(1)}, f32[32,2048]{1,0:T(8,128)S(1)}, u32[]{:S(2)}, u32[]{:S(2)}) collective-permute-start(f32[32,2048]{1,0:T(8,128)S(1)} %collective-permute-done.4.refs_7_.refs_3_), channel_id=1, source_target_pairs={{0,1},{1,0},{2,3},{3,2},{4,5},{5,4},{6,7},{7,6},{8,9},{9,8},{10,11... | collective-permute-start | bytes 786440 | tf_op jit(solution)/shard_map/ppermute | solution.py:435
  23.1 0.0 collective-permute-done.9.refs_5_
  23.1 0.6 collective-permute-start.6
  23.7 2.1 %collective-permute-done.5.refs_10_.refs_4_ = f32[32,2048]{1,0:T(8,128)S(1)} collective-permute-done((f32[32,2048]{1,0:T(8,128)S(1)}, f32[32,2048]{1,0:T(8,128)S(1)}, u32[]{:S(2)}, u32[]{:S(2)}) %collective-permute-start.5) | collective-permute-done | bytes 262176 | tf_op jit(solution)/shard_map/ppermute | solution.py:432
  25.8 1.5 %collective-permute-start.7 = (f32[32,2048]{1,0:T(8,128)S(1)}, f32[32,2048]{1,0:T(8,128)S(1)}, u32[]{:S(2)}, u32[]{:S(2)}) collective-permute-start(f32[32,2048]{1,0:T(8,128)S(1)} %collective-permute-done.5.refs_10_.refs_4_), channel_id=1, source_target_pairs={{0,2},{1,15},{2,4},{3,1},{4,6},{5,3},{6,8},{7,5},{8,10},{9,7},{10,... | collective-permute-start | bytes 786440 | tf_op jit(solution)/shard_map/ppermute | solution.py:432
  27.3 1.3 %collective-permute-done.6.refs_11_.refs_5_ = f32[32,2048]{1,0:T(8,128)S(1)} collective-permute-done((f32[32,2048]{1,0:T(8,128)S(1)}, f32[32,2048]{1,0:T(8,128)S(1)}, u32[]{:S(2)}, u32[]{:S(2)}) %collective-permute-start.6) | collective-permute-done | bytes 262176 | tf_op jit(solution)/shard_map/ppermute | solution.py:432
  28.6 2.9 %turn.1 = (bf16[2048,384]{1,0:T(8,128)(2,1)}, bf16[2048,384]{1,0:T(8,128)(2,1)}) custom-call(f32[32,2048]{1,0:T(8,128)} %bitcast.23, f32[32,2048]{1,0:T(8,128)S(1)} %collective-permute-done.refs_1_.other_ref, f32[32,2048]{1,0:T(8,128)S(1)} %collective-permute-done.1.refs_2_.refs_0_, f32[32,2048]{1,0:T(8,128)S(1)} %collective-permute-done.2.refs_3_.refs_1_, ...), custom_call_target="tpu_custom_call" | custom-call | flops 3000000000 | bytes 1048576 | tf_op jit(solution)/shard_map/turn/pallas_call | solution.py:291
  31.6 3.9 %collective-permute-start.12 = (f32[32,2048]{1,0:T(8,128)S(1)}, f32[32,2048]{1,0:T(8,128)S(1)}, u32[]{:S(2)}, u32[]{:S(2)}) collective-permute-start(f32[32,2048]{1,0:T(8,128)S(1)} %collective-permute-done.6.refs_11_.refs_5_), channel_id=1, source_target_pairs={{0,1},{1,0},{2,3},{3,2},{4,5},{5,4},{6,7},{7,6},{8,9},{9,8},{10,11... | collective-permute-start | bytes 786440 | tf_op jit(solution)/shard_map/ppermute | solution.py:435
  35.5 2.3 %gram_part.1 = f32[96,128]{1,0:T(8,128)S(1)} custom-call(s32[1]{0:T(128)} %bitcast.1.core_ref, f32[32,2048]{1,0:T(8,128)} %bitcast.24, f32[32,2048]{1,0:T(8,128)S(1)} %collective-permute-done.refs_1_.other_ref, f32[32,2048]{1,0:T(8,128)S(1)} %collective-permute-done.1.refs_2_.refs_0_, f32[32,2048]{1,0:T(8,128)S(1)} %collective-permute-done.2.refs_3_.refs_1_, ...), custom_call_target="tpu_custom_call" | custom-call | flops 2000000000 | bytes 1048576 | tf_op jit(solution)/shard_map/gram_part/pallas_call | solution.py:258
  37.8 1.3 %collective-permute-start.13 = (f32[96,128]{1,0:T(8,128)S(1)}, f32[96,128]{1,0:T(8,128)S(1)}, u32[]{:S(2)}, u32[]{:S(2)}) collective-permute-start(f32[96,128]{1,0:T(8,128)S(1)} %gram_part.1), channel_id=1, source_target_pairs={{0,16},{16,32},{32,48},{48,0},{64,80},{80,96},{96,112},{112,64},{1... | collective-permute-start | bytes 147464 | tf_op jit(solution)/shard_map/ppermute | solution.py:202
  39.1 1.5 %collective-permute-start.15 = (f32[96,128]{1,0:T(8,128)S(1)}, f32[96,128]{1,0:T(8,128)}, u32[]{:S(2)}, u32[]{:S(2)}) collective-permute-start(f32[96,128]{1,0:T(8,128)S(1)} %gram_part.1), channel_id=1, source_target_pairs={{0,48},{16,0},{32,16},{48,32},{64,112},{80,64},{96,80},{112,96},{1... | collective-permute-start | bytes 147464 | tf_op jit(solution)/shard_map/ppermute | solution.py:202
  40.6 1.5 %collective-permute-start.14 = (f32[96,128]{1,0:T(8,128)S(1)}, f32[96,128]{1,0:T(8,128)}, u32[]{:S(2)}, u32[]{:S(2)}) collective-permute-start(f32[96,128]{1,0:T(8,128)S(1)} %gram_part.1), channel_id=1, source_target_pairs={{0,32},{16,48},{32,0},{48,16},{64,96},{80,112},{96,64},{112,80},{1... | collective-permute-start | bytes 147464 | tf_op jit(solution)/shard_map/ppermute | solution.py:202
  42.1 0.8 collective-permute-start.19
  43.0 0.3 collective-permute-start.20
  43.3 0.1 stack.68.place_ref
  43.4 1.7 %collective-permute-done.14 = f32[96,128]{1,0:T(8,128)} collective-permute-done((f32[96,128]{1,0:T(8,128)S(1)}, f32[96,128]{1,0:T(8,128)}, u32[]{:S(2)}, u32[]{:S(2)}) %collective-permute-start.14) | collective-permute-done | bytes 49184 | tf_op jit(solution)/shard_map/ppermute | solution.py:202
  45.1 0.8 add_add_fusion.3
  46.0 2.8 %collective-permute-start.18 = (f32[96,128]{1,0:T(8,128)S(1)}, f32[96,128]{1,0:T(8,128)S(1)}, u32[]{:S(2)}, u32[]{:S(2)}) collective-permute-start(f32[96,128]{1,0:T(8,128)S(1)} %add_add_fusion.3), channel_id=1, source_target_pairs={{0,192},{16,208},{32,224},{48,240},{64,0},{80,16},{96,32},{112,48}... | collective-permute-start | bytes 147464 | tf_op jit(solution)/shard_map/ppermute | solution.py:202
  48.8 0.4 collective-permute-start.17
  49.1 0.7 collective-permute-start.16
  49.8 7.4 %mixed.1 = (f32[128,512]{1,0:T(8,128)S(1)}, f32[128,512]{1,0:T(8,128)S(1)}, f32[128,512]{1,0:T(8,128)S(1)}, f32[128,512]{1,0:T(8,128)S(1)}, bf16[2048,128]{1,0:T(8,128)(2,1)}, /*index=5*/bf16[2048,128]{1,0:T(8,128)(2,1)}) custom-call(s32[1]{0:T(128)} %bitcast.3.place_ref, f32[32,2048]{1,0:T(8,128)} %bitcast.25, ...), custom_call_target="tpu_custom_call" | custom-call | flops 5000000000 | bytes 1048576 | tf_op jit(solution)/shard_map/mixed/pallas_call | solution.py:341
  57.2 0.2 collective-permute-start.21
  57.4 2.3 %collective-permute-start.22 = (f32[128,512]{1,0:T(8,128)S(1)}, f32[128,512]{1,0:T(8,128)S(1)}, u32[]{:S(2)}, u32[]{:S(2)}) collective-permute-start(f32[128,512]{1,0:T(8,128)S(1)} %get-tuple-element.35), channel_id=1, source_target_pairs={{0,32},{16,48},{32,0},{48,16},{64,96},{80,112},{96,64},{112,80},{1... | collective-permute-start | bytes 786440 | tf_op jit(solution)/shard_map/ppermute | solution.py:455
  59.7 1.2 collective-permute-start.23
  60.9 19.9 %all_gather.3.part_ref = f32[1536,128]{1,0:T(8,128)S(1)} all-gather(f32[96,128]{1,0:T(8,128)S(1)} %add_add_fusion.2), channel_id=1, replica_groups=mesh['row'=16,'col'=16] {'col'}, dimensions={0}, use_global_device_ids=true | all-gather | bytes 835584 | tf_op jit(solution)/shard_map/all_gather | solution.py:459
  80.8 0.1 add_add_fusion.1
  80.9 2.1 %collective-permute-start.26 = (f32[128,512]{1,0:T(8,128)S(1)}, f32[128,512]{1,0:T(8,128)S(1)}, u32[]{:S(2)}, u32[]{:S(2)}) collective-permute-start(f32[128,512]{1,0:T(8,128)S(1)} %add_add_fusion.1), channel_id=1, source_target_pairs={{0,192},{16,208},{32,224},{48,240},{64,0},{80,16},{96,32},{112,48}... | collective-permute-start | bytes 786440 | tf_op jit(solution)/shard_map/ppermute | solution.py:202
  82.9 1.4 %collective-permute-start.25 = (f32[128,512]{1,0:T(8,128)S(1)}, f32[128,512]{1,0:T(8,128)S(1)}, u32[]{:S(2)}, u32[]{:S(2)}) collective-permute-start(f32[128,512]{1,0:T(8,128)S(1)} %add_add_fusion.1), channel_id=1, source_target_pairs={{0,128},{16,144},{32,160},{48,176},{64,192},{80,208},{96,224},{112... | collective-permute-start | bytes 786440 | tf_op jit(solution)/shard_map/ppermute | solution.py:202
  84.3 0.0 collective-permute-start.24
  84.4 9.5 %factor_first.1 = (f32[512,512]{1,0:T(8,128)S(1)}, f32[512,512]{1,0:T(8,128)S(1)}) custom-call(f32[1536,128]{1,0:T(8,128)S(1)} %all_gather.3.part_ref), custom_call_target="tpu_custom_call" | custom-call | flops 10000000000 | bytes 1048576 | tf_op jit(solution)/shard_map/factor_first/pallas_call | solution.py:171
  93.8 4.5 %collective-permute-done.24 = f32[128,512]{1,0:T(8,128)S(1)} collective-permute-done((f32[128,512]{1,0:T(8,128)S(1)}, f32[128,512]{1,0:T(8,128)S(1)}, u32[]{:S(2)}, u32[]{:S(2)}) %collective-permute-start.24) | collective-permute-done | bytes 262176 | tf_op jit(solution)/shard_map/ppermute | solution.py:202
  98.3 0.1 add_add_fusion.refs_0_
  98.4 0.1 collective-permute-start.29
  98.5 2.3 %collective-permute-start.28 = (f32[128,512]{1,0:T(8,128)S(1)}, f32[128,512]{1,0:T(8,128)S(1)}, u32[]{:S(2)}, u32[]{:S(2)}) collective-permute-start(f32[128,512]{1,0:T(8,128)S(1)} %add_add_fusion.refs_0_), channel_id=1, source_target_pairs={{0,32},{16,48},{32,0},{48,16},{64,96},{80,112},{96,64},{112,80},{1... | collective-permute-start | bytes 786440 | tf_op jit(solution)/shard_map/ppermute | solution.py:202
  100.8 0.2 collective-permute-start.27
  101.0 7.8 %factor_second.1 = (f32[512,512]{1,0:T(8,128)S(1)}, f32[512,512]{1,0:T(8,128)S(1)}, f32[32,512]{1,0:T(8,128)}) custom-call(s32[1]{0:T(128)} %bitcast.place_ref, f32[512,512]{1,0:T(8,128)S(1)} %get-tuple-element.29.work_in, f32[512,512]{1,0:T(8,128)S(1)} %get-tuple-element.30.upper_in), custom_call_target="tpu_custom_call", output_to_operand_aliasing={{0}: (1, {}), {1}: (2, {})} | custom-call | flops 8000000000 | bytes 1048576 | tf_op jit(solution)/shard_map/factor_second/pallas_call | solution.py:184
  108.8 5.1 %collective-permute-done.27.refs_1_ = f32[128,512]{1,0:T(8,128)S(1)} collective-permute-done((f32[128,512]{1,0:T(8,128)S(1)}, f32[128,512]{1,0:T(8,128)S(1)}, u32[]{:S(2)}, u32[]{:S(2)}) %collective-permute-start.27) | collective-permute-done | bytes 262176 | tf_op jit(solution)/shard_map/ppermute | solution.py:202
  113.9 8.0 %finish.1 = (f32[512,512]{1,0:T(8,128)}, f32[2048,512]{1,0:T(8,128)}) custom-call(s32[17]{0:T(128)S(1)} %stack.68.place_ref, f32[512,512]{1,0:T(8,128)S(1)} %get-tuple-element.32.inverse_ref, f32[128,512]{1,0:T(8,128)S(1)} %add_add_fusion.refs_0_, f32[128,512]{1,0:T(8,128)S(1)} %collective-permute-done.27.refs_1_, ...), custom_call_target="tpu_custom_call" | custom-call | flops 8000000000 | bytes 1048576 | tf_op jit(solution)/shard_map/finish/pallas_call | solution.py:401
  (34 shorter events, 0.1 us)
Async XLA Ops:
  0.6 7.2 %collective-permute-start = (f32[32,2048]{1,0:T(8,128)}, f32[32,2048]{1,0:T(8,128)S(1)}, u32[]{:S(2)}, u32[]{:S(2)}) collective-permute-start(f32[32,2048]{1,0:T(8,128)} %bitcast.21), channel_id=1, source_target_pairs={{0,1},{1,0},{2,3},{3,2},{4,5},{5,4},{6,7},{7,6},{8,9},{9,8},{10,11... | collective-permute-start | bytes 786440 | tf_op jit(solution)/shard_map/ppermute | solution.py:435
  4.0 7.5 %collective-permute-start.1 = (f32[32,2048]{1,0:T(8,128)}, f32[32,2048]{1,0:T(8,128)S(1)}, u32[]{:S(2)}, u32[]{:S(2)}) collective-permute-start(f32[32,2048]{1,0:T(8,128)} %bitcast.22), channel_id=1, source_target_pairs={{0,2},{1,15},{2,4},{3,1},{4,6},{5,3},{6,8},{7,5},{8,10},{9,7},{10,... | collective-permute-start | bytes 786440 | tf_op jit(solution)/shard_map/ppermute | solution.py:432
  7.8 6.6 %collective-permute-start.2 = (f32[32,2048]{1,0:T(8,128)S(1)}, f32[32,2048]{1,0:T(8,128)S(1)}, u32[]{:S(2)}, u32[]{:S(2)}) collective-permute-start(f32[32,2048]{1,0:T(8,128)S(1)} %collective-permute-done.refs_1_.other_ref), channel_id=1, source_target_pairs={{0,2},{1,15},{2,4},{3,1},{4,6},{5,3},{6,8},{7,5},{8,10},{9,7},{10,... | collective-permute-start | bytes 786440 | tf_op jit(solution)/shard_map/ppermute | solution.py:432
  11.4 6.3 %collective-permute-start.3 = (f32[32,2048]{1,0:T(8,128)S(1)}, f32[32,2048]{1,0:T(8,128)S(1)}, u32[]{:S(2)}, u32[]{:S(2)}) collective-permute-start(f32[32,2048]{1,0:T(8,128)S(1)} %collective-permute-done.1.refs_2_.refs_0_), channel_id=1, source_target_pairs={{0,2},{1,15},{2,4},{3,1},{4,6},{5,3},{6,8},{7,5},{8,10},{9,7},{10,... | collective-permute-start | bytes 786440 | tf_op jit(solution)/shard_map/ppermute | solution.py:432
  14.4 6.4 %collective-permute-start.4 = (f32[32,2048]{1,0:T(8,128)S(1)}, f32[32,2048]{1,0:T(8,128)S(1)}, u32[]{:S(2)}, u32[]{:S(2)}) collective-permute-start(f32[32,2048]{1,0:T(8,128)S(1)} %collective-permute-done.2.refs_3_.refs_1_), channel_id=1, source_target_pairs={{0,2},{1,15},{2,4},{3,1},{4,6},{5,3},{6,8},{7,5},{8,10},{9,7},{10,... | collective-permute-start | bytes 786440 | tf_op jit(solution)/shard_map/ppermute | solution.py:432
  17.3 5.9 %collective-permute-start.9 = (f32[32,2048]{1,0:T(8,128)S(1)}, f32[32,2048]{1,0:T(8,128)S(1)}, u32[]{:S(2)}, u32[]{:S(2)}) collective-permute-start(f32[32,2048]{1,0:T(8,128)S(1)} %collective-permute-done.1.refs_2_.refs_0_), channel_id=1, source_target_pairs={{0,1},{1,0},{2,3},{3,2},{4,5},{5,4},{6,7},{7,6},{8,9},{9,8},{10,11... | collective-permute-start | bytes 786440 | tf_op jit(solution)/shard_map/ppermute | solution.py:435
  17.8 9.6 %collective-permute-start.11 = (f32[32,2048]{1,0:T(8,128)S(1)}, f32[32,2048]{1,0:T(8,128)S(1)}, u32[]{:S(2)}, u32[]{:S(2)}) collective-permute-start(f32[32,2048]{1,0:T(8,128)S(1)} %collective-permute-done.3.refs_6_.refs_2_), channel_id=1, source_target_pairs={{0,1},{1,0},{2,3},{3,2},{4,5},{5,4},{6,7},{7,6},{8,9},{9,8},{10,11... | collective-permute-start | bytes 786440 | tf_op jit(solution)/shard_map/ppermute | solution.py:435
  20.3 5.5 %collective-permute-start.5 = (f32[32,2048]{1,0:T(8,128)S(1)}, f32[32,2048]{1,0:T(8,128)S(1)}, u32[]{:S(2)}, u32[]{:S(2)}) collective-permute-start(f32[32,2048]{1,0:T(8,128)S(1)} %collective-permute-done.3.refs_6_.refs_2_), channel_id=1, source_target_pairs={{0,2},{1,15},{2,4},{3,1},{4,6},{5,3},{6,8},{7,5},{8,10},{9,7},{10,... | collective-permute-start | bytes 786440 | tf_op jit(solution)/shard_map/ppermute | solution.py:432
  20.9 6.4 %collective-permute-start.8 = (f32[32,2048]{1,0:T(8,128)S(1)}, f32[32,2048]{1,0:T(8,128)S(1)}, u32[]{:S(2)}, u32[]{:S(2)}) collective-permute-start(f32[32,2048]{1,0:T(8,128)S(1)} %collective-permute-done.2.refs_3_.refs_1_), channel_id=1, source_target_pairs={{0,1},{1,0},{2,3},{3,2},{4,5},{5,4},{6,7},{7,6},{8,9},{9,8},{10,11... | collective-permute-start | bytes 786440 | tf_op jit(solution)/shard_map/ppermute | solution.py:435
  20.9 6.4 %collective-permute-start.10 = (f32[32,2048]{1,0:T(8,128)S(1)}, f32[32,2048]{1,0:T(8,128)S(1)}, u32[]{:S(2)}, u32[]{:S(2)}) collective-permute-start(f32[32,2048]{1,0:T(8,128)S(1)} %collective-permute-done.4.refs_7_.refs_3_), channel_id=1, source_target_pairs={{0,1},{1,0},{2,3},{3,2},{4,5},{5,4},{6,7},{7,6},{8,9},{9,8},{10,11... | collective-permute-start | bytes 786440 | tf_op jit(solution)/shard_map/ppermute | solution.py:435
  23.1 5.5 %collective-permute-start.6 = (f32[32,2048]{1,0:T(8,128)S(1)}, f32[32,2048]{1,0:T(8,128)S(1)}, u32[]{:S(2)}, u32[]{:S(2)}) collective-permute-start(f32[32,2048]{1,0:T(8,128)S(1)} %collective-permute-done.4.refs_7_.refs_3_), channel_id=1, source_target_pairs={{0,2},{1,15},{2,4},{3,1},{4,6},{5,3},{6,8},{7,5},{8,10},{9,7},{10,... | collective-permute-start | bytes 786440 | tf_op jit(solution)/shard_map/ppermute | solution.py:432
  25.8 5.8 %collective-permute-start.7 = (f32[32,2048]{1,0:T(8,128)S(1)}, f32[32,2048]{1,0:T(8,128)S(1)}, u32[]{:S(2)}, u32[]{:S(2)}) collective-permute-start(f32[32,2048]{1,0:T(8,128)S(1)} %collective-permute-done.5.refs_10_.refs_4_), channel_id=1, source_target_pairs={{0,2},{1,15},{2,4},{3,1},{4,6},{5,3},{6,8},{7,5},{8,10},{9,7},{10,... | collective-permute-start | bytes 786440 | tf_op jit(solution)/shard_map/ppermute | solution.py:432
  31.6 11.8 %collective-permute-start.12 = (f32[32,2048]{1,0:T(8,128)S(1)}, f32[32,2048]{1,0:T(8,128)S(1)}, u32[]{:S(2)}, u32[]{:S(2)}) collective-permute-start(f32[32,2048]{1,0:T(8,128)S(1)} %collective-permute-done.6.refs_11_.refs_5_), channel_id=1, source_target_pairs={{0,1},{1,0},{2,3},{3,2},{4,5},{5,4},{6,7},{7,6},{8,9},{9,8},{10,11... | collective-permute-start | bytes 786440 | tf_op jit(solution)/shard_map/ppermute | solution.py:435
  37.8 5.1 %collective-permute-start.13 = (f32[96,128]{1,0:T(8,128)S(1)}, f32[96,128]{1,0:T(8,128)S(1)}, u32[]{:S(2)}, u32[]{:S(2)}) collective-permute-start(f32[96,128]{1,0:T(8,128)S(1)} %gram_part.1), channel_id=1, source_target_pairs={{0,16},{16,32},{32,48},{48,0},{64,80},{80,96},{96,112},{112,64},{1... | collective-permute-start | bytes 147464 | tf_op jit(solution)/shard_map/ppermute | solution.py:202
  39.1 4.3 %collective-permute-start.15 = (f32[96,128]{1,0:T(8,128)S(1)}, f32[96,128]{1,0:T(8,128)}, u32[]{:S(2)}, u32[]{:S(2)}) collective-permute-start(f32[96,128]{1,0:T(8,128)S(1)} %gram_part.1), channel_id=1, source_target_pairs={{0,48},{16,0},{32,16},{48,32},{64,112},{80,64},{96,80},{112,96},{1... | collective-permute-start | bytes 147464 | tf_op jit(solution)/shard_map/ppermute | solution.py:202
  40.6 4.6 %collective-permute-start.14 = (f32[96,128]{1,0:T(8,128)S(1)}, f32[96,128]{1,0:T(8,128)}, u32[]{:S(2)}, u32[]{:S(2)}) collective-permute-start(f32[96,128]{1,0:T(8,128)S(1)} %gram_part.1), channel_id=1, source_target_pairs={{0,32},{16,48},{32,0},{48,16},{64,96},{80,112},{96,64},{112,80},{1... | collective-permute-start | bytes 147464 | tf_op jit(solution)/shard_map/ppermute | solution.py:202
  42.1 7.7 %collective-permute-start.19 = (f32[32,2048]{1,0:T(8,128)S(1)}, f32[32,2048]{1,0:T(8,128)}, u32[]{:S(2)}, u32[]{:S(2)}) collective-permute-start(f32[32,2048]{1,0:T(8,128)S(1)} %collective-permute-done.5.refs_10_.refs_4_), channel_id=1, source_target_pairs={{0,1},{1,0},{2,3},{3,2},{4,5},{5,4},{6,7},{7,6},{8,9},{9,8},{10,11... | collective-permute-start | bytes 786440 | tf_op jit(solution)/shard_map/ppermute | solution.py:435
  43.0 6.9 %collective-permute-start.20 = (f32[32,2048]{1,0:T(8,128)S(1)}, f32[32,2048]{1,0:T(8,128)}, u32[]{:S(2)}, u32[]{:S(2)}) collective-permute-start(f32[32,2048]{1,0:T(8,128)S(1)} %collective-permute-done.7.refs_6_.refs_14_), channel_id=1, source_target_pairs={{0,1},{1,0},{2,3},{3,2},{4,5},{5,4},{6,7},{7,6},{8,9},{9,8},{10,11... | collective-permute-start | bytes 786440 | tf_op jit(solution)/shard_map/ppermute | solution.py:435
  46.0 13.8 %collective-permute-start.18 = (f32[96,128]{1,0:T(8,128)S(1)}, f32[96,128]{1,0:T(8,128)S(1)}, u32[]{:S(2)}, u32[]{:S(2)}) collective-permute-start(f32[96,128]{1,0:T(8,128)S(1)} %add_add_fusion.3), channel_id=1, source_target_pairs={{0,192},{16,208},{32,224},{48,240},{64,0},{80,16},{96,32},{112,48}... | collective-permute-start | bytes 147464 | tf_op jit(solution)/shard_map/ppermute | solution.py:202
  48.8 12.1 %collective-permute-start.17 = (f32[96,128]{1,0:T(8,128)S(1)}, f32[96,128]{1,0:T(8,128)S(1)}, u32[]{:S(2)}, u32[]{:S(2)}) collective-permute-start(f32[96,128]{1,0:T(8,128)S(1)} %add_add_fusion.3), channel_id=1, source_target_pairs={{0,128},{16,144},{32,160},{48,176},{64,192},{80,208},{96,224},{112... | collective-permute-start | bytes 147464 | tf_op jit(solution)/shard_map/ppermute | solution.py:202
  49.1 11.8 %collective-permute-start.16 = (f32[96,128]{1,0:T(8,128)S(1)}, f32[96,128]{1,0:T(8,128)S(1)}, u32[]{:S(2)}, u32[]{:S(2)}) collective-permute-start(f32[96,128]{1,0:T(8,128)S(1)} %add_add_fusion.3), channel_id=1, source_target_pairs={{0,64},{16,80},{32,96},{48,112},{64,128},{80,144},{96,160},{112,17... | collective-permute-start | bytes 147464 | tf_op jit(solution)/shard_map/ppermute | solution.py:202
  57.2 23.6 %collective-permute-start.21 = (f32[128,512]{1,0:T(8,128)S(1)}, f32[128,512]{1,0:T(8,128)S(1)}, u32[]{:S(2)}, u32[]{:S(2)}) collective-permute-start(f32[128,512]{1,0:T(8,128)S(1)} %get-tuple-element.34), channel_id=1, source_target_pairs={{0,16},{16,32},{32,48},{48,0},{64,80},{80,96},{96,112},{112,64},{1... | collective-permute-start | bytes 786440 | tf_op jit(solution)/shard_map/ppermute | solution.py:455
  57.4 23.3 %collective-permute-start.22 = (f32[128,512]{1,0:T(8,128)S(1)}, f32[128,512]{1,0:T(8,128)S(1)}, u32[]{:S(2)}, u32[]{:S(2)}) collective-permute-start(f32[128,512]{1,0:T(8,128)S(1)} %get-tuple-element.35), channel_id=1, source_target_pairs={{0,32},{16,48},{32,0},{48,16},{64,96},{80,112},{96,64},{112,80},{1... | collective-permute-start | bytes 786440 | tf_op jit(solution)/shard_map/ppermute | solution.py:455
  59.7 21.0 %collective-permute-start.23 = (f32[128,512]{1,0:T(8,128)S(1)}, f32[128,512]{1,0:T(8,128)S(1)}, u32[]{:S(2)}, u32[]{:S(2)}) collective-permute-start(f32[128,512]{1,0:T(8,128)S(1)} %get-tuple-element.36), channel_id=1, source_target_pairs={{0,48},{16,0},{32,16},{48,32},{64,112},{80,64},{96,80},{112,96},{1... | collective-permute-start | bytes 786440 | tf_op jit(solution)/shard_map/ppermute | solution.py:455
  80.9 12.9 %collective-permute-start.26 = (f32[128,512]{1,0:T(8,128)S(1)}, f32[128,512]{1,0:T(8,128)S(1)}, u32[]{:S(2)}, u32[]{:S(2)}) collective-permute-start(f32[128,512]{1,0:T(8,128)S(1)} %add_add_fusion.1), channel_id=1, source_target_pairs={{0,192},{16,208},{32,224},{48,240},{64,0},{80,16},{96,32},{112,48}... | collective-permute-start | bytes 786440 | tf_op jit(solution)/shard_map/ppermute | solution.py:202
  82.9 10.9 %collective-permute-start.25 = (f32[128,512]{1,0:T(8,128)S(1)}, f32[128,512]{1,0:T(8,128)S(1)}, u32[]{:S(2)}, u32[]{:S(2)}) collective-permute-start(f32[128,512]{1,0:T(8,128)S(1)} %add_add_fusion.1), channel_id=1, source_target_pairs={{0,128},{16,144},{32,160},{48,176},{64,192},{80,208},{96,224},{112... | collective-permute-start | bytes 786440 | tf_op jit(solution)/shard_map/ppermute | solution.py:202
  84.3 13.9 %collective-permute-start.24 = (f32[128,512]{1,0:T(8,128)S(1)}, f32[128,512]{1,0:T(8,128)S(1)}, u32[]{:S(2)}, u32[]{:S(2)}) collective-permute-start(f32[128,512]{1,0:T(8,128)S(1)} %add_add_fusion.1), channel_id=1, source_target_pairs={{0,64},{16,80},{32,96},{48,112},{64,128},{80,144},{96,160},{112,17... | collective-permute-start | bytes 786440 | tf_op jit(solution)/shard_map/ppermute | solution.py:202
  98.4 10.4 %collective-permute-start.29 = (f32[128,512]{1,0:T(8,128)S(1)}, f32[128,512]{1,0:T(8,128)S(1)}, u32[]{:S(2)}, u32[]{:S(2)}) collective-permute-start(f32[128,512]{1,0:T(8,128)S(1)} %add_add_fusion.refs_0_), channel_id=1, source_target_pairs={{0,48},{16,0},{32,16},{48,32},{64,112},{80,64},{96,80},{112,96},{1... | collective-permute-start | bytes 786440 | tf_op jit(solution)/shard_map/ppermute | solution.py:202
  98.5 10.3 %collective-permute-start.28 = (f32[128,512]{1,0:T(8,128)S(1)}, f32[128,512]{1,0:T(8,128)S(1)}, u32[]{:S(2)}, u32[]{:S(2)}) collective-permute-start(f32[128,512]{1,0:T(8,128)S(1)} %add_add_fusion.refs_0_), channel_id=1, source_target_pairs={{0,32},{16,48},{32,0},{48,16},{64,96},{80,112},{96,64},{112,80},{1... | collective-permute-start | bytes 786440 | tf_op jit(solution)/shard_map/ppermute | solution.py:202
  100.8 13.1 %collective-permute-start.27 = (f32[128,512]{1,0:T(8,128)S(1)}, f32[128,512]{1,0:T(8,128)S(1)}, u32[]{:S(2)}, u32[]{:S(2)}) collective-permute-start(f32[128,512]{1,0:T(8,128)S(1)} %add_add_fusion.refs_0_), channel_id=1, source_target_pairs={{0,16},{16,32},{32,48},{48,0},{64,80},{80,96},{96,112},{112,64},{1... | collective-permute-start | bytes 786440 | tf_op jit(solution)/shard_map/ppermute | solution.py:202
  101.0 12.9 %copy-start = (f32[2048,512]{1,0:T(8,128)S(1)}, f32[2048,512]{1,0:T(8,128)}, u32[]{:S(2)}) copy-start(f32[2048,512]{1,0:T(8,128)} %refs_8_.1) | copy-start | bytes 12582916
  101.0 12.9 %copy-start.1 = (bf16[2048,384]{1,0:T(8,128)(2,1)S(1)}, bf16[2048,384]{1,0:T(8,128)(2,1)}, u32[]{:S(2)}) copy-start(bf16[2048,384]{1,0:T(8,128)(2,1)} %get-tuple-element.37.refs_4_) | copy-start | bytes 4718596
  101.0 12.9 %copy-start.2 = (bf16[2048,384]{1,0:T(8,128)(2,1)S(1)}, bf16[2048,384]{1,0:T(8,128)(2,1)}, u32[]{:S(2)}) copy-start(bf16[2048,384]{1,0:T(8,128)(2,1)} %get-tuple-element.39.refs_6_) | copy-start | bytes 4718596
  101.0 12.9 %copy-start.3 = (bf16[2048,128]{1,0:T(8,128)(2,1)S(1)}, bf16[2048,128]{1,0:T(8,128)(2,1)}, u32[]{:S(2)}) copy-start(bf16[2048,128]{1,0:T(8,128)(2,1)} %get-tuple-element.38.refs_5_) | copy-start | bytes 1572868
  101.0 12.9 %copy-start.4 = (bf16[2048,128]{1,0:T(8,128)(2,1)S(1)}, bf16[2048,128]{1,0:T(8,128)(2,1)}, u32[]{:S(2)}) copy-start(bf16[2048,128]{1,0:T(8,128)(2,1)} %get-tuple-element.40.refs_7_) | copy-start | bytes 1572868

commit v3 on v2

--- a/solution.py
+++ b/solution.py
@@ -140,10 +140,35 @@
     eliminate(0, steps, work_ref, upper_ref)
 
 
-def second_kernel(begin, place_ref, work_in, upper_in, work_ref, upper_ref, own_ref, turned_ref):
+def split(value):
+    high = value.astype(jnp.bfloat16)
+    return high, (value - high.astype(jnp.float32)).astype(jnp.bfloat16)
+
+
+def three_products(left, right, left_dim, right_dim):
+    def one(a, b):
+        return lax.dot_general(a, b, (((left_dim,), (right_dim,)), ((), ())), preferred_element_type=jnp.float32)
+
+    return one(left[0], right[0]) + (one(left[0], right[1]) + one(left[1], right[0]))
+
+
+def second_kernel(begin, place_ref, work_in, upper_in, work_ref, upper_ref, own_ref, *refs):
+    by_piece_refs, by_block_refs, (turned_ref, inverse_ref) = refs[:2], refs[2:4], refs[4:]
     size = work_ref.shape[0]
-
+    count = size // NARROW
     eliminate(begin, size // BLOCK, work_ref, upper_ref)
+    inverse_ref[...] = work_ref[...].T
+
+    def rows(at):
+        return inverse_ref[pl.ds(pl.multiple_of(place_ref[at] * NARROW, NARROW), NARROW), :]
+
+    near = split(jnp.concatenate([rows(i) for i in range(count)], 0))
+    quarter = count // SIDE
+    first = [lax.rem(place_ref[count] - k + SIDE, SIDE) * quarter for k in range(SIDE)]
+    pieces = split(jnp.concatenate([rows(first[k] + j) for k in range(SIDE) for j in range(quarter)], 0).T)
+    for i in range(2):
+        by_block_refs[i][...] = near[i]
+        by_piece_refs[i][...] = pieces[i]
     first = place_ref[0] * NARROW
     group = pl.multiple_of(first // BLOCK * BLOCK, BLOCK)
     turned_ref[...] = upper_ref[:, pl.ds(group, BLOCK)].T
@@ -173,25 +198,27 @@
         out_shape=[jax.ShapeDtypeStruct((size, size), jnp.float32)] * 2,
         in_specs=[VMEM],
         out_specs=[VMEM] * 2,
-        compiler_params=pltpu.CompilerParams(vmem_limit_bytes=16 << 20),
+        compiler_params=pltpu.CompilerParams(vmem_limit_bytes=10 << 20),
         cost_estimate=cost(10_000_000_000),
         name="factor_first",
     )(parts)
 
 
-def factor_second(work, upper, begin):
+def factor_second(places, work, upper, begin):
     size = work.shape[0]
+    whole = jax.ShapeDtypeStruct((size, size), jnp.float32)
     return pl.pallas_call(
         functools.partial(second_kernel, begin),
-        out_shape=[jax.ShapeDtypeStruct((size, size), jnp.float32)] * 2 + [jax.ShapeDtypeStruct((NARROW, size), jnp.float32)],
+        out_shape=[whole, whole, jax.ShapeDtypeStruct((NARROW, size), jnp.float32)]
+        + [pltpu.VMEM((size, size), jnp.bfloat16)] * 4,
         in_specs=[SMEM, VMEM, VMEM],
-        out_specs=[VMEM] * 3,
-        scratch_shapes=[pltpu.VMEM((BLOCK, size), jnp.float32)],
+        out_specs=[VMEM] * 7,
+        scratch_shapes=[pltpu.VMEM((BLOCK, size), jnp.float32), pltpu.VMEM((size, size), jnp.float32)],
         input_output_aliases={1: 0, 2: 1},
-        compiler_params=pltpu.CompilerParams(vmem_limit_bytes=16 << 20),
+        compiler_params=pltpu.CompilerParams(vmem_limit_bytes=12 << 20),
         cost_estimate=cost(8_000_000_000),
         name="factor_second",
-    )(scalar(lax.axis_index("col")), work, upper)
+    )(places, work, upper)
 
 
 def shifted(dy, dx):
@@ -209,30 +236,12 @@
 LINES = [[y * SIDE + x for x in range(SIDE)] for y in range(SIDE)]
 
 
-def split(value):
-    high = value.astype(jnp.bfloat16)
-    return high, (value - high.astype(jnp.float32)).astype(jnp.bfloat16)
-
-
-def three_products(left, right, left_dim, right_dim):
-    def one(a, b):
-        return lax.dot_general(a, b, (((left_dim,), (right_dim,)), ((), ())), preferred_element_type=jnp.float32)
-
-    return one(left[0], right[0]) + (one(left[0], right[1]) + one(left[1], right[0]))
-
-
 def part_kernel(core_ref, own_ref, other_ref, *refs):
-    part_ref, own, sem = refs[-3:]
-    refs = refs[:-2]
-    load = pltpu.make_async_copy(own_ref, own, sem)
-    load.start()
-    load.wait()
-    own_ref = own
+    part_ref = refs[-1]
     narrow = own_ref.shape[0]
     even = core_ref[0] == 0
-    blocks = jnp.concatenate([own_ref[...], other_ref[...]] + [ref[...] for ref in refs[:-1]], 0)
-    count, pair = blocks.shape[0], 2 * narrow
-    left = three_parts(blocks)
+    left = three_parts(jnp.concatenate([own_ref[...], other_ref[...]] + [ref[...] for ref in refs[:-1]], 0))
+    count, pair = left[0].shape[0], 2 * narrow
     right = jnp.concatenate([part[:pair] for part in left], 0)
     products = lax.dot_general(
         jnp.concatenate(left, 0), right, (((1,), (1,)), ((), ())), preferred_element_type=jnp.float32
@@ -258,73 +267,69 @@
     return pl.pallas_call(
         part_kernel,
         out_shape=jax.ShapeDtypeStruct((3 * NARROW, 4 * NARROW), jnp.float32),
-        in_specs=[SMEM, HBM] + [VMEM] * (1 + len(blocks)),
+        in_specs=[SMEM] + [VMEM] * (2 + len(blocks)),
         out_specs=VMEM,
-        scratch_shapes=[pltpu.VMEM(own.shape, jnp.float32), pltpu.SemaphoreType.DMA],
-        compiler_params=pltpu.CompilerParams(vmem_limit_bytes=16 << 20),
+        compiler_params=pltpu.CompilerParams(vmem_limit_bytes=10 << 20),
         cost_estimate=cost(2_000_000_000),
         name="gram_part",
-    )(scalar(lax.rem(lax.axis_index("col"), 2)), pltpu.with_memory_space_constraint(own, pltpu.HBM), in_vmem(other), *[in_vmem(block) for block in blocks])
-
-
-def turn_kernel(tile, *refs):
-    own_ref, *blocks, high_ref, low_ref, own, high, low, sems = refs
-    load = pltpu.make_async_copy(own_ref, own, sems.at[0])
-    load.start()
-    load.wait()
+    )(scalar(lax.rem(lax.axis_index("col"), 2)), *[in_vmem(block) for block in (own, other, *blocks)])
+
+
+def products_and_turned(tile, blocks, taken, loads, trailing_into, kept, outs, sems):
     stores = []
-    for t in range(high.shape[0]):
-        rows = jnp.concatenate([ref[:, t * tile : (t + 1) * tile] for ref in [own] + blocks], 0)
-        here = pl.ds(t * tile, tile)
-        for value, kept, out, i in zip(split(rows.T), (high, low), (high_ref, low_ref), range(2)):
-            kept[t] = value
-            stores.append(pltpu.make_async_copy(kept.at[t], out.at[here, :], sems.at[1 + 2 * t + i]))
+    for t, load in enumerate(loads):
+        rows = split(jnp.concatenate([ref[:, t * tile : (t + 1) * tile] for ref in blocks], 0))
+        for value, turned, out, i in zip(rows, kept, outs, range(2)):
+            turned[t] = value.T
+            stores.append(pltpu.make_async_copy(turned.at[t], out.at[pl.ds(t * tile, tile), :], sems.at[2 * t + i]))
             stores[-1].start()
+        load.wait()
+        trailing_into(t, three_products(rows, split(taken[t]), 1, 0))
+    return stores
+
+
+def load_tiles(tile, trailing_ref, taken, sems):
+    loads = [
+        pltpu.make_async_copy(trailing_ref.at[pl.ds(t * tile, tile), :], taken.at[t], sems.at[t])
+        for t in range(taken.shape[0])
+    ]
+    for load in loads:
+        load.start()
+    return loads
+
+
+def mixed_kernel(tile, own_ref, *refs):
+    *blocks, trailing_ref, mixed_ref, own, high_ref, low_ref, taken, high, low, loads_sem, stores_sem, whole = refs
+    load_own = pltpu.make_async_copy(own_ref, own, loads_sem.at[taken.shape[0]])
+    load_own.start()
+    loads = load_tiles(tile, trailing_ref, taken, loads_sem)
+
+    def put(t, product):
+        whole[...] = product if t == 0 else whole[...] + product
+
+    load_own.wait()
+    outs = high_ref, low_ref
+    stores = products_and_turned(tile, [own] + blocks, taken, loads, put, (high, low), outs, stores_sem)
+    stores.append(pltpu.make_async_copy(whole, mixed_ref, loads_sem.at[0]))
+    stores[-1].start()
     for store in stores:
         store.wait()
 
 
-def turn(blocks, tile):
-    count = sum(block.shape[0] for block in blocks)
-    depth = blocks[0].shape[1]
-    tiles = depth // tile
-    return pl.pallas_call(
-        functools.partial(turn_kernel, tile),
-        out_shape=[pltpu.HBM((depth, count), jnp.bfloat16)] * 2,
-        in_specs=[HBM] + [VMEM] * (len(blocks) - 1),
-        out_specs=[HBM, HBM],
-        scratch_shapes=[pltpu.VMEM(blocks[0].shape, jnp.float32)]
-        + [pltpu.VMEM((tiles, tile, count), jnp.bfloat16)] * 2
-        + [pltpu.SemaphoreType.DMA((2 * tiles + 1,))],
-        compiler_params=pltpu.CompilerParams(vmem_limit_bytes=16 << 20),
-        cost_estimate=cost(3_000_000_000),
-        name="turn",
-    )(pltpu.with_memory_space_constraint(blocks[0], pltpu.HBM), *[in_vmem(block) for block in blocks[1:]])
-
-
-def mixed_kernel(tile, turned, place_ref, *refs):
-    own_ref, *blocks = refs[: -(10 + SIDE)]
-    trailing_ref, *quarter_refs = refs[-(10 + SIDE) : -9]
-    high_ref, low_ref, own, taken, high, low, loads_sem, stores_sem, whole = refs[-9:]
-    tiles = taken.shape[0]
-    here = [pl.ds(t * tile, tile) for t in range(tiles)]
-    load_own = pltpu.make_async_copy(own_ref, own, loads_sem.at[tiles])
-    load_own.start()
-    loads = [pltpu.make_async_copy(trailing_ref.at[here[t], :], taken.at[t], loads_sem.at[t]) for t in range(tiles)]
-    for load in loads:
-        load.start()
-    load_own.wait()
-    blocks = [own] + blocks
-    stores = []
-    for t in range(tiles):
-        rows = split(jnp.concatenate([ref[:, t * tile : (t + 1) * tile] for ref in blocks], 0))
-        loads[t].wait()
-        product = three_products(rows, split(taken[t]), 1, 0)
-        whole[...] = product if t == 0 else whole[...] + product
-        for value, kept, out, i in ((rows[0], high, high_ref, 0), (rows[1], low, low_ref, 1)):
-            kept[t] = value[-turned:].T
-            stores.append(pltpu.make_async_copy(kept.at[t], out.at[here[t], :], stores_sem.at[2 * t + i]))
-            stores[-1].start()
+def mixed_last_kernel(tile, place_ref, done_ref, *refs):
+    *blocks, trailing_ref = refs[: -(SIDE + 8)]
+    quarter_refs, (high_ref, low_ref, taken, high, low, loads_sem, stores_sem, whole) = refs[-(SIDE + 8) : -8], refs[-8:]
+    loads = load_tiles(tile, trailing_ref, taken, loads_sem)
+    count = done_ref.shape[0]
+    load_done = pltpu.make_async_copy(done_ref, whole.at[pl.ds(0, count), :], loads_sem.at[taken.shape[0]])
+    load_done.start()
+
+    def put(t, product):
+        whole[count:, :] = product if t == 0 else whole[count:, :] + product
+
+    outs = high_ref, low_ref
+    stores = products_and_turned(tile, blocks, taken, loads, put, (high, low), outs, stores_sem)
+    load_done.wait()
     size = whole.shape[0] // SIDE
     for k in range(SIDE):
         quarter_refs[k][...] = whole[pl.ds(pl.multiple_of(lax.rem(place_ref[0] + k, SIDE) * size, size), size), :]
@@ -332,60 +337,71 @@
         store.wait()
 
 
-def mix(early, late, trailing, tile):
+def scratch_for(depth, across, count, tile):
+    tiles = depth // tile
+    return [
+        pltpu.VMEM((tiles, tile, across), jnp.float32),
+        pltpu.VMEM((tiles, tile, count), jnp.bfloat16),
+        pltpu.VMEM((tiles, tile, count), jnp.bfloat16),
+        pltpu.SemaphoreType.DMA((tiles + 1,)),
+        pltpu.SemaphoreType.DMA((2 * tiles,)),
+    ]
+
+
+def mix(blocks, trailing, tile):
+    count = sum(block.shape[0] for block in blocks)
     depth, across = trailing.shape
-    tiles = depth // tile
-    blocks = early + late
-    width = sum(block.shape[0] for block in blocks)
-    turned = sum(block.shape[0] for block in late)
     return pl.pallas_call(
-        functools.partial(mixed_kernel, tile, turned),
-        out_shape=[jax.ShapeDtypeStruct((width // SIDE, across), jnp.float32)] * SIDE
-        + [pltpu.HBM((depth, turned), jnp.bfloat16)] * 2,
-        in_specs=[SMEM, HBM] + [VMEM] * (len(blocks) - 1) + [HBM],
-        out_specs=[VMEM] * SIDE + [HBM, HBM],
-        scratch_shapes=[
-            pltpu.VMEM(blocks[0].shape, jnp.float32),
-            pltpu.VMEM((tiles, tile, across), jnp.float32),
-            pltpu.VMEM((tiles, tile, turned), jnp.bfloat16),
-            pltpu.VMEM((tiles, tile, turned), jnp.bfloat16),
-            pltpu.SemaphoreType.DMA((tiles + 1,)),
-            pltpu.SemaphoreType.DMA((2 * tiles,)),
-            pltpu.VMEM((width, across), jnp.float32),
-        ],
-        compiler_params=pltpu.CompilerParams(vmem_limit_bytes=20 << 20),
-        cost_estimate=cost(5_000_000_000),
+        functools.partial(mixed_kernel, tile),
+        out_shape=[pltpu.HBM((count, across), jnp.float32), pltpu.VMEM(blocks[0].shape, jnp.float32)]
+        + [pltpu.HBM((depth, count), jnp.bfloat16)] * 2,
+        in_specs=[HBM] + [VMEM] * (len(blocks) - 1) + [HBM],
+        out_specs=[HBM, VMEM, HBM, HBM],
+        scratch_shapes=scratch_for(depth, across, count, tile) + [pltpu.VMEM((count, across), jnp.float32)],
+        compiler_params=pltpu.CompilerParams(vmem_limit_bytes=14 << 20),
+        cost_estimate=cost(3_000_000_000),
         name="mixed",
     )(
-        scalar(lax.rem(lax.axis_index("row"), SIDE)),
         pltpu.with_memory_space_constraint(blocks[0], pltpu.HBM),
         *[in_vmem(block) for block in blocks[1:]],
         pltpu.with_memory_space_constraint(trailing, pltpu.HBM),
     )
 
 
-def last_kernel(tile, place_ref, inverse_ref, *refs):
-    pieces, refs = refs[:SIDE], refs[SIDE:]
+def mix_last(done, blocks, trailing, tile):
+    count = sum(block.shape[0] for block in blocks)
+    depth, across = trailing.shape
+    width = done.shape[0] + count
+    return pl.pallas_call(
+        functools.partial(mixed_last_kernel, tile),
+        out_shape=[jax.ShapeDtypeStruct((width // SIDE, across), jnp.float32)] * SIDE
+        + [pltpu.HBM((depth, count), jnp.bfloat16)] * 2,
+        in_specs=[SMEM, HBM] + [VMEM] * len(blocks) + [HBM],
+        out_specs=[VMEM] * SIDE + [HBM, HBM],
+        scratch_shapes=scratch_for(depth, across, count, tile) + [pltpu.VMEM((width, across), jnp.float32)],
+        compiler_params=pltpu.CompilerParams(vmem_limit_bytes=12 << 20),
+        cost_estimate=cost(3_000_000_000),
+        name="mixed_last",
+    )(
+        scalar(lax.rem(lax.axis_index("row"), SIDE)),
+        pltpu.with_memory_space_constraint(done, pltpu.HBM),
+        *[in_vmem(block) for block in blocks],
+        pltpu.with_memory_space_constraint(trailing, pltpu.HBM),
+    )
+
+
+def last_kernel(tile, *refs):
+    by_piece, by_block, pieces, refs = refs[:2], refs[2:4], refs[4 : 4 + SIDE], refs[4 + SIDE :]
     highs, lows, refs = refs[:2], refs[2:4], refs[4:]
-    trailing_ref, top_ref, out_ref, rows, tiles, sems = refs
-    width = inverse_ref.shape[0]
-    count = width // NARROW
-    quarter = count // SIDE
-
-    def placed(i):
-        return pl.ds(pl.multiple_of(place_ref[i] * NARROW, NARROW), NARROW)
-
-    for k in range(SIDE):
-        for j in range(quarter):
-            at = placed(lax.rem(place_ref[count] - k + SIDE, SIDE) * quarter + j)
-            rows[at, :] = pieces[k][j * NARROW : (j + 1) * NARROW, :]
-    inverse = split(inverse_ref[...])
-    top = three_products(inverse, split(rows[...]), 1, 0)
-    top_ref[...] = top
-    rows[...] = three_products(inverse, split(top), 0, 0)
-    weights = split(jnp.concatenate([rows[placed(i), :] for i in range(count)], 0))
-    copies = []
-    for t in range(trailing_ref.shape[0] // tile):
+    trailing_ref, top_ref, out_ref, top, tiles, sems = refs
+    count = tiles.shape[0]
+    values = split(jnp.concatenate([ref[...] for ref in pieces], 0))
+    product = three_products([ref[...] for ref in by_piece], values, 1, 0)
+    top[...] = product
+    copies = [pltpu.make_async_copy(top, top_ref, sems.at[count])]
+    copies[0].start()
+    weights = split(three_products([ref[...] for ref in by_block], split(product), 1, 0))
+    for t in range(count):
         here = slice(t * tile, (t + 1) * tile)
         left = [jnp.concatenate([a[here, :], b[here, :]], 1) for a, b in (highs, lows)]
         tiles[t] = trailing_ref[here, :] - three_products(left, weights, 1, 0)
@@ -395,23 +411,28 @@
         copy.wait()
 
 
-def finish(places, inverse_t, pieces, highs, lows, trailing, tile):
+def finish(by_piece, by_block, pieces, highs, lows, trailing, tile):
     depth, across = trailing.shape
-    width = inverse_t.shape[0]
+    width = by_block[0].shape[0]
+    tiles = depth // tile
+    operands = *by_piece, *by_block, *pieces, *highs, *lows, trailing
     return pl.pallas_call(
         functools.partial(last_kernel, tile),
         out_shape=[
             jax.ShapeDtypeStruct((width, across), jnp.float32),
             jax.ShapeDtypeStruct((depth, across), jnp.float32),
         ],
-        in_specs=[SMEM] + [VMEM] * (2 + SIDE + 2 * len(highs)),
-        out_specs=[VMEM, pl.BlockSpec(memory_space=pl.ANY)],
-        scratch_shapes=[pltpu.VMEM((width, across), jnp.float32)]
-        + [pltpu.VMEM((depth // tile, tile, across), jnp.float32), pltpu.SemaphoreType.DMA((depth // tile,))],
-        compiler_params=pltpu.CompilerParams(vmem_limit_bytes=24 << 20),
+        in_specs=[VMEM] * len(operands),
+        out_specs=[pl.BlockSpec(memory_space=pl.ANY)] * 2,
+        scratch_shapes=[
+            pltpu.VMEM((width, across), jnp.float32),
+            pltpu.VMEM((tiles, tile, across), jnp.float32),
+            pltpu.SemaphoreType.DMA((tiles + 1,)),
+        ],
+        compiler_params=pltpu.CompilerParams(vmem_limit_bytes=16 << 20),
         cost_estimate=cost(8_000_000_000),
         name="finish",
-    )(places, inverse_t, *pieces, *highs, *lows, trailing)
+    )(*[in_vmem(operand) for operand in operands])
 
 
 def round_z(chips):
@@ -442,25 +463,21 @@
         blocks += [first[s], second[s], exchange(second[s]), exchange(first[s])]
     first.append(send(first[-1]))
     early = blocks[: 4 * far - 4]
-    high, low = turn(early, 512)
-    first[far], high = lax.optimization_barrier((first[far], high))
+    mixed, near, high, low = mix(early, trailing, 512)
+    first[far], mixed = lax.optimization_barrier((first[far], mixed))
 
     received = [first[s] if core == 0 else second[s] for s in range(1, far) for core in range(2)] + [first[far]]
-    part = gram_part(own, second[0], received)
+    part = gram_part(near, second[0], received)
     pieces = sent_along(part, False)
     late = blocks[4 * far - 4 :] + [first[far], exchange(first[far])]
     late[0], pieces[0] = lax.optimization_barrier((late[0], pieces[0]))
-    *quarters, late_high, late_low = mix(early, late, trailing, 512)
+    *quarters, late_high, late_low = mix_last(mixed, late, trailing, 512)
     part = sum(pieces, part)
     quarters[1:] = [lax.ppermute(quarter, "row", shifted(0, k + 1)) for k, quarter in enumerate(quarters[1:])]
     part, quarters[0] = lax.optimization_barrier((sum_along(part, True), quarters[0]))
     mixed = sum(quarters[1:], quarters[0])
     mixed = sum_along(mixed, True)
     parts = lax.all_gather(part, "col", axis=0, tiled=True)
-
-    work, upper = factor_first(parts, width, 2)
-    quarters = [mixed] + sent_along(mixed, False)
-    inverse_t, upper, own_factor = factor_second(work, upper, 2)
 
     row, col = lax.axis_index("row"), lax.axis_index("col")
     z, c = lax.div(col, 2), lax.rem(col, 2)
@@ -472,7 +489,12 @@
     chip = lax.rem(z + far, chips)
     places += [2 * chip + c, 2 * chip + 1 - c, lax.rem(row, SIDE)]
     places = jnp.stack(places).astype(jnp.int32)
-    top_rows, projected = finish(places, inverse_t, quarters, [high, late_high], [low, late_low], trailing, 512)
+
+    work, upper = factor_first(parts, width, 2)
+    quarters = [mixed] + sent_along(mixed, False)
+    _, _, own_factor, *arranged = factor_second(places, work, upper, 2)
+    highs, lows = [high, late_high], [low, late_low]
+    top_rows, projected = finish(arranged[:2], arranged[2:], quarters, highs, lows, trailing, 512)
     return (own_factor.T, top_rows, projected)
 
 

time: 122 us -> 115 us (0.943)
  waiting for transfers between devices: 17.6 us -> 13.5 us
  Pallas kernels: 37.8 us -> 34.5 us
    ppermute x7, starting transfers between devices: 13.6 us -> 19.6 us  [send(): return lax.ppermute(value, 'col', ring)]
    ppermute x8, starting transfers between devices: 13.2 us -> 8.63 us  [exchange(): return lax.ppermute(value, 'col', swap)]
    ppermute x7, waiting for transfers between devices: 6.24 us -> 3.28 us  [send(): return lax.ppermute(value, 'col', ring)]
    pallas_call x1, Pallas kernels: 7.95 us -> 6.26 us  [finish(): pl.pallas_call(functools.partial(last_kernel, tile), out_shape=[jax.Shape...]
  transfers between devices with their start and end apart: 30 -> 30, of which waited for: 7 -> 6; matrix products, arithmetic and copies ran while one was open for 1% -> 0% of each run, Pallas kernels for 24% -> 24%
where the time goes in v3:
time: 115 us
  starting transfers between devices  45.8 us (40%)
  Pallas kernels  34.5 us (30%)
  blocking collectives  20 us (17%)
  waiting for transfers between devices  13.5 us (12%)
    all_gather x1, blocking collectives, on_device(): parts = lax.all_gather(part, 'col', axis=0, tiled=True)  20 us
    ppermute x7, starting transfers between devices, send(): return lax.ppermute(value, 'col', ring)  19.6 us
    ppermute x12, starting transfers between devices, sent_along(): lax.ppermute(value, 'row', shifted(k, 0) if along_y else shifted(0, k))  14 us
    ppermute x12, waiting for transfers between devices, sent_along(): lax.ppermute(value, 'row', shifted(k, 0) if along_y else shifted(0, k))  10.2 us
    pallas_call x1, Pallas kernels, factor_first(): pl.pallas_call(functools.partial(first_kernel, steps), out_shape=[jax.Sha...  9.45 us
    pallas_call x1, Pallas kernels, factor_second(): pl.pallas_call(functools.partial(second_kernel, begin), out_shape=[whole,...  9.06 us
    ppermute x8, starting transfers between devices, exchange(): return lax.ppermute(value, 'col', swap)  8.63 us
    pallas_call x1, Pallas kernels, finish(): pl.pallas_call(functools.partial(last_kernel, tile), out_shape=[jax.Shape...  6.26 us
  transfers between devices with their start and end apart: 30, of which 6 were waited for; matrix products, arithmetic and copies ran while one was open for 0% of the time, Pallas kernels for 24%

profile of v3, /device:TPU:1, one launch (start us, length us, event | category | flops | bytes accessed | tf_op | source)
XLA Modules:
  0.0 115.1 jit_solution(13775464580899150427)
XLA Ops:
  0.6 3.3 %collective-permute-start = (f32[32,2048]{1,0:T(8,128)}, f32[32,2048]{1,0:T(8,128)S(1)}, u32[]{:S(2)}, u32[]{:S(2)}) collective-permute-start(f32[32,2048]{1,0:T(8,128)} %bitcast.20), channel_id=1, source_target_pairs={{0,1},{1,0},{2,3},{3,2},{4,5},{5,4},{6,7},{7,6},{8,9},{9,8},{10,11... | collective-permute-start | bytes 786440 | tf_op jit(solution)/shard_map/ppermute | solution.py:456
  4.0 3.8 %collective-permute-start.1 = (f32[32,2048]{1,0:T(8,128)}, f32[32,2048]{1,0:T(8,128)S(1)}, u32[]{:S(2)}, u32[]{:S(2)}) collective-permute-start(f32[32,2048]{1,0:T(8,128)} %bitcast.21), channel_id=1, source_target_pairs={{0,2},{1,15},{2,4},{3,1},{4,6},{5,3},{6,8},{7,5},{8,10},{9,7},{10,... | collective-permute-start | bytes 786440 | tf_op jit(solution)/shard_map/ppermute | solution.py:453
  7.8 1.4 %collective-permute-start.2 = (f32[32,2048]{1,0:T(8,128)S(1)}, f32[32,2048]{1,0:T(8,128)S(1)}, u32[]{:S(2)}, u32[]{:S(2)}) collective-permute-start(f32[32,2048]{1,0:T(8,128)S(1)} %collective-permute-done.refs_0_.other_ref), channel_id=1, source_target_pairs={{0,2},{1,15},{2,4},{3,1},{4,6},{5,3},{6,8},{7,5},{8,10},{9,7},{10,... | collective-permute-start | bytes 786440 | tf_op jit(solution)/shard_map/ppermute | solution.py:453
  9.2 2.3 %collective-permute-done.1.refs_1_.refs_0_ = f32[32,2048]{1,0:T(8,128)S(1)} collective-permute-done((f32[32,2048]{1,0:T(8,128)}, f32[32,2048]{1,0:T(8,128)S(1)}, u32[]{:S(2)}, u32[]{:S(2)}) %collective-permute-start.1) | collective-permute-done | bytes 262176 | tf_op jit(solution)/shard_map/ppermute | solution.py:453
  11.4 3.0 %collective-permute-start.5 = (f32[32,2048]{1,0:T(8,128)S(1)}, f32[32,2048]{1,0:T(8,128)S(1)}, u32[]{:S(2)}, u32[]{:S(2)}) collective-permute-start(f32[32,2048]{1,0:T(8,128)S(1)} %collective-permute-done.1.refs_1_.refs_0_), channel_id=1, source_target_pairs={{0,2},{1,15},{2,4},{3,1},{4,6},{5,3},{6,8},{7,5},{8,10},{9,7},{10,... | collective-permute-start | bytes 786440 | tf_op jit(solution)/shard_map/ppermute | solution.py:453
  14.4 0.0 collective-permute-done.2.refs_2_.refs_1_
  14.4 2.8 %collective-permute-start.6 = (f32[32,2048]{1,0:T(8,128)S(1)}, f32[32,2048]{1,0:T(8,128)S(1)}, u32[]{:S(2)}, u32[]{:S(2)}) collective-permute-start(f32[32,2048]{1,0:T(8,128)S(1)} %collective-permute-done.2.refs_2_.refs_1_), channel_id=1, source_target_pairs={{0,2},{1,15},{2,4},{3,1},{4,6},{5,3},{6,8},{7,5},{8,10},{9,7},{10,... | collective-permute-start | bytes 786440 | tf_op jit(solution)/shard_map/ppermute | solution.py:453
  17.3 0.5 collective-permute-done.5.refs_5_.refs_2_
  17.8 3.1 %collective-permute-start.9 = (f32[32,2048]{1,0:T(8,128)S(1)}, f32[32,2048]{1,0:T(8,128)S(1)}, u32[]{:S(2)}, u32[]{:S(2)}) collective-permute-start(f32[32,2048]{1,0:T(8,128)S(1)} %collective-permute-done.5.refs_5_.refs_2_), channel_id=1, source_target_pairs={{0,2},{1,15},{2,4},{3,1},{4,6},{5,3},{6,8},{7,5},{8,10},{9,7},{10,... | collective-permute-start | bytes 786440 | tf_op jit(solution)/shard_map/ppermute | solution.py:453
  20.9 0.5 collective-permute-start.3
  21.4 0.0 collective-permute-done.6.refs_6_.refs_3_
  21.4 2.3 %collective-permute-start.10 = (f32[32,2048]{1,0:T(8,128)S(1)}, f32[32,2048]{1,0:T(8,128)S(1)}, u32[]{:S(2)}, u32[]{:S(2)}) collective-permute-start(f32[32,2048]{1,0:T(8,128)S(1)} %collective-permute-done.6.refs_6_.refs_3_), channel_id=1, source_target_pairs={{0,2},{1,15},{2,4},{3,1},{4,6},{5,3},{6,8},{7,5},{8,10},{9,7},{10,... | collective-permute-start | bytes 786440 | tf_op jit(solution)/shard_map/ppermute | solution.py:453
  23.7 0.0 collective-permute-done.4.refs_4_
  23.7 0.5 collective-permute-done.9.refs_9_.refs_4_
  24.2 3.1 %collective-permute-start.11 = (f32[32,2048]{1,0:T(8,128)S(1)}, f32[32,2048]{1,0:T(8,128)S(1)}, u32[]{:S(2)}, u32[]{:S(2)}) collective-permute-start(f32[32,2048]{1,0:T(8,128)S(1)} %collective-permute-done.9.refs_9_.refs_4_), channel_id=1, source_target_pairs={{0,2},{1,15},{2,4},{3,1},{4,6},{5,3},{6,8},{7,5},{8,10},{9,7},{10,... | collective-permute-start | bytes 786440 | tf_op jit(solution)/shard_map/ppermute | solution.py:453
  27.3 0.0 collective-permute-done.7.refs_7_
  27.3 5.2 %mixed.1 = (f32[384,512]{1,0:T(8,128)}, f32[32,2048]{1,0:T(8,128)S(1)}, bf16[2048,384]{1,0:T(8,128)(2,1)}, bf16[2048,384]{1,0:T(8,128)(2,1)}) custom-call(f32[32,2048]{1,0:T(8,128)} %bitcast.22, f32[32,2048]{1,0:T(8,128)S(1)} %collective-permute-done.refs_0_.other_ref, f32[32,2048]{1,0:T(8,128)S(1)} %collective-permute-done.1.refs_1_.refs_0_, ...), custom_call_target="tpu_custom_call" | custom-call | flops 3000000000 | bytes 1048576 | tf_op jit(solution)/shard_map/mixed/pallas_call | solution.py:354
  32.5 3.6 %collective-permute-start.12 = (f32[32,2048]{1,0:T(8,128)S(1)}, f32[32,2048]{1,0:T(8,128)S(1)}, u32[]{:S(2)}, u32[]{:S(2)}) collective-permute-start(f32[32,2048]{1,0:T(8,128)S(1)} %collective-permute-done.10.refs_10_.refs_5_), channel_id=1, source_target_pairs={{0,1},{1,0},{2,3},{3,2},{4,5},{5,4},{6,7},{7,6},{8,9},{9,8},{10,11... | collective-permute-start | bytes 786440 | tf_op jit(solution)/shard_map/ppermute | solution.py:456
  36.2 1.4 %gram_part.1 = f32[96,128]{1,0:T(8,128)S(1)} custom-call(s32[1]{0:T(128)} %bitcast.17.core_ref, f32[32,2048]{1,0:T(8,128)S(1)} %get-tuple-element.28.own_ref, f32[32,2048]{1,0:T(8,128)S(1)} %collective-permute-done.refs_0_.other_ref, f32[32,2048]{1,0:T(8,128)S(1)} %collective-permute-done.1.refs_1_.refs_0_, ...), custom_call_target="tpu_custom_call" | custom-call | flops 2000000000 | bytes 1048576 | tf_op jit(solution)/shard_map/gram_part/pallas_call | solution.py:267
  37.5 1.3 %collective-permute-start.13 = (f32[96,128]{1,0:T(8,128)S(1)}, f32[96,128]{1,0:T(8,128)S(1)}, u32[]{:S(2)}, u32[]{:S(2)}) collective-permute-start(f32[96,128]{1,0:T(8,128)S(1)} %gram_part.1), channel_id=1, source_target_pairs={{0,16},{16,32},{32,48},{48,0},{64,80},{80,96},{96,112},{112,64},{1... | collective-permute-start | bytes 147464 | tf_op jit(solution)/shard_map/ppermute | solution.py:229
  38.8 1.5 %collective-permute-start.15 = (f32[96,128]{1,0:T(8,128)S(1)}, f32[96,128]{1,0:T(8,128)S(1)}, u32[]{:S(2)}, u32[]{:S(2)}) collective-permute-start(f32[96,128]{1,0:T(8,128)S(1)} %gram_part.1), channel_id=1, source_target_pairs={{0,48},{16,0},{32,16},{48,32},{64,112},{80,64},{96,80},{112,96},{1... | collective-permute-start | bytes 147464 | tf_op jit(solution)/shard_map/ppermute | solution.py:229
  40.3 1.5 %collective-permute-start.14 = (f32[96,128]{1,0:T(8,128)S(1)}, f32[96,128]{1,0:T(8,128)S(1)}, u32[]{:S(2)}, u32[]{:S(2)}) collective-permute-start(f32[96,128]{1,0:T(8,128)S(1)} %gram_part.1), channel_id=1, source_target_pairs={{0,32},{16,48},{32,0},{48,16},{64,96},{80,112},{96,64},{112,80},{1... | collective-permute-start | bytes 147464 | tf_op jit(solution)/shard_map/ppermute | solution.py:229
  41.8 0.9 collective-permute-start.19
  42.7 0.0 collective-permute-done.13
  42.7 0.3 collective-permute-start.20
  43.0 0.1 stack.71.place_ref
  43.1 1.6 %collective-permute-done.14 = f32[96,128]{1,0:T(8,128)S(1)} collective-permute-done((f32[96,128]{1,0:T(8,128)S(1)}, f32[96,128]{1,0:T(8,128)S(1)}, u32[]{:S(2)}, u32[]{:S(2)}) %collective-permute-start.14) | collective-permute-done | bytes 49184 | tf_op jit(solution)/shard_map/ppermute | solution.py:229
  44.8 2.8 %collective-permute-start.18 = (f32[96,128]{1,0:T(8,128)S(1)}, f32[96,128]{1,0:T(8,128)S(1)}, u32[]{:S(2)}, u32[]{:S(2)}) collective-permute-start(f32[96,128]{1,0:T(8,128)S(1)} %add_add_fusion.3), channel_id=1, source_target_pairs={{0,192},{16,208},{32,224},{48,240},{64,0},{80,16},{96,32},{112,48}... | collective-permute-start | bytes 147464 | tf_op jit(solution)/shard_map/ppermute | solution.py:229
  47.6 0.4 collective-permute-start.17
  47.9 0.7 collective-permute-start.16
  48.6 3.1 %mixed_last.1 = (f32[128,512]{1,0:T(8,128)S(1)}, f32[128,512]{1,0:T(8,128)S(1)}, f32[128,512]{1,0:T(8,128)S(1)}, f32[128,512]{1,0:T(8,128)S(1)}, bf16[2048,128]{1,0:T(8,128)(2,1)}, /*index=5*/bf16[2048,128]{1,0:T(8,128)(2,1)}) custom-call(s32[1]{0:T(128)} %bitcast.16.place_ref, f32[384,512]{1,0:T(8,128)} %get-tuple-element.32.done_ref, ...), custom_call_target="tpu_custom_call" | custom-call | flops 3000000000 | bytes 1048576 | tf_op jit(solution)/shard_map/mixed_last/pallas_call | solution.py:375
  51.8 0.2 collective-permute-start.21
  52.0 2.3 %collective-permute-start.22 = (f32[128,512]{1,0:T(8,128)S(1)}, f32[128,512]{1,0:T(8,128)S(1)}, u32[]{:S(2)}, u32[]{:S(2)}) collective-permute-start(f32[128,512]{1,0:T(8,128)S(1)} %get-tuple-element.45), channel_id=1, source_target_pairs={{0,32},{16,48},{32,0},{48,16},{64,96},{80,112},{96,64},{112,80},{1... | collective-permute-start | bytes 786440 | tf_op jit(solution)/shard_map/ppermute | solution.py:476
  54.3 1.1 collective-permute-start.23
  55.5 20.0 %all_gather.3.part_ref = f32[1536,128]{1,0:T(8,128)S(1)} all-gather(f32[96,128]{1,0:T(8,128)S(1)} %add_add_fusion.2), channel_id=1, replica_groups=mesh['row'=16,'col'=16] {'col'}, dimensions={0}, use_global_device_ids=true | all-gather | bytes 835584 | tf_op jit(solution)/shard_map/all_gather | solution.py:480
  75.4 0.1 add_add_fusion.1
  75.5 2.1 %collective-permute-start.26 = (f32[128,512]{1,0:T(8,128)S(1)}, f32[128,512]{1,0:T(8,128)S(1)}, u32[]{:S(2)}, u32[]{:S(2)}) collective-permute-start(f32[128,512]{1,0:T(8,128)S(1)} %add_add_fusion.1), channel_id=1, source_target_pairs={{0,192},{16,208},{32,224},{48,240},{64,0},{80,16},{96,32},{112,48}... | collective-permute-start | bytes 786440 | tf_op jit(solution)/shard_map/ppermute | solution.py:229
  77.6 1.4 %collective-permute-start.25 = (f32[128,512]{1,0:T(8,128)S(1)}, f32[128,512]{1,0:T(8,128)S(1)}, u32[]{:S(2)}, u32[]{:S(2)}) collective-permute-start(f32[128,512]{1,0:T(8,128)S(1)} %add_add_fusion.1), channel_id=1, source_target_pairs={{0,128},{16,144},{32,160},{48,176},{64,192},{80,208},{96,224},{112... | collective-permute-start | bytes 786440 | tf_op jit(solution)/shard_map/ppermute | solution.py:229
  79.0 0.0 collective-permute-start.24
  79.0 9.5 %factor_first.1 = (f32[512,512]{1,0:T(8,128)S(1)}, f32[512,512]{1,0:T(8,128)S(1)}) custom-call(f32[1536,128]{1,0:T(8,128)S(1)} %all_gather.3.part_ref), custom_call_target="tpu_custom_call" | custom-call | flops 10000000000 | bytes 1048576 | tf_op jit(solution)/shard_map/factor_first/pallas_call | solution.py:196
  88.5 4.5 %collective-permute-done.24 = f32[128,512]{1,0:T(8,128)S(1)} collective-permute-done((f32[128,512]{1,0:T(8,128)S(1)}, f32[128,512]{1,0:T(8,128)S(1)}, u32[]{:S(2)}, u32[]{:S(2)}) %collective-permute-start.24) | collective-permute-done | bytes 262176 | tf_op jit(solution)/shard_map/ppermute | solution.py:229
  93.0 0.1 add_add_fusion.refs_4_
  93.1 0.1 collective-permute-start.29
  93.2 2.1 %collective-permute-start.28 = (f32[128,512]{1,0:T(8,128)S(1)}, f32[128,512]{1,0:T(8,128)S(1)}, u32[]{:S(2)}, u32[]{:S(2)}) collective-permute-start(f32[128,512]{1,0:T(8,128)S(1)} %add_add_fusion.refs_4_), channel_id=1, source_target_pairs={{0,32},{16,48},{32,0},{48,16},{64,96},{80,112},{96,64},{112,80},{1... | collective-permute-start | bytes 786440 | tf_op jit(solution)/shard_map/ppermute | solution.py:229
  95.2 0.2 collective-permute-start.27
  95.5 9.1 %factor_second.1 = (f32[512,512]{1,0:T(8,128)S(1)}, f32[512,512]{1,0:T(8,128)S(1)}, f32[32,512]{1,0:T(8,128)}, bf16[512,512]{1,0:T(8,128)(2,1)S(1)}, bf16[512,51...) custom-call(s32[17]{0:T(128)S(1)} %stack.71.place_ref, ...), custom_call_target="tpu_custom_call", output_to_operand_aliasing={{0}: (1, {}), {1}: (2, {})} | custom-call | flops 8000000000 | bytes 1048576 | tf_op jit(solution)/shard_map/factor_second/pallas_call | solution.py:210
  104.5 4.1 %collective-permute-done.27.refs_5_ = f32[128,512]{1,0:T(8,128)S(1)} collective-permute-done((f32[128,512]{1,0:T(8,128)S(1)}, f32[128,512]{1,0:T(8,128)S(1)}, u32[]{:S(2)}, u32[]{:S(2)}) %collective-permute-start.27) | collective-permute-done | bytes 262176 | tf_op jit(solution)/shard_map/ppermute | solution.py:229
  108.6 6.3 %finish.1 = (f32[512,512]{1,0:T(8,128)}, f32[2048,512]{1,0:T(8,128)}) custom-call(bf16[512,512]{1,0:T(8,128)(2,1)S(1)} %get-tuple-element.39.refs_0_, bf16[512,512]{1,0:T(8,128)(2,1)S(1)} %get-tuple-element.40.refs_1_, bf16[512,512]{1,0:T(8,128)(2,1)S(1)} %get-tuple-element.41.refs_2_, bf16[512,512]{1,0:T(8,128)(2,1)S(1)} %get-tuple-element.42.refs_3_, ...), custom_call_target="tpu_custom_call" | custom-call | flops 8000000000 | bytes 1048576 | tf_op jit(solution)/shard_map/finish/pallas_call | solution.py:419
  (34 shorter events, 0.1 us)
Async XLA Ops:
  0.6 7.2 %collective-permute-start = (f32[32,2048]{1,0:T(8,128)}, f32[32,2048]{1,0:T(8,128)S(1)}, u32[]{:S(2)}, u32[]{:S(2)}) collective-permute-start(f32[32,2048]{1,0:T(8,128)} %bitcast.20), channel_id=1, source_target_pairs={{0,1},{1,0},{2,3},{3,2},{4,5},{5,4},{6,7},{7,6},{8,9},{9,8},{10,11... | collective-permute-start | bytes 786440 | tf_op jit(solution)/shard_map/ppermute | solution.py:456
  4.0 7.5 %collective-permute-start.1 = (f32[32,2048]{1,0:T(8,128)}, f32[32,2048]{1,0:T(8,128)S(1)}, u32[]{:S(2)}, u32[]{:S(2)}) collective-permute-start(f32[32,2048]{1,0:T(8,128)} %bitcast.21), channel_id=1, source_target_pairs={{0,2},{1,15},{2,4},{3,1},{4,6},{5,3},{6,8},{7,5},{8,10},{9,7},{10,... | collective-permute-start | bytes 786440 | tf_op jit(solution)/shard_map/ppermute | solution.py:453
  7.8 6.6 %collective-permute-start.2 = (f32[32,2048]{1,0:T(8,128)S(1)}, f32[32,2048]{1,0:T(8,128)S(1)}, u32[]{:S(2)}, u32[]{:S(2)}) collective-permute-start(f32[32,2048]{1,0:T(8,128)S(1)} %collective-permute-done.refs_0_.other_ref), channel_id=1, source_target_pairs={{0,2},{1,15},{2,4},{3,1},{4,6},{5,3},{6,8},{7,5},{8,10},{9,7},{10,... | collective-permute-start | bytes 786440 | tf_op jit(solution)/shard_map/ppermute | solution.py:453
  11.4 6.3 %collective-permute-start.5 = (f32[32,2048]{1,0:T(8,128)S(1)}, f32[32,2048]{1,0:T(8,128)S(1)}, u32[]{:S(2)}, u32[]{:S(2)}) collective-permute-start(f32[32,2048]{1,0:T(8,128)S(1)} %collective-permute-done.1.refs_1_.refs_0_), channel_id=1, source_target_pairs={{0,2},{1,15},{2,4},{3,1},{4,6},{5,3},{6,8},{7,5},{8,10},{9,7},{10,... | collective-permute-start | bytes 786440 | tf_op jit(solution)/shard_map/ppermute | solution.py:453
  14.4 6.9 %collective-permute-start.6 = (f32[32,2048]{1,0:T(8,128)S(1)}, f32[32,2048]{1,0:T(8,128)S(1)}, u32[]{:S(2)}, u32[]{:S(2)}) collective-permute-start(f32[32,2048]{1,0:T(8,128)S(1)} %collective-permute-done.2.refs_2_.refs_1_), channel_id=1, source_target_pairs={{0,2},{1,15},{2,4},{3,1},{4,6},{5,3},{6,8},{7,5},{8,10},{9,7},{10,... | collective-permute-start | bytes 786440 | tf_op jit(solution)/shard_map/ppermute | solution.py:453
  17.3 6.4 %collective-permute-start.4 = (f32[32,2048]{1,0:T(8,128)S(1)}, f32[32,2048]{1,0:T(8,128)S(1)}, u32[]{:S(2)}, u32[]{:S(2)}) collective-permute-start(f32[32,2048]{1,0:T(8,128)S(1)} %collective-permute-done.1.refs_1_.refs_0_), channel_id=1, source_target_pairs={{0,1},{1,0},{2,3},{3,2},{4,5},{5,4},{6,7},{7,6},{8,9},{9,8},{10,11... | collective-permute-start | bytes 786440 | tf_op jit(solution)/shard_map/ppermute | solution.py:456
  17.8 6.4 %collective-permute-start.9 = (f32[32,2048]{1,0:T(8,128)S(1)}, f32[32,2048]{1,0:T(8,128)S(1)}, u32[]{:S(2)}, u32[]{:S(2)}) collective-permute-start(f32[32,2048]{1,0:T(8,128)S(1)} %collective-permute-done.5.refs_5_.refs_2_), channel_id=1, source_target_pairs={{0,2},{1,15},{2,4},{3,1},{4,6},{5,3},{6,8},{7,5},{8,10},{9,7},{10,... | collective-permute-start | bytes 786440 | tf_op jit(solution)/shard_map/ppermute | solution.py:453
  20.9 6.4 %collective-permute-start.8 = (f32[32,2048]{1,0:T(8,128)S(1)}, f32[32,2048]{1,0:T(8,128)S(1)}, u32[]{:S(2)}, u32[]{:S(2)}) collective-permute-start(f32[32,2048]{1,0:T(8,128)S(1)} %collective-permute-done.5.refs_5_.refs_2_), channel_id=1, source_target_pairs={{0,1},{1,0},{2,3},{3,2},{4,5},{5,4},{6,7},{7,6},{8,9},{9,8},{10,11... | collective-permute-start | bytes 786440 | tf_op jit(solution)/shard_map/ppermute | solution.py:456
  20.9 6.4 %collective-permute-start.3 = (f32[32,2048]{1,0:T(8,128)S(1)}, f32[32,2048]{1,0:T(8,128)S(1)}, u32[]{:S(2)}, u32[]{:S(2)}) collective-permute-start(f32[32,2048]{1,0:T(8,128)S(1)} %collective-permute-done.2.refs_2_.refs_1_), channel_id=1, source_target_pairs={{0,1},{1,0},{2,3},{3,2},{4,5},{5,4},{6,7},{7,6},{8,9},{9,8},{10,11... | collective-permute-start | bytes 786440 | tf_op jit(solution)/shard_map/ppermute | solution.py:456
  21.4 5.9 %collective-permute-start.10 = (f32[32,2048]{1,0:T(8,128)S(1)}, f32[32,2048]{1,0:T(8,128)S(1)}, u32[]{:S(2)}, u32[]{:S(2)}) collective-permute-start(f32[32,2048]{1,0:T(8,128)S(1)} %collective-permute-done.6.refs_6_.refs_3_), channel_id=1, source_target_pairs={{0,2},{1,15},{2,4},{3,1},{4,6},{5,3},{6,8},{7,5},{8,10},{9,7},{10,... | collective-permute-start | bytes 786440 | tf_op jit(solution)/shard_map/ppermute | solution.py:453
  23.7 3.6 %collective-permute-start.7 = (f32[32,2048]{1,0:T(8,128)S(1)}, f32[32,2048]{1,0:T(8,128)S(1)}, u32[]{:S(2)}, u32[]{:S(2)}) collective-permute-start(f32[32,2048]{1,0:T(8,128)S(1)} %collective-permute-done.6.refs_6_.refs_3_), channel_id=1, source_target_pairs={{0,1},{1,0},{2,3},{3,2},{4,5},{5,4},{6,7},{7,6},{8,9},{9,8},{10,11... | collective-permute-start | bytes 786440 | tf_op jit(solution)/shard_map/ppermute | solution.py:456
  24.2 8.3 %collective-permute-start.11 = (f32[32,2048]{1,0:T(8,128)S(1)}, f32[32,2048]{1,0:T(8,128)S(1)}, u32[]{:S(2)}, u32[]{:S(2)}) collective-permute-start(f32[32,2048]{1,0:T(8,128)S(1)} %collective-permute-done.9.refs_9_.refs_4_), channel_id=1, source_target_pairs={{0,2},{1,15},{2,4},{3,1},{4,6},{5,3},{6,8},{7,5},{8,10},{9,7},{10,... | collective-permute-start | bytes 786440 | tf_op jit(solution)/shard_map/ppermute | solution.py:453
  32.5 10.6 %collective-permute-start.12 = (f32[32,2048]{1,0:T(8,128)S(1)}, f32[32,2048]{1,0:T(8,128)S(1)}, u32[]{:S(2)}, u32[]{:S(2)}) collective-permute-start(f32[32,2048]{1,0:T(8,128)S(1)} %collective-permute-done.10.refs_10_.refs_5_), channel_id=1, source_target_pairs={{0,1},{1,0},{2,3},{3,2},{4,5},{5,4},{6,7},{7,6},{8,9},{9,8},{10,11... | collective-permute-start | bytes 786440 | tf_op jit(solution)/shard_map/ppermute | solution.py:456
  37.5 5.2 %collective-permute-start.13 = (f32[96,128]{1,0:T(8,128)S(1)}, f32[96,128]{1,0:T(8,128)S(1)}, u32[]{:S(2)}, u32[]{:S(2)}) collective-permute-start(f32[96,128]{1,0:T(8,128)S(1)} %gram_part.1), channel_id=1, source_target_pairs={{0,16},{16,32},{32,48},{48,0},{64,80},{80,96},{96,112},{112,64},{1... | collective-permute-start | bytes 147464 | tf_op jit(solution)/shard_map/ppermute | solution.py:229
  38.8 4.3 %collective-permute-start.15 = (f32[96,128]{1,0:T(8,128)S(1)}, f32[96,128]{1,0:T(8,128)S(1)}, u32[]{:S(2)}, u32[]{:S(2)}) collective-permute-start(f32[96,128]{1,0:T(8,128)S(1)} %gram_part.1), channel_id=1, source_target_pairs={{0,48},{16,0},{32,16},{48,32},{64,112},{80,64},{96,80},{112,96},{1... | collective-permute-start | bytes 147464 | tf_op jit(solution)/shard_map/ppermute | solution.py:229
  40.3 4.4 %collective-permute-start.14 = (f32[96,128]{1,0:T(8,128)S(1)}, f32[96,128]{1,0:T(8,128)S(1)}, u32[]{:S(2)}, u32[]{:S(2)}) collective-permute-start(f32[96,128]{1,0:T(8,128)S(1)} %gram_part.1), channel_id=1, source_target_pairs={{0,32},{16,48},{32,0},{48,16},{64,96},{80,112},{96,64},{112,80},{1... | collective-permute-start | bytes 147464 | tf_op jit(solution)/shard_map/ppermute | solution.py:229
  41.8 6.8 %collective-permute-start.19 = (f32[32,2048]{1,0:T(8,128)S(1)}, f32[32,2048]{1,0:T(8,128)S(1)}, u32[]{:S(2)}, u32[]{:S(2)}) collective-permute-start(f32[32,2048]{1,0:T(8,128)S(1)} %collective-permute-done.9.refs_9_.refs_4_), channel_id=1, source_target_pairs={{0,1},{1,0},{2,3},{3,2},{4,5},{5,4},{6,7},{7,6},{8,9},{9,8},{10,11... | collective-permute-start | bytes 786440 | tf_op jit(solution)/shard_map/ppermute | solution.py:456
  42.7 5.9 %collective-permute-start.20 = (f32[32,2048]{1,0:T(8,128)S(1)}, f32[32,2048]{1,0:T(8,128)S(1)}, u32[]{:S(2)}, u32[]{:S(2)}) collective-permute-start(f32[32,2048]{1,0:T(8,128)S(1)} %collective-permute-done.11.refs_6_.refs_2_), channel_id=1, source_target_pairs={{0,1},{1,0},{2,3},{3,2},{4,5},{5,4},{6,7},{7,6},{8,9},{9,8},{10,11... | collective-permute-start | bytes 786440 | tf_op jit(solution)/shard_map/ppermute | solution.py:456
  44.8 9.5 %collective-permute-start.18 = (f32[96,128]{1,0:T(8,128)S(1)}, f32[96,128]{1,0:T(8,128)S(1)}, u32[]{:S(2)}, u32[]{:S(2)}) collective-permute-start(f32[96,128]{1,0:T(8,128)S(1)} %add_add_fusion.3), channel_id=1, source_target_pairs={{0,192},{16,208},{32,224},{48,240},{64,0},{80,16},{96,32},{112,48}... | collective-permute-start | bytes 147464 | tf_op jit(solution)/shard_map/ppermute | solution.py:229
  47.6 7.9 %collective-permute-start.17 = (f32[96,128]{1,0:T(8,128)S(1)}, f32[96,128]{1,0:T(8,128)S(1)}, u32[]{:S(2)}, u32[]{:S(2)}) collective-permute-start(f32[96,128]{1,0:T(8,128)S(1)} %add_add_fusion.3), channel_id=1, source_target_pairs={{0,128},{16,144},{32,160},{48,176},{64,192},{80,208},{96,224},{112... | collective-permute-start | bytes 147464 | tf_op jit(solution)/shard_map/ppermute | solution.py:229
  47.9 7.5 %collective-permute-start.16 = (f32[96,128]{1,0:T(8,128)S(1)}, f32[96,128]{1,0:T(8,128)S(1)}, u32[]{:S(2)}, u32[]{:S(2)}) collective-permute-start(f32[96,128]{1,0:T(8,128)S(1)} %add_add_fusion.3), channel_id=1, source_target_pairs={{0,64},{16,80},{32,96},{48,112},{64,128},{80,144},{96,160},{112,17... | collective-permute-start | bytes 147464 | tf_op jit(solution)/shard_map/ppermute | solution.py:229
  51.8 23.7 %collective-permute-start.21 = (f32[128,512]{1,0:T(8,128)S(1)}, f32[128,512]{1,0:T(8,128)S(1)}, u32[]{:S(2)}, u32[]{:S(2)}) collective-permute-start(f32[128,512]{1,0:T(8,128)S(1)} %get-tuple-element.44), channel_id=1, source_target_pairs={{0,16},{16,32},{32,48},{48,0},{64,80},{80,96},{96,112},{112,64},{1... | collective-permute-start | bytes 786440 | tf_op jit(solution)/shard_map/ppermute | solution.py:476
  52.0 23.5 %collective-permute-start.22 = (f32[128,512]{1,0:T(8,128)S(1)}, f32[128,512]{1,0:T(8,128)S(1)}, u32[]{:S(2)}, u32[]{:S(2)}) collective-permute-start(f32[128,512]{1,0:T(8,128)S(1)} %get-tuple-element.45), channel_id=1, source_target_pairs={{0,32},{16,48},{32,0},{48,16},{64,96},{80,112},{96,64},{112,80},{1... | collective-permute-start | bytes 786440 | tf_op jit(solution)/shard_map/ppermute | solution.py:476
  54.3 21.2 %collective-permute-start.23 = (f32[128,512]{1,0:T(8,128)S(1)}, f32[128,512]{1,0:T(8,128)S(1)}, u32[]{:S(2)}, u32[]{:S(2)}) collective-permute-start(f32[128,512]{1,0:T(8,128)S(1)} %get-tuple-element.46), channel_id=1, source_target_pairs={{0,48},{16,0},{32,16},{48,32},{64,112},{80,64},{96,80},{112,96},{1... | collective-permute-start | bytes 786440 | tf_op jit(solution)/shard_map/ppermute | solution.py:476
  75.5 12.9 %collective-permute-start.26 = (f32[128,512]{1,0:T(8,128)S(1)}, f32[128,512]{1,0:T(8,128)S(1)}, u32[]{:S(2)}, u32[]{:S(2)}) collective-permute-start(f32[128,512]{1,0:T(8,128)S(1)} %add_add_fusion.1), channel_id=1, source_target_pairs={{0,192},{16,208},{32,224},{48,240},{64,0},{80,16},{96,32},{112,48}... | collective-permute-start | bytes 786440 | tf_op jit(solution)/shard_map/ppermute | solution.py:229
  77.6 10.9 %collective-permute-start.25 = (f32[128,512]{1,0:T(8,128)S(1)}, f32[128,512]{1,0:T(8,128)S(1)}, u32[]{:S(2)}, u32[]{:S(2)}) collective-permute-start(f32[128,512]{1,0:T(8,128)S(1)} %add_add_fusion.1), channel_id=1, source_target_pairs={{0,128},{16,144},{32,160},{48,176},{64,192},{80,208},{96,224},{112... | collective-permute-start | bytes 786440 | tf_op jit(solution)/shard_map/ppermute | solution.py:229
  79.0 13.9 %collective-permute-start.24 = (f32[128,512]{1,0:T(8,128)S(1)}, f32[128,512]{1,0:T(8,128)S(1)}, u32[]{:S(2)}, u32[]{:S(2)}) collective-permute-start(f32[128,512]{1,0:T(8,128)S(1)} %add_add_fusion.1), channel_id=1, source_target_pairs={{0,64},{16,80},{32,96},{48,112},{64,128},{80,144},{96,160},{112,17... | collective-permute-start | bytes 786440 | tf_op jit(solution)/shard_map/ppermute | solution.py:229
  93.1 11.5 %collective-permute-start.29 = (f32[128,512]{1,0:T(8,128)S(1)}, f32[128,512]{1,0:T(8,128)S(1)}, u32[]{:S(2)}, u32[]{:S(2)}) collective-permute-start(f32[128,512]{1,0:T(8,128)S(1)} %add_add_fusion.refs_4_), channel_id=1, source_target_pairs={{0,48},{16,0},{32,16},{48,32},{64,112},{80,64},{96,80},{112,96},{1... | collective-permute-start | bytes 786440 | tf_op jit(solution)/shard_map/ppermute | solution.py:229
  93.2 11.4 %collective-permute-start.28 = (f32[128,512]{1,0:T(8,128)S(1)}, f32[128,512]{1,0:T(8,128)S(1)}, u32[]{:S(2)}, u32[]{:S(2)}) collective-permute-start(f32[128,512]{1,0:T(8,128)S(1)} %add_add_fusion.refs_4_), channel_id=1, source_target_pairs={{0,32},{16,48},{32,0},{48,16},{64,96},{80,112},{96,64},{112,80},{1... | collective-permute-start | bytes 786440 | tf_op jit(solution)/shard_map/ppermute | solution.py:229
  95.2 13.3 %collective-permute-start.27 = (f32[128,512]{1,0:T(8,128)S(1)}, f32[128,512]{1,0:T(8,128)S(1)}, u32[]{:S(2)}, u32[]{:S(2)}) collective-permute-start(f32[128,512]{1,0:T(8,128)S(1)} %add_add_fusion.refs_4_), channel_id=1, source_target_pairs={{0,16},{16,32},{32,48},{48,0},{64,80},{80,96},{96,112},{112,64},{1... | collective-permute-start | bytes 786440 | tf_op jit(solution)/shard_map/ppermute | solution.py:229
  95.4 13.2 %copy-start = (f32[2048,512]{1,0:T(8,128)S(1)}, f32[2048,512]{1,0:T(8,128)}, u32[]{:S(2)}) copy-start(f32[2048,512]{1,0:T(8,128)} %refs_12_.1) | copy-start | bytes 12582916
  95.4 13.2 %copy-start.1 = (bf16[2048,384]{1,0:T(8,128)(2,1)S(1)}, bf16[2048,384]{1,0:T(8,128)(2,1)}, u32[]{:S(2)}) copy-start(bf16[2048,384]{1,0:T(8,128)(2,1)} %get-tuple-element.47.refs_8_) | copy-start | bytes 4718596
  95.4 13.2 %copy-start.2 = (bf16[2048,384]{1,0:T(8,128)(2,1)S(1)}, bf16[2048,384]{1,0:T(8,128)(2,1)}, u32[]{:S(2)}) copy-start(bf16[2048,384]{1,0:T(8,128)(2,1)} %get-tuple-element.49.refs_10_) | copy-start | bytes 4718596
  95.4 13.2 %copy-start.3 = (bf16[2048,128]{1,0:T(8,128)(2,1)S(1)}, bf16[2048,128]{1,0:T(8,128)(2,1)}, u32[]{:S(2)}) copy-start(bf16[2048,128]{1,0:T(8,128)(2,1)} %get-tuple-element.48.refs_9_) | copy-start | bytes 1572868
  95.5 13.2 %copy-start.4 = (bf16[2048,128]{1,0:T(8,128)(2,1)S(1)}, bf16[2048,128]{1,0:T(8,128)(2,1)}, u32[]{:S(2)}) copy-start(bf16[2048,128]{1,0:T(8,128)(2,1)} %get-tuple-element.50.refs_11_) | copy-start | bytes 1572868

commit v4 on v3

--- a/solution.py
+++ b/solution.py
@@ -470,8 +470,9 @@
     part = gram_part(near, second[0], received)
     pieces = sent_along(part, False)
     late = blocks[4 * far - 4 :] + [first[far], exchange(first[far])]
-    late[0], pieces[0] = lax.optimization_barrier((late[0], pieces[0]))
+    late[0], part = lax.optimization_barrier((late[0], part))
     *quarters, late_high, late_low = mix_last(mixed, late, trailing, 512)
+    *pieces, quarters[0] = lax.optimization_barrier((*pieces, quarters[0]))
     part = sum(pieces, part)
     quarters[1:] = [lax.ppermute(quarter, "row", shifted(0, k + 1)) for k, quarter in enumerate(quarters[1:])]
     part, quarters[0] = lax.optimization_barrier((sum_along(part, True), quarters[0]))

time: 115 us -> 112 us (0.974)
  waiting for transfers between devices: 13.5 us -> 12 us
    ppermute x7, starting transfers between devices: 19.6 us -> 16.9 us  [send(): return lax.ppermute(value, 'col', ring)]
    ppermute x8, starting transfers between devices: 8.63 us -> 10.6 us  [exchange(): return lax.ppermute(value, 'col', swap)]
  transfers between devices with their start and end apart: 30 -> 30, of which waited for: 6 -> 7; matrix products, arithmetic and copies ran while one was open for 0% -> 0% of each run, Pallas kernels for 24% -> 25%
where the time goes in v4:
time: 112 us
  starting transfers between devices  44.7 us (40%)
  Pallas kernels  34.3 us (31%)
  blocking collectives  19.9 us (18%)
  waiting for transfers between devices  12 us (11%)
    all_gather x1, blocking collectives, on_device(): parts = lax.all_gather(part, 'col', axis=0, tiled=True)  19.9 us
    ppermute x7, starting transfers between devices, send(): return lax.ppermute(value, 'col', ring)  16.9 us
    ppermute x12, starting transfers between devices, sent_along(): lax.ppermute(value, 'row', shifted(k, 0) if along_y else shifted(0, k))  13.5 us
    ppermute x8, starting transfers between devices, exchange(): return lax.ppermute(value, 'col', swap)  10.6 us
    pallas_call x1, Pallas kernels, factor_first(): pl.pallas_call(functools.partial(first_kernel, steps), out_shape=[jax.Sha...  9.45 us
    ppermute x12, waiting for transfers between devices, sent_along(): lax.ppermute(value, 'row', shifted(k, 0) if along_y else shifted(0, k))  9.22 us
    pallas_call x1, Pallas kernels, factor_second(): pl.pallas_call(functools.partial(second_kernel, begin), out_shape=[whole,...  9.06 us
    pallas_call x1, Pallas kernels, finish(): pl.pallas_call(functools.partial(last_kernel, tile), out_shape=[jax.Shape...  6.26 us
  transfers between devices with their start and end apart: 30, of which 7 were waited for; matrix products, arithmetic and copies ran while one was open for 0% of the time, Pallas kernels for 25%

profile of v4, /device:TPU:1, one launch (start us, length us, event | category | flops | bytes accessed | tf_op | source)
XLA Modules:
  0.0 112.2 jit_solution(8160045516999186862)
XLA Ops:
  0.6 3.3 %collective-permute-start = (f32[32,2048]{1,0:T(8,128)}, f32[32,2048]{1,0:T(8,128)S(1)}, u32[]{:S(2)}, u32[]{:S(2)}) collective-permute-start(f32[32,2048]{1,0:T(8,128)} %bitcast.20), channel_id=1, source_target_pairs={{0,1},{1,0},{2,3},{3,2},{4,5},{5,4},{6,7},{7,6},{8,9},{9,8},{10,11... | collective-permute-start | bytes 786440 | tf_op jit(solution)/shard_map/ppermute | solution.py:456
  4.0 3.8 %collective-permute-start.5 = (f32[32,2048]{1,0:T(8,128)}, f32[32,2048]{1,0:T(8,128)S(1)}, u32[]{:S(2)}, u32[]{:S(2)}) collective-permute-start(f32[32,2048]{1,0:T(8,128)} %bitcast.21), channel_id=1, source_target_pairs={{0,2},{1,15},{2,4},{3,1},{4,6},{5,3},{6,8},{7,5},{8,10},{9,7},{10,... | collective-permute-start | bytes 786440 | tf_op jit(solution)/shard_map/ppermute | solution.py:453
  7.8 1.4 %collective-permute-start.1 = (f32[32,2048]{1,0:T(8,128)S(1)}, f32[32,2048]{1,0:T(8,128)S(1)}, u32[]{:S(2)}, u32[]{:S(2)}) collective-permute-start(f32[32,2048]{1,0:T(8,128)S(1)} %collective-permute-done.refs_0_.other_ref), channel_id=1, source_target_pairs={{0,2},{1,15},{2,4},{3,1},{4,6},{5,3},{6,8},{7,5},{8,10},{9,7},{10,... | collective-permute-start | bytes 786440 | tf_op jit(solution)/shard_map/ppermute | solution.py:453
  9.2 2.3 %collective-permute-done.5.refs_1_.refs_0_ = f32[32,2048]{1,0:T(8,128)S(1)} collective-permute-done((f32[32,2048]{1,0:T(8,128)}, f32[32,2048]{1,0:T(8,128)S(1)}, u32[]{:S(2)}, u32[]{:S(2)}) %collective-permute-start.5) | collective-permute-done | bytes 262176 | tf_op jit(solution)/shard_map/ppermute | solution.py:453
  11.4 3.0 %collective-permute-start.8 = (f32[32,2048]{1,0:T(8,128)S(1)}, f32[32,2048]{1,0:T(8,128)S(1)}, u32[]{:S(2)}, u32[]{:S(2)}) collective-permute-start(f32[32,2048]{1,0:T(8,128)S(1)} %collective-permute-done.5.refs_1_.refs_0_), channel_id=1, source_target_pairs={{0,2},{1,15},{2,4},{3,1},{4,6},{5,3},{6,8},{7,5},{8,10},{9,7},{10,... | collective-permute-start | bytes 786440 | tf_op jit(solution)/shard_map/ppermute | solution.py:453
  14.4 0.0 collective-permute-done.1.refs_2_.refs_1_
  14.4 2.8 %collective-permute-start.2 = (f32[32,2048]{1,0:T(8,128)S(1)}, f32[32,2048]{1,0:T(8,128)S(1)}, u32[]{:S(2)}, u32[]{:S(2)}) collective-permute-start(f32[32,2048]{1,0:T(8,128)S(1)} %collective-permute-done.1.refs_2_.refs_1_), channel_id=1, source_target_pairs={{0,2},{1,15},{2,4},{3,1},{4,6},{5,3},{6,8},{7,5},{8,10},{9,7},{10,... | collective-permute-start | bytes 786440 | tf_op jit(solution)/shard_map/ppermute | solution.py:453
  17.3 0.5 collective-permute-done.8.refs_5_.refs_2_
  17.8 3.1 %collective-permute-start.11 = (f32[32,2048]{1,0:T(8,128)S(1)}, f32[32,2048]{1,0:T(8,128)S(1)}, u32[]{:S(2)}, u32[]{:S(2)}) collective-permute-start(f32[32,2048]{1,0:T(8,128)S(1)} %collective-permute-done.8.refs_5_.refs_2_), channel_id=1, source_target_pairs={{0,2},{1,15},{2,4},{3,1},{4,6},{5,3},{6,8},{7,5},{8,10},{9,7},{10,... | collective-permute-start | bytes 786440 | tf_op jit(solution)/shard_map/ppermute | solution.py:453
  20.9 0.0 collective-permute-start.10
  20.9 0.0 collective-permute-done.2.refs_6_.refs_3_
  20.9 2.8 %collective-permute-start.3 = (f32[32,2048]{1,0:T(8,128)S(1)}, f32[32,2048]{1,0:T(8,128)S(1)}, u32[]{:S(2)}, u32[]{:S(2)}) collective-permute-start(f32[32,2048]{1,0:T(8,128)S(1)} %collective-permute-done.2.refs_6_.refs_3_), channel_id=1, source_target_pairs={{0,2},{1,15},{2,4},{3,1},{4,6},{5,3},{6,8},{7,5},{8,10},{9,7},{10,... | collective-permute-start | bytes 786440 | tf_op jit(solution)/shard_map/ppermute | solution.py:453
  23.7 0.5 collective-permute-start.9
  24.2 3.7 %collective-permute-start.16 = (f32[32,2048]{1,0:T(8,128)S(1)}, f32[32,2048]{1,0:T(8,128)S(1)}, u32[]{:S(2)}, u32[]{:S(2)}) collective-permute-start(f32[32,2048]{1,0:T(8,128)S(1)} %collective-permute-done.11.refs_9_.refs_4_), channel_id=1, source_target_pairs={{0,1},{1,0},{2,3},{3,2},{4,5},{5,4},{6,7},{7,6},{8,9},{9,8},{10,11... | collective-permute-start | bytes 786440 | tf_op jit(solution)/shard_map/ppermute | solution.py:456
  27.9 0.0 collective-permute-done.10.refs_8_
  27.9 0.0 collective-permute-start.12
  27.9 2.8 %collective-permute-start.4 = (f32[32,2048]{1,0:T(8,128)S(1)}, f32[32,2048]{1,0:T(8,128)S(1)}, u32[]{:S(2)}, u32[]{:S(2)}) collective-permute-start(f32[32,2048]{1,0:T(8,128)S(1)} %collective-permute-done.3.refs_10_.refs_5_), channel_id=1, source_target_pairs={{0,1},{1,0},{2,3},{3,2},{4,5},{5,4},{6,7},{7,6},{8,9},{9,8},{10,11... | collective-permute-start | bytes 786440 | tf_op jit(solution)/shard_map/ppermute | solution.py:456
  30.7 5.1 %mixed.1 = (f32[384,512]{1,0:T(8,128)}, f32[32,2048]{1,0:T(8,128)S(1)}, bf16[2048,384]{1,0:T(8,128)(2,1)}, bf16[2048,384]{1,0:T(8,128)(2,1)}) custom-call(f32[32,2048]{1,0:T(8,128)} %bitcast.22, f32[32,2048]{1,0:T(8,128)S(1)} %collective-permute-done.refs_0_.other_ref, f32[32,2048]{1,0:T(8,128)S(1)} %collective-permute-done.5.refs_1_.refs_0_, ...), custom_call_target="tpu_custom_call" | custom-call | flops 3000000000 | bytes 1048576 | tf_op jit(solution)/shard_map/mixed/pallas_call | solution.py:354
  35.8 0.3 collective-permute-start.17
  36.1 1.4 %gram_part.1 = f32[96,128]{1,0:T(8,128)S(1)} custom-call(s32[1]{0:T(128)} %bitcast.18.core_ref, f32[32,2048]{1,0:T(8,128)S(1)} %get-tuple-element.32.own_ref, f32[32,2048]{1,0:T(8,128)S(1)} %collective-permute-done.refs_0_.other_ref, f32[32,2048]{1,0:T(8,128)S(1)} %collective-permute-done.5.refs_1_.refs_0_, ...), custom_call_target="tpu_custom_call" | custom-call | flops 2000000000 | bytes 1048576 | tf_op jit(solution)/shard_map/gram_part/pallas_call | solution.py:267
  37.5 2.6 %collective-permute-start.15 = (f32[96,128]{1,0:T(8,128)S(1)}, f32[96,128]{1,0:T(8,128)S(1)}, u32[]{:S(2)}, u32[]{:S(2)}) collective-permute-start(f32[96,128]{1,0:T(8,128)S(1)} %gram_part.1), channel_id=1, source_target_pairs={{0,48},{16,0},{32,16},{48,32},{64,112},{80,64},{96,80},{112,96},{1... | collective-permute-start | bytes 147464 | tf_op jit(solution)/shard_map/ppermute | solution.py:229
  40.0 0.5 collective-permute-start.14
  40.5 0.6 collective-permute-start.13
  41.2 3.1 %mixed_last.1 = (f32[128,512]{1,0:T(8,128)S(1)}, f32[128,512]{1,0:T(8,128)S(1)}, f32[128,512]{1,0:T(8,128)S(1)}, f32[128,512]{1,0:T(8,128)S(1)}, bf16[2048,128]{1,0:T(8,128)(2,1)}, /*index=5*/bf16[2048,128]{1,0:T(8,128)(2,1)}) custom-call(s32[1]{0:T(128)} %bitcast.16.place_ref, f32[384,512]{1,0:T(8,128)} %get-tuple-element.36.done_ref, ...), custom_call_target="tpu_custom_call" | custom-call | flops 3000000000 | bytes 1048576 | tf_op jit(solution)/shard_map/mixed_last/pallas_call | solution.py:375
  44.2 0.2 collective-permute-done.14
  44.5 0.5 collective-permute-done.13
  45.0 2.8 %collective-permute-start.20 = (f32[96,128]{1,0:T(8,128)S(1)}, f32[96,128]{1,0:T(8,128)S(1)}, u32[]{:S(2)}, u32[]{:S(2)}) collective-permute-start(f32[96,128]{1,0:T(8,128)S(1)} %add_add_fusion.3), channel_id=1, source_target_pairs={{0,192},{16,208},{32,224},{48,240},{64,0},{80,16},{96,32},{112,48}... | collective-permute-start | bytes 147464 | tf_op jit(solution)/shard_map/ppermute | solution.py:229
  47.8 0.3 collective-permute-start.19
  48.2 0.7 collective-permute-start.18
  48.9 0.1 stack.71.place_ref
  49.0 0.9 collective-permute-start.21
  49.8 1.7 %collective-permute-start.22 = (f32[128,512]{1,0:T(8,128)S(1)}, f32[128,512]{1,0:T(8,128)S(1)}, u32[]{:S(2)}, u32[]{:S(2)}) collective-permute-start(f32[128,512]{1,0:T(8,128)S(1)} %get-tuple-element.53), channel_id=1, source_target_pairs={{0,32},{16,48},{32,0},{48,16},{64,96},{80,112},{96,64},{112,80},{1... | collective-permute-start | bytes 786440 | tf_op jit(solution)/shard_map/ppermute | solution.py:477
  51.6 1.1 collective-permute-start.23
  52.6 0.2 collective-permute-done.18
  52.8 19.9 %all_gather.3.part_ref = f32[1536,128]{1,0:T(8,128)S(1)} all-gather(f32[96,128]{1,0:T(8,128)S(1)} %add_add_fusion.2), channel_id=1, replica_groups=mesh['row'=16,'col'=16] {'col'}, dimensions={0}, use_global_device_ids=true | all-gather | bytes 835584 | tf_op jit(solution)/shard_map/all_gather | solution.py:481
  72.7 0.1 add_add_fusion.1
  72.8 1.9 %collective-permute-start.26 = (f32[128,512]{1,0:T(8,128)S(1)}, f32[128,512]{1,0:T(8,128)S(1)}, u32[]{:S(2)}, u32[]{:S(2)}) collective-permute-start(f32[128,512]{1,0:T(8,128)S(1)} %add_add_fusion.1), channel_id=1, source_target_pairs={{0,192},{16,208},{32,224},{48,240},{64,0},{80,16},{96,32},{112,48}... | collective-permute-start | bytes 786440 | tf_op jit(solution)/shard_map/ppermute | solution.py:229
  74.7 1.4 %collective-permute-start.25 = (f32[128,512]{1,0:T(8,128)S(1)}, f32[128,512]{1,0:T(8,128)S(1)}, u32[]{:S(2)}, u32[]{:S(2)}) collective-permute-start(f32[128,512]{1,0:T(8,128)S(1)} %add_add_fusion.1), channel_id=1, source_target_pairs={{0,128},{16,144},{32,160},{48,176},{64,192},{80,208},{96,224},{112... | collective-permute-start | bytes 786440 | tf_op jit(solution)/shard_map/ppermute | solution.py:229
  76.1 0.0 collective-permute-start.24
  76.1 9.4 %factor_first.1 = (f32[512,512]{1,0:T(8,128)S(1)}, f32[512,512]{1,0:T(8,128)S(1)}) custom-call(f32[1536,128]{1,0:T(8,128)S(1)} %all_gather.3.part_ref), custom_call_target="tpu_custom_call" | custom-call | flops 10000000000 | bytes 1048576 | tf_op jit(solution)/shard_map/factor_first/pallas_call | solution.py:196
  85.6 4.5 %collective-permute-done.24 = f32[128,512]{1,0:T(8,128)S(1)} collective-permute-done((f32[128,512]{1,0:T(8,128)S(1)}, f32[128,512]{1,0:T(8,128)S(1)}, u32[]{:S(2)}, u32[]{:S(2)}) %collective-permute-start.24) | collective-permute-done | bytes 262176 | tf_op jit(solution)/shard_map/ppermute | solution.py:229
  90.0 0.1 add_add_fusion.refs_4_
  90.1 0.2 collective-permute-start.29
  90.4 1.7 %collective-permute-start.28 = (f32[128,512]{1,0:T(8,128)S(1)}, f32[128,512]{1,0:T(8,128)S(1)}, u32[]{:S(2)}, u32[]{:S(2)}) collective-permute-start(f32[128,512]{1,0:T(8,128)S(1)} %add_add_fusion.refs_4_), channel_id=1, source_target_pairs={{0,32},{16,48},{32,0},{48,16},{64,96},{80,112},{96,64},{112,80},{1... | collective-permute-start | bytes 786440 | tf_op jit(solution)/shard_map/ppermute | solution.py:229
  92.1 0.7 collective-permute-start.27
  92.8 9.1 %factor_second.1 = (f32[512,512]{1,0:T(8,128)S(1)}, f32[512,512]{1,0:T(8,128)S(1)}, f32[32,512]{1,0:T(8,128)}, bf16[512,512]{1,0:T(8,128)(2,1)S(1)}, bf16[512,51...) custom-call(s32[17]{0:T(128)S(1)} %stack.71.place_ref, ...), custom_call_target="tpu_custom_call", output_to_operand_aliasing={{0}: (1, {}), {1}: (2, {})} | custom-call | flops 8000000000 | bytes 1048576 | tf_op jit(solution)/shard_map/factor_second/pallas_call | solution.py:210
  101.9 3.8 %collective-permute-done.27.refs_5_ = f32[128,512]{1,0:T(8,128)S(1)} collective-permute-done((f32[128,512]{1,0:T(8,128)S(1)}, f32[128,512]{1,0:T(8,128)S(1)}, u32[]{:S(2)}, u32[]{:S(2)}) %collective-permute-start.27) | collective-permute-done | bytes 262176 | tf_op jit(solution)/shard_map/ppermute | solution.py:229
  105.8 6.3 %finish.1 = (f32[512,512]{1,0:T(8,128)}, f32[2048,512]{1,0:T(8,128)}) custom-call(bf16[512,512]{1,0:T(8,128)(2,1)S(1)} %get-tuple-element.47.refs_0_, bf16[512,512]{1,0:T(8,128)(2,1)S(1)} %get-tuple-element.48.refs_1_, bf16[512,512]{1,0:T(8,128)(2,1)S(1)} %get-tuple-element.49.refs_2_, bf16[512,512]{1,0:T(8,128)(2,1)S(1)} %get-tuple-element.50.refs_3_, ...), custom_call_target="tpu_custom_call" | custom-call | flops 8000000000 | bytes 1048576 | tf_op jit(solution)/shard_map/finish/pallas_call | solution.py:419
  (34 shorter events, 0.1 us)
Async XLA Ops:
  0.6 7.2 %collective-permute-start = (f32[32,2048]{1,0:T(8,128)}, f32[32,2048]{1,0:T(8,128)S(1)}, u32[]{:S(2)}, u32[]{:S(2)}) collective-permute-start(f32[32,2048]{1,0:T(8,128)} %bitcast.20), channel_id=1, source_target_pairs={{0,1},{1,0},{2,3},{3,2},{4,5},{5,4},{6,7},{7,6},{8,9},{9,8},{10,11... | collective-permute-start | bytes 786440 | tf_op jit(solution)/shard_map/ppermute | solution.py:456
  4.0 7.5 %collective-permute-start.5 = (f32[32,2048]{1,0:T(8,128)}, f32[32,2048]{1,0:T(8,128)S(1)}, u32[]{:S(2)}, u32[]{:S(2)}) collective-permute-start(f32[32,2048]{1,0:T(8,128)} %bitcast.21), channel_id=1, source_target_pairs={{0,2},{1,15},{2,4},{3,1},{4,6},{5,3},{6,8},{7,5},{8,10},{9,7},{10,... | collective-permute-start | bytes 786440 | tf_op jit(solution)/shard_map/ppermute | solution.py:453
  7.8 6.6 %collective-permute-start.1 = (f32[32,2048]{1,0:T(8,128)S(1)}, f32[32,2048]{1,0:T(8,128)S(1)}, u32[]{:S(2)}, u32[]{:S(2)}) collective-permute-start(f32[32,2048]{1,0:T(8,128)S(1)} %collective-permute-done.refs_0_.other_ref), channel_id=1, source_target_pairs={{0,2},{1,15},{2,4},{3,1},{4,6},{5,3},{6,8},{7,5},{8,10},{9,7},{10,... | collective-permute-start | bytes 786440 | tf_op jit(solution)/shard_map/ppermute | solution.py:453
  11.4 6.3 %collective-permute-start.8 = (f32[32,2048]{1,0:T(8,128)S(1)}, f32[32,2048]{1,0:T(8,128)S(1)}, u32[]{:S(2)}, u32[]{:S(2)}) collective-permute-start(f32[32,2048]{1,0:T(8,128)S(1)} %collective-permute-done.5.refs_1_.refs_0_), channel_id=1, source_target_pairs={{0,2},{1,15},{2,4},{3,1},{4,6},{5,3},{6,8},{7,5},{8,10},{9,7},{10,... | collective-permute-start | bytes 786440 | tf_op jit(solution)/shard_map/ppermute | solution.py:453
  14.4 6.4 %collective-permute-start.2 = (f32[32,2048]{1,0:T(8,128)S(1)}, f32[32,2048]{1,0:T(8,128)S(1)}, u32[]{:S(2)}, u32[]{:S(2)}) collective-permute-start(f32[32,2048]{1,0:T(8,128)S(1)} %collective-permute-done.1.refs_2_.refs_1_), channel_id=1, source_target_pairs={{0,2},{1,15},{2,4},{3,1},{4,6},{5,3},{6,8},{7,5},{8,10},{9,7},{10,... | collective-permute-start | bytes 786440 | tf_op jit(solution)/shard_map/ppermute | solution.py:453
  17.3 6.4 %collective-permute-start.7 = (f32[32,2048]{1,0:T(8,128)S(1)}, f32[32,2048]{1,0:T(8,128)S(1)}, u32[]{:S(2)}, u32[]{:S(2)}) collective-permute-start(f32[32,2048]{1,0:T(8,128)S(1)} %collective-permute-done.5.refs_1_.refs_0_), channel_id=1, source_target_pairs={{0,1},{1,0},{2,3},{3,2},{4,5},{5,4},{6,7},{7,6},{8,9},{9,8},{10,11... | collective-permute-start | bytes 786440 | tf_op jit(solution)/shard_map/ppermute | solution.py:456
  17.8 6.4 %collective-permute-start.11 = (f32[32,2048]{1,0:T(8,128)S(1)}, f32[32,2048]{1,0:T(8,128)S(1)}, u32[]{:S(2)}, u32[]{:S(2)}) collective-permute-start(f32[32,2048]{1,0:T(8,128)S(1)} %collective-permute-done.8.refs_5_.refs_2_), channel_id=1, source_target_pairs={{0,2},{1,15},{2,4},{3,1},{4,6},{5,3},{6,8},{7,5},{8,10},{9,7},{10,... | collective-permute-start | bytes 786440 | tf_op jit(solution)/shard_map/ppermute | solution.py:453
  20.9 7.0 %collective-permute-start.10 = (f32[32,2048]{1,0:T(8,128)S(1)}, f32[32,2048]{1,0:T(8,128)S(1)}, u32[]{:S(2)}, u32[]{:S(2)}) collective-permute-start(f32[32,2048]{1,0:T(8,128)S(1)} %collective-permute-done.8.refs_5_.refs_2_), channel_id=1, source_target_pairs={{0,1},{1,0},{2,3},{3,2},{4,5},{5,4},{6,7},{7,6},{8,9},{9,8},{10,11... | collective-permute-start | bytes 786440 | tf_op jit(solution)/shard_map/ppermute | solution.py:456
  20.9 7.0 %collective-permute-start.3 = (f32[32,2048]{1,0:T(8,128)S(1)}, f32[32,2048]{1,0:T(8,128)S(1)}, u32[]{:S(2)}, u32[]{:S(2)}) collective-permute-start(f32[32,2048]{1,0:T(8,128)S(1)} %collective-permute-done.2.refs_6_.refs_3_), channel_id=1, source_target_pairs={{0,2},{1,15},{2,4},{3,1},{4,6},{5,3},{6,8},{7,5},{8,10},{9,7},{10,... | collective-permute-start | bytes 786440 | tf_op jit(solution)/shard_map/ppermute | solution.py:453
  23.7 7.0 %collective-permute-start.6 = (f32[32,2048]{1,0:T(8,128)S(1)}, f32[32,2048]{1,0:T(8,128)S(1)}, u32[]{:S(2)}, u32[]{:S(2)}) collective-permute-start(f32[32,2048]{1,0:T(8,128)S(1)} %collective-permute-done.1.refs_2_.refs_1_), channel_id=1, source_target_pairs={{0,1},{1,0},{2,3},{3,2},{4,5},{5,4},{6,7},{7,6},{8,9},{9,8},{10,11... | collective-permute-start | bytes 786440 | tf_op jit(solution)/shard_map/ppermute | solution.py:456
  23.7 7.0 %collective-permute-start.9 = (f32[32,2048]{1,0:T(8,128)S(1)}, f32[32,2048]{1,0:T(8,128)S(1)}, u32[]{:S(2)}, u32[]{:S(2)}) collective-permute-start(f32[32,2048]{1,0:T(8,128)S(1)} %collective-permute-done.2.refs_6_.refs_3_), channel_id=1, source_target_pairs={{0,1},{1,0},{2,3},{3,2},{4,5},{5,4},{6,7},{7,6},{8,9},{9,8},{10,11... | collective-permute-start | bytes 786440 | tf_op jit(solution)/shard_map/ppermute | solution.py:456
  24.2 17.0 %collective-permute-start.16 = (f32[32,2048]{1,0:T(8,128)S(1)}, f32[32,2048]{1,0:T(8,128)S(1)}, u32[]{:S(2)}, u32[]{:S(2)}) collective-permute-start(f32[32,2048]{1,0:T(8,128)S(1)} %collective-permute-done.11.refs_9_.refs_4_), channel_id=1, source_target_pairs={{0,1},{1,0},{2,3},{3,2},{4,5},{5,4},{6,7},{7,6},{8,9},{9,8},{10,11... | collective-permute-start | bytes 786440 | tf_op jit(solution)/shard_map/ppermute | solution.py:456
  27.9 7.9 %collective-permute-start.12 = (f32[32,2048]{1,0:T(8,128)S(1)}, f32[32,2048]{1,0:T(8,128)S(1)}, u32[]{:S(2)}, u32[]{:S(2)}) collective-permute-start(f32[32,2048]{1,0:T(8,128)S(1)} %collective-permute-done.11.refs_9_.refs_4_), channel_id=1, source_target_pairs={{0,2},{1,15},{2,4},{3,1},{4,6},{5,3},{6,8},{7,5},{8,10},{9,7},{10,... | collective-permute-start | bytes 786440 | tf_op jit(solution)/shard_map/ppermute | solution.py:453
  27.9 12.6 %collective-permute-start.4 = (f32[32,2048]{1,0:T(8,128)S(1)}, f32[32,2048]{1,0:T(8,128)S(1)}, u32[]{:S(2)}, u32[]{:S(2)}) collective-permute-start(f32[32,2048]{1,0:T(8,128)S(1)} %collective-permute-done.3.refs_10_.refs_5_), channel_id=1, source_target_pairs={{0,1},{1,0},{2,3},{3,2},{4,5},{5,4},{6,7},{7,6},{8,9},{9,8},{10,11... | collective-permute-start | bytes 786440 | tf_op jit(solution)/shard_map/ppermute | solution.py:456
  35.8 5.4 %collective-permute-start.17 = (f32[32,2048]{1,0:T(8,128)S(1)}, f32[32,2048]{1,0:T(8,128)S(1)}, u32[]{:S(2)}, u32[]{:S(2)}) collective-permute-start(f32[32,2048]{1,0:T(8,128)S(1)} %collective-permute-done.12.refs_6_.refs_2_), channel_id=1, source_target_pairs={{0,1},{1,0},{2,3},{3,2},{4,5},{5,4},{6,7},{7,6},{8,9},{9,8},{10,11... | collective-permute-start | bytes 786440 | tf_op jit(solution)/shard_map/ppermute | solution.py:456
  37.5 6.8 %collective-permute-start.15 = (f32[96,128]{1,0:T(8,128)S(1)}, f32[96,128]{1,0:T(8,128)S(1)}, u32[]{:S(2)}, u32[]{:S(2)}) collective-permute-start(f32[96,128]{1,0:T(8,128)S(1)} %gram_part.1), channel_id=1, source_target_pairs={{0,48},{16,0},{32,16},{48,32},{64,112},{80,64},{96,80},{112,96},{1... | collective-permute-start | bytes 147464 | tf_op jit(solution)/shard_map/ppermute | solution.py:229
  40.0 4.5 %collective-permute-start.14 = (f32[96,128]{1,0:T(8,128)S(1)}, f32[96,128]{1,0:T(8,128)S(1)}, u32[]{:S(2)}, u32[]{:S(2)}) collective-permute-start(f32[96,128]{1,0:T(8,128)S(1)} %gram_part.1), channel_id=1, source_target_pairs={{0,32},{16,48},{32,0},{48,16},{64,96},{80,112},{96,64},{112,80},{1... | collective-permute-start | bytes 147464 | tf_op jit(solution)/shard_map/ppermute | solution.py:229
  40.5 4.5 %collective-permute-start.13 = (f32[96,128]{1,0:T(8,128)S(1)}, f32[96,128]{1,0:T(8,128)S(1)}, u32[]{:S(2)}, u32[]{:S(2)}) collective-permute-start(f32[96,128]{1,0:T(8,128)S(1)} %gram_part.1), channel_id=1, source_target_pairs={{0,16},{16,32},{32,48},{48,0},{64,80},{80,96},{96,112},{112,64},{1... | collective-permute-start | bytes 147464 | tf_op jit(solution)/shard_map/ppermute | solution.py:229
  45.0 6.5 %collective-permute-start.20 = (f32[96,128]{1,0:T(8,128)S(1)}, f32[96,128]{1,0:T(8,128)S(1)}, u32[]{:S(2)}, u32[]{:S(2)}) collective-permute-start(f32[96,128]{1,0:T(8,128)S(1)} %add_add_fusion.3), channel_id=1, source_target_pairs={{0,192},{16,208},{32,224},{48,240},{64,0},{80,16},{96,32},{112,48}... | collective-permute-start | bytes 147464 | tf_op jit(solution)/shard_map/ppermute | solution.py:229
  47.8 4.8 %collective-permute-start.19 = (f32[96,128]{1,0:T(8,128)S(1)}, f32[96,128]{1,0:T(8,128)S(1)}, u32[]{:S(2)}, u32[]{:S(2)}) collective-permute-start(f32[96,128]{1,0:T(8,128)S(1)} %add_add_fusion.3), channel_id=1, source_target_pairs={{0,128},{16,144},{32,160},{48,176},{64,192},{80,208},{96,224},{112... | collective-permute-start | bytes 147464 | tf_op jit(solution)/shard_map/ppermute | solution.py:229
  48.2 4.6 %collective-permute-start.18 = (f32[96,128]{1,0:T(8,128)S(1)}, f32[96,128]{1,0:T(8,128)S(1)}, u32[]{:S(2)}, u32[]{:S(2)}) collective-permute-start(f32[96,128]{1,0:T(8,128)S(1)} %add_add_fusion.3), channel_id=1, source_target_pairs={{0,64},{16,80},{32,96},{48,112},{64,128},{80,144},{96,160},{112,17... | collective-permute-start | bytes 147464 | tf_op jit(solution)/shard_map/ppermute | solution.py:229
  49.0 23.7 %collective-permute-start.21 = (f32[128,512]{1,0:T(8,128)S(1)}, f32[128,512]{1,0:T(8,128)S(1)}, u32[]{:S(2)}, u32[]{:S(2)}) collective-permute-start(f32[128,512]{1,0:T(8,128)S(1)} %get-tuple-element.52), channel_id=1, source_target_pairs={{0,16},{16,32},{32,48},{48,0},{64,80},{80,96},{96,112},{112,64},{1... | collective-permute-start | bytes 786440 | tf_op jit(solution)/shard_map/ppermute | solution.py:477
  49.8 22.9 %collective-permute-start.22 = (f32[128,512]{1,0:T(8,128)S(1)}, f32[128,512]{1,0:T(8,128)S(1)}, u32[]{:S(2)}, u32[]{:S(2)}) collective-permute-start(f32[128,512]{1,0:T(8,128)S(1)} %get-tuple-element.53), channel_id=1, source_target_pairs={{0,32},{16,48},{32,0},{48,16},{64,96},{80,112},{96,64},{112,80},{1... | collective-permute-start | bytes 786440 | tf_op jit(solution)/shard_map/ppermute | solution.py:477
  51.6 21.2 %collective-permute-start.23 = (f32[128,512]{1,0:T(8,128)S(1)}, f32[128,512]{1,0:T(8,128)S(1)}, u32[]{:S(2)}, u32[]{:S(2)}) collective-permute-start(f32[128,512]{1,0:T(8,128)S(1)} %get-tuple-element.54), channel_id=1, source_target_pairs={{0,48},{16,0},{32,16},{48,32},{64,112},{80,64},{96,80},{112,96},{1... | collective-permute-start | bytes 786440 | tf_op jit(solution)/shard_map/ppermute | solution.py:477
  72.8 12.7 %collective-permute-start.26 = (f32[128,512]{1,0:T(8,128)S(1)}, f32[128,512]{1,0:T(8,128)S(1)}, u32[]{:S(2)}, u32[]{:S(2)}) collective-permute-start(f32[128,512]{1,0:T(8,128)S(1)} %add_add_fusion.1), channel_id=1, source_target_pairs={{0,192},{16,208},{32,224},{48,240},{64,0},{80,16},{96,32},{112,48}... | collective-permute-start | bytes 786440 | tf_op jit(solution)/shard_map/ppermute | solution.py:229
  74.7 10.9 %collective-permute-start.25 = (f32[128,512]{1,0:T(8,128)S(1)}, f32[128,512]{1,0:T(8,128)S(1)}, u32[]{:S(2)}, u32[]{:S(2)}) collective-permute-start(f32[128,512]{1,0:T(8,128)S(1)} %add_add_fusion.1), channel_id=1, source_target_pairs={{0,128},{16,144},{32,160},{48,176},{64,192},{80,208},{96,224},{112... | collective-permute-start | bytes 786440 | tf_op jit(solution)/shard_map/ppermute | solution.py:229
  76.1 13.9 %collective-permute-start.24 = (f32[128,512]{1,0:T(8,128)S(1)}, f32[128,512]{1,0:T(8,128)S(1)}, u32[]{:S(2)}, u32[]{:S(2)}) collective-permute-start(f32[128,512]{1,0:T(8,128)S(1)} %add_add_fusion.1), channel_id=1, source_target_pairs={{0,64},{16,80},{32,96},{48,112},{64,128},{80,144},{96,160},{112,17... | collective-permute-start | bytes 786440 | tf_op jit(solution)/shard_map/ppermute | solution.py:229
  90.1 11.8 %collective-permute-start.29 = (f32[128,512]{1,0:T(8,128)S(1)}, f32[128,512]{1,0:T(8,128)S(1)}, u32[]{:S(2)}, u32[]{:S(2)}) collective-permute-start(f32[128,512]{1,0:T(8,128)S(1)} %add_add_fusion.refs_4_), channel_id=1, source_target_pairs={{0,48},{16,0},{32,16},{48,32},{64,112},{80,64},{96,80},{112,96},{1... | collective-permute-start | bytes 786440 | tf_op jit(solution)/shard_map/ppermute | solution.py:229
  90.4 11.5 %collective-permute-start.28 = (f32[128,512]{1,0:T(8,128)S(1)}, f32[128,512]{1,0:T(8,128)S(1)}, u32[]{:S(2)}, u32[]{:S(2)}) collective-permute-start(f32[128,512]{1,0:T(8,128)S(1)} %add_add_fusion.refs_4_), channel_id=1, source_target_pairs={{0,32},{16,48},{32,0},{48,16},{64,96},{80,112},{96,64},{112,80},{1... | collective-permute-start | bytes 786440 | tf_op jit(solution)/shard_map/ppermute | solution.py:229
  92.1 13.6 %collective-permute-start.27 = (f32[128,512]{1,0:T(8,128)S(1)}, f32[128,512]{1,0:T(8,128)S(1)}, u32[]{:S(2)}, u32[]{:S(2)}) collective-permute-start(f32[128,512]{1,0:T(8,128)S(1)} %add_add_fusion.refs_4_), channel_id=1, source_target_pairs={{0,16},{16,32},{32,48},{48,0},{64,80},{80,96},{96,112},{112,64},{1... | collective-permute-start | bytes 786440 | tf_op jit(solution)/shard_map/ppermute | solution.py:229
  92.8 12.9 %copy-start = (f32[2048,512]{1,0:T(8,128)S(1)}, f32[2048,512]{1,0:T(8,128)}, u32[]{:S(2)}) copy-start(f32[2048,512]{1,0:T(8,128)} %refs_12_.1) | copy-start | bytes 12582916
  92.8 12.9 %copy-start.1 = (bf16[2048,384]{1,0:T(8,128)(2,1)S(1)}, bf16[2048,384]{1,0:T(8,128)(2,1)}, u32[]{:S(2)}) copy-start(bf16[2048,384]{1,0:T(8,128)(2,1)} %get-tuple-element.55.refs_8_) | copy-start | bytes 4718596
  92.8 12.9 %copy-start.2 = (bf16[2048,384]{1,0:T(8,128)(2,1)S(1)}, bf16[2048,384]{1,0:T(8,128)(2,1)}, u32[]{:S(2)}) copy-start(bf16[2048,384]{1,0:T(8,128)(2,1)} %get-tuple-element.57.refs_10_) | copy-start | bytes 4718596
  92.8 12.9 %copy-start.3 = (bf16[2048,128]{1,0:T(8,128)(2,1)S(1)}, bf16[2048,128]{1,0:T(8,128)(2,1)}, u32[]{:S(2)}) copy-start(bf16[2048,128]{1,0:T(8,128)(2,1)} %get-tuple-element.56.refs_9_) | copy-start | bytes 1572868
  92.8 12.9 %copy-start.4 = (bf16[2048,128]{1,0:T(8,128)(2,1)S(1)}, bf16[2048,128]{1,0:T(8,128)(2,1)}, u32[]{:S(2)}) copy-start(bf16[2048,128]{1,0:T(8,128)(2,1)} %get-tuple-element.58.refs_11_) | copy-start | bytes 1572868

commit v5 on v4

--- a/solution.py
+++ b/solution.py
@@ -9,6 +9,8 @@
 
 BLOCK = 128
 SIDE = 4
+STEPS = 1, 2, 3
+LARGE_STEPS = 3, 1, 2
 NARROW = 32
 
 
@@ -164,7 +166,7 @@
 
     near = split(jnp.concatenate([rows(i) for i in range(count)], 0))
     quarter = count // SIDE
-    first = [lax.rem(place_ref[count] - k + SIDE, SIDE) * quarter for k in range(SIDE)]
+    first = [lax.rem(place_ref[count] - k + SIDE, SIDE) * quarter for k in (0, *LARGE_STEPS)]
     pieces = split(jnp.concatenate([rows(first[k] + j) for k in range(SIDE) for j in range(quarter)], 0).T)
     for i in range(2):
         by_block_refs[i][...] = near[i]
@@ -225,12 +227,12 @@
     return [(y * SIDE + x, (y + dy) % SIDE * SIDE + (x + dx) % SIDE) for y in range(SIDE) for x in range(SIDE)]
 
 
-def sent_along(value, along_y):
-    return [lax.ppermute(value, "row", shifted(k, 0) if along_y else shifted(0, k)) for k in range(1, SIDE)]
-
-
-def sum_along(value, along_y):
-    return sum(sent_along(value, along_y), value)
+def sent_along(value, along_y, steps):
+    return [lax.ppermute(value, "row", shifted(k, 0) if along_y else shifted(0, k)) for k in steps]
+
+
+def sum_along(value, along_y, steps):
+    return sum(sent_along(value, along_y, steps), value)
 
 
 LINES = [[y * SIDE + x for x in range(SIDE)] for y in range(SIDE)]
@@ -468,16 +470,16 @@
 
     received = [first[s] if core == 0 else second[s] for s in range(1, far) for core in range(2)] + [first[far]]
     part = gram_part(near, second[0], received)
-    pieces = sent_along(part, False)
+    pieces = sent_along(part, False, STEPS)
     late = blocks[4 * far - 4 :] + [first[far], exchange(first[far])]
     late[0], part = lax.optimization_barrier((late[0], part))
     *quarters, late_high, late_low = mix_last(mixed, late, trailing, 512)
     *pieces, quarters[0] = lax.optimization_barrier((*pieces, quarters[0]))
     part = sum(pieces, part)
     quarters[1:] = [lax.ppermute(quarter, "row", shifted(0, k + 1)) for k, quarter in enumerate(quarters[1:])]
-    part, quarters[0] = lax.optimization_barrier((sum_along(part, True), quarters[0]))
+    part, quarters[0] = lax.optimization_barrier((sum_along(part, True, STEPS), quarters[0]))
     mixed = sum(quarters[1:], quarters[0])
-    mixed = sum_along(mixed, True)
+    mixed = sum_along(mixed, True, LARGE_STEPS)
     parts = lax.all_gather(part, "col", axis=0, tiled=True)
 
     row, col = lax.axis_index("row"), lax.axis_index("col")
@@ -492,7 +494,7 @@
     places = jnp.stack(places).astype(jnp.int32)
 
     work, upper = factor_first(parts, width, 2)
-    quarters = [mixed] + sent_along(mixed, False)
+    quarters = [mixed] + sent_along(mixed, False, LARGE_STEPS)
     _, _, own_factor, *arranged = factor_second(places, work, upper, 2)
     highs, lows = [high, late_high], [low, late_low]
     top_rows, projected = finish(arranged[:2], arranged[2:], quarters, highs, lows, trailing, 512)

time: 112 us -> 110 us (0.982)
  waiting for transfers between devices: 12 us -> 7.55 us
  starting transfers between devices: 44.7 us -> 47.3 us
    ppermute x12, waiting for transfers between devices: 9.22 us -> 4.75 us  [sent_along(): lax.ppermute(value, 'row', shifted(k, 0) if along_y else shifted(0, k))]
    ppermute x12, starting transfers between devices: 13.5 us -> 16.1 us  [sent_along(): lax.ppermute(value, 'row', shifted(k, 0) if along_y else shifted(0, k))]
where the time goes in v5:
time: 110 us
  starting transfers between devices  47.3 us (43%)
  Pallas kernels  34.3 us (31%)
  blocking collectives  19.9 us (18%)
  waiting for transfers between devices  7.55 us (7%)
    all_gather x1, blocking collectives, on_device(): parts = lax.all_gather(part, 'col', axis=0, tiled=True)  19.9 us
    ppermute x7, starting transfers between devices, send(): return lax.ppermute(value, 'col', ring)  16.9 us
    ppermute x12, starting transfers between devices, sent_along(): lax.ppermute(value, 'row', shifted(k, 0) if along_y else shifted(0, k))  16.1 us
    ppermute x8, starting transfers between devices, exchange(): return lax.ppermute(value, 'col', swap)  10.6 us
    pallas_call x1, Pallas kernels, factor_first(): pl.pallas_call(functools.partial(first_kernel, steps), out_shape=[jax.Sha...  9.45 us
    pallas_call x1, Pallas kernels, factor_second(): pl.pallas_call(functools.partial(second_kernel, begin), out_shape=[whole,...  9.07 us
    pallas_call x1, Pallas kernels, finish(): pl.pallas_call(functools.partial(last_kernel, tile), out_shape=[jax.Shape...  6.26 us
    pallas_call x1, Pallas kernels, mix(): pl.pallas_call(functools.partial(mixed_kernel, tile), out_shape=[pltpu.HB...  5.07 us
  transfers between devices with their start and end apart: 30, of which 7 were waited for; matrix products, arithmetic and copies ran while one was open for 0% of the time, Pallas kernels for 25%

profile of v5, /device:TPU:1, one launch (start us, length us, event | category | flops | bytes accessed | tf_op | source)
XLA Modules:
  0.0 110.3 jit_solution(13775582619442393519)
XLA Ops:
  0.6 3.3 %collective-permute-start = (f32[32,2048]{1,0:T(8,128)}, f32[32,2048]{1,0:T(8,128)S(1)}, u32[]{:S(2)}, u32[]{:S(2)}) collective-permute-start(f32[32,2048]{1,0:T(8,128)} %bitcast.20), channel_id=1, source_target_pairs={{0,1},{1,0},{2,3},{3,2},{4,5},{5,4},{6,7},{7,6},{8,9},{9,8},{10,11... | collective-permute-start | bytes 786440 | tf_op jit(solution)/shard_map/ppermute | solution.py:458
  4.0 3.8 %collective-permute-start.5 = (f32[32,2048]{1,0:T(8,128)}, f32[32,2048]{1,0:T(8,128)S(1)}, u32[]{:S(2)}, u32[]{:S(2)}) collective-permute-start(f32[32,2048]{1,0:T(8,128)} %bitcast.21), channel_id=1, source_target_pairs={{0,2},{1,15},{2,4},{3,1},{4,6},{5,3},{6,8},{7,5},{8,10},{9,7},{10,... | collective-permute-start | bytes 786440 | tf_op jit(solution)/shard_map/ppermute | solution.py:455
  7.8 0.0 collective-permute-done.refs_0_.other_ref
  7.8 1.4 %collective-permute-start.1 = (f32[32,2048]{1,0:T(8,128)S(1)}, f32[32,2048]{1,0:T(8,128)S(1)}, u32[]{:S(2)}, u32[]{:S(2)}) collective-permute-start(f32[32,2048]{1,0:T(8,128)S(1)} %collective-permute-done.refs_0_.other_ref), channel_id=1, source_target_pairs={{0,2},{1,15},{2,4},{3,1},{4,6},{5,3},{6,8},{7,5},{8,10},{9,7},{10,... | collective-permute-start | bytes 786440 | tf_op jit(solution)/shard_map/ppermute | solution.py:455
  9.2 2.3 %collective-permute-done.5.refs_1_.refs_0_ = f32[32,2048]{1,0:T(8,128)S(1)} collective-permute-done((f32[32,2048]{1,0:T(8,128)}, f32[32,2048]{1,0:T(8,128)S(1)}, u32[]{:S(2)}, u32[]{:S(2)}) %collective-permute-start.5) | collective-permute-done | bytes 262176 | tf_op jit(solution)/shard_map/ppermute | solution.py:455
  11.4 3.0 %collective-permute-start.8 = (f32[32,2048]{1,0:T(8,128)S(1)}, f32[32,2048]{1,0:T(8,128)S(1)}, u32[]{:S(2)}, u32[]{:S(2)}) collective-permute-start(f32[32,2048]{1,0:T(8,128)S(1)} %collective-permute-done.5.refs_1_.refs_0_), channel_id=1, source_target_pairs={{0,2},{1,15},{2,4},{3,1},{4,6},{5,3},{6,8},{7,5},{8,10},{9,7},{10,... | collective-permute-start | bytes 786440 | tf_op jit(solution)/shard_map/ppermute | solution.py:455
  14.4 2.8 %collective-permute-start.2 = (f32[32,2048]{1,0:T(8,128)S(1)}, f32[32,2048]{1,0:T(8,128)S(1)}, u32[]{:S(2)}, u32[]{:S(2)}) collective-permute-start(f32[32,2048]{1,0:T(8,128)S(1)} %collective-permute-done.1.refs_2_.refs_1_), channel_id=1, source_target_pairs={{0,2},{1,15},{2,4},{3,1},{4,6},{5,3},{6,8},{7,5},{8,10},{9,7},{10,... | collective-permute-start | bytes 786440 | tf_op jit(solution)/shard_map/ppermute | solution.py:455
  17.3 0.0 collective-permute-start.7
  17.3 0.5 collective-permute-done.8.refs_5_.refs_2_
  17.8 3.1 %collective-permute-start.11 = (f32[32,2048]{1,0:T(8,128)S(1)}, f32[32,2048]{1,0:T(8,128)S(1)}, u32[]{:S(2)}, u32[]{:S(2)}) collective-permute-start(f32[32,2048]{1,0:T(8,128)S(1)} %collective-permute-done.8.refs_5_.refs_2_), channel_id=1, source_target_pairs={{0,2},{1,15},{2,4},{3,1},{4,6},{5,3},{6,8},{7,5},{8,10},{9,7},{10,... | collective-permute-start | bytes 786440 | tf_op jit(solution)/shard_map/ppermute | solution.py:455
  20.9 2.8 %collective-permute-start.3 = (f32[32,2048]{1,0:T(8,128)S(1)}, f32[32,2048]{1,0:T(8,128)S(1)}, u32[]{:S(2)}, u32[]{:S(2)}) collective-permute-start(f32[32,2048]{1,0:T(8,128)S(1)} %collective-permute-done.2.refs_6_.refs_3_), channel_id=1, source_target_pairs={{0,2},{1,15},{2,4},{3,1},{4,6},{5,3},{6,8},{7,5},{8,10},{9,7},{10,... | collective-permute-start | bytes 786440 | tf_op jit(solution)/shard_map/ppermute | solution.py:455
  23.7 0.0 collective-permute-start.6
  23.7 0.0 collective-permute-done.7.refs_4_
  23.7 0.5 collective-permute-start.9
  24.2 0.0 collective-permute-done.11.refs_9_.refs_4_
  24.2 3.7 %collective-permute-start.16 = (f32[32,2048]{1,0:T(8,128)S(1)}, f32[32,2048]{1,0:T(8,128)S(1)}, u32[]{:S(2)}, u32[]{:S(2)}) collective-permute-start(f32[32,2048]{1,0:T(8,128)S(1)} %collective-permute-done.11.refs_9_.refs_4_), channel_id=1, source_target_pairs={{0,1},{1,0},{2,3},{3,2},{4,5},{5,4},{6,7},{7,6},{8,9},{9,8},{10,11... | collective-permute-start | bytes 786440 | tf_op jit(solution)/shard_map/ppermute | solution.py:458
  27.9 2.8 %collective-permute-start.4 = (f32[32,2048]{1,0:T(8,128)S(1)}, f32[32,2048]{1,0:T(8,128)S(1)}, u32[]{:S(2)}, u32[]{:S(2)}) collective-permute-start(f32[32,2048]{1,0:T(8,128)S(1)} %collective-permute-done.3.refs_10_.refs_5_), channel_id=1, source_target_pairs={{0,1},{1,0},{2,3},{3,2},{4,5},{5,4},{6,7},{7,6},{8,9},{9,8},{10,11... | collective-permute-start | bytes 786440 | tf_op jit(solution)/shard_map/ppermute | solution.py:458
  30.7 0.0 collective-permute-done.6.refs_3_
  30.7 5.1 %mixed.1 = (f32[384,512]{1,0:T(8,128)}, f32[32,2048]{1,0:T(8,128)S(1)}, bf16[2048,384]{1,0:T(8,128)(2,1)}, bf16[2048,384]{1,0:T(8,128)(2,1)}) custom-call(f32[32,2048]{1,0:T(8,128)} %bitcast.22, f32[32,2048]{1,0:T(8,128)S(1)} %collective-permute-done.refs_0_.other_ref, f32[32,2048]{1,0:T(8,128)S(1)} %collective-permute-done.5.refs_1_.refs_0_, ...), custom_call_target="tpu_custom_call" | custom-call | flops 3000000000 | bytes 1048576 | tf_op jit(solution)/shard_map/mixed/pallas_call | solution.py:356
  35.8 0.3 collective-permute-start.17
  36.1 1.4 %gram_part.1 = f32[96,128]{1,0:T(8,128)S(1)} custom-call(s32[1]{0:T(128)} %bitcast.18.core_ref, f32[32,2048]{1,0:T(8,128)S(1)} %get-tuple-element.32.own_ref, f32[32,2048]{1,0:T(8,128)S(1)} %collective-permute-done.refs_0_.other_ref, f32[32,2048]{1,0:T(8,128)S(1)} %collective-permute-done.5.refs_1_.refs_0_, ...), custom_call_target="tpu_custom_call" | custom-call | flops 2000000000 | bytes 1048576 | tf_op jit(solution)/shard_map/gram_part/pallas_call | solution.py:269
  37.5 2.6 %collective-permute-start.15 = (f32[96,128]{1,0:T(8,128)S(1)}, f32[96,128]{1,0:T(8,128)S(1)}, u32[]{:S(2)}, u32[]{:S(2)}) collective-permute-start(f32[96,128]{1,0:T(8,128)S(1)} %gram_part.1), channel_id=1, source_target_pairs={{0,48},{16,0},{32,16},{48,32},{64,112},{80,64},{96,80},{112,96},{1... | collective-permute-start | bytes 147464 | tf_op jit(solution)/shard_map/ppermute | solution.py:231
  40.0 0.5 collective-permute-start.14
  40.5 0.6 collective-permute-start.13
  41.2 3.1 %mixed_last.1 = (f32[128,512]{1,0:T(8,128)S(1)}, f32[128,512]{1,0:T(8,128)S(1)}, f32[128,512]{1,0:T(8,128)S(1)}, f32[128,512]{1,0:T(8,128)S(1)}, bf16[2048,128]{1,0:T(8,128)(2,1)}, /*index=5*/bf16[2048,128]{1,0:T(8,128)(2,1)}) custom-call(s32[1]{0:T(128)} %bitcast.16.place_ref, f32[384,512]{1,0:T(8,128)} %get-tuple-element.36.done_ref, ...), custom_call_target="tpu_custom_call" | custom-call | flops 3000000000 | bytes 1048576 | tf_op jit(solution)/shard_map/mixed_last/pallas_call | solution.py:377
  44.2 0.2 collective-permute-done.14
  44.5 0.5 collective-permute-done.13
  45.0 2.8 %collective-permute-start.20 = (f32[96,128]{1,0:T(8,128)S(1)}, f32[96,128]{1,0:T(8,128)S(1)}, u32[]{:S(2)}, u32[]{:S(2)}) collective-permute-start(f32[96,128]{1,0:T(8,128)S(1)} %add_add_fusion.3), channel_id=1, source_target_pairs={{0,192},{16,208},{32,224},{48,240},{64,0},{80,16},{96,32},{112,48}... | collective-permute-start | bytes 147464 | tf_op jit(solution)/shard_map/ppermute | solution.py:231
  47.8 0.3 collective-permute-start.19
  48.2 0.7 collective-permute-start.18
  48.9 0.1 stack.71.place_ref
  49.0 0.9 collective-permute-start.21
  49.8 1.7 %collective-permute-start.22 = (f32[128,512]{1,0:T(8,128)S(1)}, f32[128,512]{1,0:T(8,128)S(1)}, u32[]{:S(2)}, u32[]{:S(2)}) collective-permute-start(f32[128,512]{1,0:T(8,128)S(1)} %get-tuple-element.53), channel_id=1, source_target_pairs={{0,32},{16,48},{32,0},{48,16},{64,96},{80,112},{96,64},{112,80},{1... | collective-permute-start | bytes 786440 | tf_op jit(solution)/shard_map/ppermute | solution.py:479
  51.6 1.1 collective-permute-start.23
  52.6 0.2 collective-permute-done.18
  52.8 19.9 %all_gather.3.part_ref = f32[1536,128]{1,0:T(8,128)S(1)} all-gather(f32[96,128]{1,0:T(8,128)S(1)} %add_add_fusion.2), channel_id=1, replica_groups=mesh['row'=16,'col'=16] {'col'}, dimensions={0}, use_global_device_ids=true | all-gather | bytes 835584 | tf_op jit(solution)/shard_map/all_gather | solution.py:483
  72.7 0.1 add_add_fusion.1
  72.8 1.5 %collective-permute-start.26 = (f32[128,512]{1,0:T(8,128)S(1)}, f32[128,512]{1,0:T(8,128)S(1)}, u32[]{:S(2)}, u32[]{:S(2)}) collective-permute-start(f32[128,512]{1,0:T(8,128)S(1)} %add_add_fusion.1), channel_id=1, source_target_pairs={{0,128},{16,144},{32,160},{48,176},{64,192},{80,208},{96,224},{112... | collective-permute-start | bytes 786440 | tf_op jit(solution)/shard_map/ppermute | solution.py:231
  74.4 0.9 collective-permute-start.25
  75.3 1.8 %collective-permute-start.24 = (f32[128,512]{1,0:T(8,128)S(1)}, f32[128,512]{1,0:T(8,128)S(1)}, u32[]{:S(2)}, u32[]{:S(2)}) collective-permute-start(f32[128,512]{1,0:T(8,128)S(1)} %add_add_fusion.1), channel_id=1, source_target_pairs={{0,192},{16,208},{32,224},{48,240},{64,0},{80,16},{96,32},{112,48}... | collective-permute-start | bytes 786440 | tf_op jit(solution)/shard_map/ppermute | solution.py:231
  77.0 9.5 %factor_first.1 = (f32[512,512]{1,0:T(8,128)S(1)}, f32[512,512]{1,0:T(8,128)S(1)}) custom-call(f32[1536,128]{1,0:T(8,128)S(1)} %all_gather.3.part_ref), custom_call_target="tpu_custom_call" | custom-call | flops 10000000000 | bytes 1048576 | tf_op jit(solution)/shard_map/factor_first/pallas_call | solution.py:198
  86.5 1.8 %collective-permute-done.25 = f32[128,512]{1,0:T(8,128)S(1)} collective-permute-done((f32[128,512]{1,0:T(8,128)S(1)}, f32[128,512]{1,0:T(8,128)S(1)}, u32[]{:S(2)}, u32[]{:S(2)}) %collective-permute-start.25) | collective-permute-done | bytes 262176 | tf_op jit(solution)/shard_map/ppermute | solution.py:231
  88.3 0.1 add_add_fusion.refs_4_
  88.4 1.6 %collective-permute-start.29 = (f32[128,512]{1,0:T(8,128)S(1)}, f32[128,512]{1,0:T(8,128)S(1)}, u32[]{:S(2)}, u32[]{:S(2)}) collective-permute-start(f32[128,512]{1,0:T(8,128)S(1)} %add_add_fusion.refs_4_), channel_id=1, source_target_pairs={{0,32},{16,48},{32,0},{48,16},{64,96},{80,112},{96,64},{112,80},{1... | collective-permute-start | bytes 786440 | tf_op jit(solution)/shard_map/ppermute | solution.py:231
  90.0 2.7 %collective-permute-start.27 = (f32[128,512]{1,0:T(8,128)S(1)}, f32[128,512]{1,0:T(8,128)S(1)}, u32[]{:S(2)}, u32[]{:S(2)}) collective-permute-start(f32[128,512]{1,0:T(8,128)S(1)} %add_add_fusion.refs_4_), channel_id=1, source_target_pairs={{0,48},{16,0},{32,16},{48,32},{64,112},{80,64},{96,80},{112,96},{1... | collective-permute-start | bytes 786440 | tf_op jit(solution)/shard_map/ppermute | solution.py:231
  92.7 9.1 %factor_second.1 = (f32[512,512]{1,0:T(8,128)S(1)}, f32[512,512]{1,0:T(8,128)S(1)}, f32[32,512]{1,0:T(8,128)}, bf16[512,512]{1,0:T(8,128)(2,1)S(1)}, bf16[512,51...) custom-call(s32[17]{0:T(128)S(1)} %stack.71.place_ref, ...), custom_call_target="tpu_custom_call", output_to_operand_aliasing={{0}: (1, {}), {1}: (2, {})} | custom-call | flops 8000000000 | bytes 1048576 | tf_op jit(solution)/shard_map/factor_second/pallas_call | solution.py:212
  101.8 2.0 %collective-permute-done.28.refs_6_ = f32[128,512]{1,0:T(8,128)S(1)} collective-permute-done((f32[128,512]{1,0:T(8,128)S(1)}, f32[128,512]{1,0:T(8,128)S(1)}, u32[]{:S(2)}, u32[]{:S(2)}) %collective-permute-start.28) | collective-permute-done | bytes 262176 | tf_op jit(solution)/shard_map/ppermute | solution.py:231
  103.9 6.3 %finish.1 = (f32[512,512]{1,0:T(8,128)}, f32[2048,512]{1,0:T(8,128)}) custom-call(bf16[512,512]{1,0:T(8,128)(2,1)S(1)} %get-tuple-element.47.refs_0_, bf16[512,512]{1,0:T(8,128)(2,1)S(1)} %get-tuple-element.48.refs_1_, bf16[512,512]{1,0:T(8,128)(2,1)S(1)} %get-tuple-element.49.refs_2_, bf16[512,512]{1,0:T(8,128)(2,1)S(1)} %get-tuple-element.50.refs_3_, ...), custom_call_target="tpu_custom_call" | custom-call | flops 8000000000 | bytes 1048576 | tf_op jit(solution)/shard_map/finish/pallas_call | solution.py:421
  (34 shorter events, 0.1 us)
Async XLA Ops:
  0.6 7.2 %collective-permute-start = (f32[32,2048]{1,0:T(8,128)}, f32[32,2048]{1,0:T(8,128)S(1)}, u32[]{:S(2)}, u32[]{:S(2)}) collective-permute-start(f32[32,2048]{1,0:T(8,128)} %bitcast.20), channel_id=1, source_target_pairs={{0,1},{1,0},{2,3},{3,2},{4,5},{5,4},{6,7},{7,6},{8,9},{9,8},{10,11... | collective-permute-start | bytes 786440 | tf_op jit(solution)/shard_map/ppermute | solution.py:458
  4.0 7.5 %collective-permute-start.5 = (f32[32,2048]{1,0:T(8,128)}, f32[32,2048]{1,0:T(8,128)S(1)}, u32[]{:S(2)}, u32[]{:S(2)}) collective-permute-start(f32[32,2048]{1,0:T(8,128)} %bitcast.21), channel_id=1, source_target_pairs={{0,2},{1,15},{2,4},{3,1},{4,6},{5,3},{6,8},{7,5},{8,10},{9,7},{10,... | collective-permute-start | bytes 786440 | tf_op jit(solution)/shard_map/ppermute | solution.py:455
  7.8 6.6 %collective-permute-start.1 = (f32[32,2048]{1,0:T(8,128)S(1)}, f32[32,2048]{1,0:T(8,128)S(1)}, u32[]{:S(2)}, u32[]{:S(2)}) collective-permute-start(f32[32,2048]{1,0:T(8,128)S(1)} %collective-permute-done.refs_0_.other_ref), channel_id=1, source_target_pairs={{0,2},{1,15},{2,4},{3,1},{4,6},{5,3},{6,8},{7,5},{8,10},{9,7},{10,... | collective-permute-start | bytes 786440 | tf_op jit(solution)/shard_map/ppermute | solution.py:455
  11.4 6.3 %collective-permute-start.8 = (f32[32,2048]{1,0:T(8,128)S(1)}, f32[32,2048]{1,0:T(8,128)S(1)}, u32[]{:S(2)}, u32[]{:S(2)}) collective-permute-start(f32[32,2048]{1,0:T(8,128)S(1)} %collective-permute-done.5.refs_1_.refs_0_), channel_id=1, source_target_pairs={{0,2},{1,15},{2,4},{3,1},{4,6},{5,3},{6,8},{7,5},{8,10},{9,7},{10,... | collective-permute-start | bytes 786440 | tf_op jit(solution)/shard_map/ppermute | solution.py:455
  14.4 6.4 %collective-permute-start.2 = (f32[32,2048]{1,0:T(8,128)S(1)}, f32[32,2048]{1,0:T(8,128)S(1)}, u32[]{:S(2)}, u32[]{:S(2)}) collective-permute-start(f32[32,2048]{1,0:T(8,128)S(1)} %collective-permute-done.1.refs_2_.refs_1_), channel_id=1, source_target_pairs={{0,2},{1,15},{2,4},{3,1},{4,6},{5,3},{6,8},{7,5},{8,10},{9,7},{10,... | collective-permute-start | bytes 786440 | tf_op jit(solution)/shard_map/ppermute | solution.py:455
  17.3 6.4 %collective-permute-start.7 = (f32[32,2048]{1,0:T(8,128)S(1)}, f32[32,2048]{1,0:T(8,128)S(1)}, u32[]{:S(2)}, u32[]{:S(2)}) collective-permute-start(f32[32,2048]{1,0:T(8,128)S(1)} %collective-permute-done.5.refs_1_.refs_0_), channel_id=1, source_target_pairs={{0,1},{1,0},{2,3},{3,2},{4,5},{5,4},{6,7},{7,6},{8,9},{9,8},{10,11... | collective-permute-start | bytes 786440 | tf_op jit(solution)/shard_map/ppermute | solution.py:458
  17.8 6.4 %collective-permute-start.11 = (f32[32,2048]{1,0:T(8,128)S(1)}, f32[32,2048]{1,0:T(8,128)S(1)}, u32[]{:S(2)}, u32[]{:S(2)}) collective-permute-start(f32[32,2048]{1,0:T(8,128)S(1)} %collective-permute-done.8.refs_5_.refs_2_), channel_id=1, source_target_pairs={{0,2},{1,15},{2,4},{3,1},{4,6},{5,3},{6,8},{7,5},{8,10},{9,7},{10,... | collective-permute-start | bytes 786440 | tf_op jit(solution)/shard_map/ppermute | solution.py:455
  20.9 7.0 %collective-permute-start.10 = (f32[32,2048]{1,0:T(8,128)S(1)}, f32[32,2048]{1,0:T(8,128)S(1)}, u32[]{:S(2)}, u32[]{:S(2)}) collective-permute-start(f32[32,2048]{1,0:T(8,128)S(1)} %collective-permute-done.8.refs_5_.refs_2_), channel_id=1, source_target_pairs={{0,1},{1,0},{2,3},{3,2},{4,5},{5,4},{6,7},{7,6},{8,9},{9,8},{10,11... | collective-permute-start | bytes 786440 | tf_op jit(solution)/shard_map/ppermute | solution.py:458
  20.9 7.0 %collective-permute-start.3 = (f32[32,2048]{1,0:T(8,128)S(1)}, f32[32,2048]{1,0:T(8,128)S(1)}, u32[]{:S(2)}, u32[]{:S(2)}) collective-permute-start(f32[32,2048]{1,0:T(8,128)S(1)} %collective-permute-done.2.refs_6_.refs_3_), channel_id=1, source_target_pairs={{0,2},{1,15},{2,4},{3,1},{4,6},{5,3},{6,8},{7,5},{8,10},{9,7},{10,... | collective-permute-start | bytes 786440 | tf_op jit(solution)/shard_map/ppermute | solution.py:455
  23.7 7.0 %collective-permute-start.6 = (f32[32,2048]{1,0:T(8,128)S(1)}, f32[32,2048]{1,0:T(8,128)S(1)}, u32[]{:S(2)}, u32[]{:S(2)}) collective-permute-start(f32[32,2048]{1,0:T(8,128)S(1)} %collective-permute-done.1.refs_2_.refs_1_), channel_id=1, source_target_pairs={{0,1},{1,0},{2,3},{3,2},{4,5},{5,4},{6,7},{7,6},{8,9},{9,8},{10,11... | collective-permute-start | bytes 786440 | tf_op jit(solution)/shard_map/ppermute | solution.py:458
  23.7 7.0 %collective-permute-start.9 = (f32[32,2048]{1,0:T(8,128)S(1)}, f32[32,2048]{1,0:T(8,128)S(1)}, u32[]{:S(2)}, u32[]{:S(2)}) collective-permute-start(f32[32,2048]{1,0:T(8,128)S(1)} %collective-permute-done.2.refs_6_.refs_3_), channel_id=1, source_target_pairs={{0,1},{1,0},{2,3},{3,2},{4,5},{5,4},{6,7},{7,6},{8,9},{9,8},{10,11... | collective-permute-start | bytes 786440 | tf_op jit(solution)/shard_map/ppermute | solution.py:458
  24.2 17.0 %collective-permute-start.16 = (f32[32,2048]{1,0:T(8,128)S(1)}, f32[32,2048]{1,0:T(8,128)S(1)}, u32[]{:S(2)}, u32[]{:S(2)}) collective-permute-start(f32[32,2048]{1,0:T(8,128)S(1)} %collective-permute-done.11.refs_9_.refs_4_), channel_id=1, source_target_pairs={{0,1},{1,0},{2,3},{3,2},{4,5},{5,4},{6,7},{7,6},{8,9},{9,8},{10,11... | collective-permute-start | bytes 786440 | tf_op jit(solution)/shard_map/ppermute | solution.py:458
  27.9 7.9 %collective-permute-start.12 = (f32[32,2048]{1,0:T(8,128)S(1)}, f32[32,2048]{1,0:T(8,128)S(1)}, u32[]{:S(2)}, u32[]{:S(2)}) collective-permute-start(f32[32,2048]{1,0:T(8,128)S(1)} %collective-permute-done.11.refs_9_.refs_4_), channel_id=1, source_target_pairs={{0,2},{1,15},{2,4},{3,1},{4,6},{5,3},{6,8},{7,5},{8,10},{9,7},{10,... | collective-permute-start | bytes 786440 | tf_op jit(solution)/shard_map/ppermute | solution.py:455
  27.9 12.6 %collective-permute-start.4 = (f32[32,2048]{1,0:T(8,128)S(1)}, f32[32,2048]{1,0:T(8,128)S(1)}, u32[]{:S(2)}, u32[]{:S(2)}) collective-permute-start(f32[32,2048]{1,0:T(8,128)S(1)} %collective-permute-done.3.refs_10_.refs_5_), channel_id=1, source_target_pairs={{0,1},{1,0},{2,3},{3,2},{4,5},{5,4},{6,7},{7,6},{8,9},{9,8},{10,11... | collective-permute-start | bytes 786440 | tf_op jit(solution)/shard_map/ppermute | solution.py:458
  35.8 5.4 %collective-permute-start.17 = (f32[32,2048]{1,0:T(8,128)S(1)}, f32[32,2048]{1,0:T(8,128)S(1)}, u32[]{:S(2)}, u32[]{:S(2)}) collective-permute-start(f32[32,2048]{1,0:T(8,128)S(1)} %collective-permute-done.12.refs_6_.refs_2_), channel_id=1, source_target_pairs={{0,1},{1,0},{2,3},{3,2},{4,5},{5,4},{6,7},{7,6},{8,9},{9,8},{10,11... | collective-permute-start | bytes 786440 | tf_op jit(solution)/shard_map/ppermute | solution.py:458
  37.5 6.8 %collective-permute-start.15 = (f32[96,128]{1,0:T(8,128)S(1)}, f32[96,128]{1,0:T(8,128)S(1)}, u32[]{:S(2)}, u32[]{:S(2)}) collective-permute-start(f32[96,128]{1,0:T(8,128)S(1)} %gram_part.1), channel_id=1, source_target_pairs={{0,48},{16,0},{32,16},{48,32},{64,112},{80,64},{96,80},{112,96},{1... | collective-permute-start | bytes 147464 | tf_op jit(solution)/shard_map/ppermute | solution.py:231
  40.0 4.5 %collective-permute-start.14 = (f32[96,128]{1,0:T(8,128)S(1)}, f32[96,128]{1,0:T(8,128)S(1)}, u32[]{:S(2)}, u32[]{:S(2)}) collective-permute-start(f32[96,128]{1,0:T(8,128)S(1)} %gram_part.1), channel_id=1, source_target_pairs={{0,32},{16,48},{32,0},{48,16},{64,96},{80,112},{96,64},{112,80},{1... | collective-permute-start | bytes 147464 | tf_op jit(solution)/shard_map/ppermute | solution.py:231
  40.5 4.5 %collective-permute-start.13 = (f32[96,128]{1,0:T(8,128)S(1)}, f32[96,128]{1,0:T(8,128)S(1)}, u32[]{:S(2)}, u32[]{:S(2)}) collective-permute-start(f32[96,128]{1,0:T(8,128)S(1)} %gram_part.1), channel_id=1, source_target_pairs={{0,16},{16,32},{32,48},{48,0},{64,80},{80,96},{96,112},{112,64},{1... | collective-permute-start | bytes 147464 | tf_op jit(solution)/shard_map/ppermute | solution.py:231
  45.0 6.5 %collective-permute-start.20 = (f32[96,128]{1,0:T(8,128)S(1)}, f32[96,128]{1,0:T(8,128)S(1)}, u32[]{:S(2)}, u32[]{:S(2)}) collective-permute-start(f32[96,128]{1,0:T(8,128)S(1)} %add_add_fusion.3), channel_id=1, source_target_pairs={{0,192},{16,208},{32,224},{48,240},{64,0},{80,16},{96,32},{112,48}... | collective-permute-start | bytes 147464 | tf_op jit(solution)/shard_map/ppermute | solution.py:231
  47.8 4.8 %collective-permute-start.19 = (f32[96,128]{1,0:T(8,128)S(1)}, f32[96,128]{1,0:T(8,128)S(1)}, u32[]{:S(2)}, u32[]{:S(2)}) collective-permute-start(f32[96,128]{1,0:T(8,128)S(1)} %add_add_fusion.3), channel_id=1, source_target_pairs={{0,128},{16,144},{32,160},{48,176},{64,192},{80,208},{96,224},{112... | collective-permute-start | bytes 147464 | tf_op jit(solution)/shard_map/ppermute | solution.py:231
  48.2 4.6 %collective-permute-start.18 = (f32[96,128]{1,0:T(8,128)S(1)}, f32[96,128]{1,0:T(8,128)S(1)}, u32[]{:S(2)}, u32[]{:S(2)}) collective-permute-start(f32[96,128]{1,0:T(8,128)S(1)} %add_add_fusion.3), channel_id=1, source_target_pairs={{0,64},{16,80},{32,96},{48,112},{64,128},{80,144},{96,160},{112,17... | collective-permute-start | bytes 147464 | tf_op jit(solution)/shard_map/ppermute | solution.py:231
  49.0 23.7 %collective-permute-start.21 = (f32[128,512]{1,0:T(8,128)S(1)}, f32[128,512]{1,0:T(8,128)S(1)}, u32[]{:S(2)}, u32[]{:S(2)}) collective-permute-start(f32[128,512]{1,0:T(8,128)S(1)} %get-tuple-element.52), channel_id=1, source_target_pairs={{0,16},{16,32},{32,48},{48,0},{64,80},{80,96},{96,112},{112,64},{1... | collective-permute-start | bytes 786440 | tf_op jit(solution)/shard_map/ppermute | solution.py:479
  49.8 22.9 %collective-permute-start.22 = (f32[128,512]{1,0:T(8,128)S(1)}, f32[128,512]{1,0:T(8,128)S(1)}, u32[]{:S(2)}, u32[]{:S(2)}) collective-permute-start(f32[128,512]{1,0:T(8,128)S(1)} %get-tuple-element.53), channel_id=1, source_target_pairs={{0,32},{16,48},{32,0},{48,16},{64,96},{80,112},{96,64},{112,80},{1... | collective-permute-start | bytes 786440 | tf_op jit(solution)/shard_map/ppermute | solution.py:479
  51.6 21.2 %collective-permute-start.23 = (f32[128,512]{1,0:T(8,128)S(1)}, f32[128,512]{1,0:T(8,128)S(1)}, u32[]{:S(2)}, u32[]{:S(2)}) collective-permute-start(f32[128,512]{1,0:T(8,128)S(1)} %get-tuple-element.54), channel_id=1, source_target_pairs={{0,48},{16,0},{32,16},{48,32},{64,112},{80,64},{96,80},{112,96},{1... | collective-permute-start | bytes 786440 | tf_op jit(solution)/shard_map/ppermute | solution.py:479
  72.8 13.7 %collective-permute-start.26 = (f32[128,512]{1,0:T(8,128)S(1)}, f32[128,512]{1,0:T(8,128)S(1)}, u32[]{:S(2)}, u32[]{:S(2)}) collective-permute-start(f32[128,512]{1,0:T(8,128)S(1)} %add_add_fusion.1), channel_id=1, source_target_pairs={{0,128},{16,144},{32,160},{48,176},{64,192},{80,208},{96,224},{112... | collective-permute-start | bytes 786440 | tf_op jit(solution)/shard_map/ppermute | solution.py:231
  74.4 13.9 %collective-permute-start.25 = (f32[128,512]{1,0:T(8,128)S(1)}, f32[128,512]{1,0:T(8,128)S(1)}, u32[]{:S(2)}, u32[]{:S(2)}) collective-permute-start(f32[128,512]{1,0:T(8,128)S(1)} %add_add_fusion.1), channel_id=1, source_target_pairs={{0,64},{16,80},{32,96},{48,112},{64,128},{80,144},{96,160},{112,17... | collective-permute-start | bytes 786440 | tf_op jit(solution)/shard_map/ppermute | solution.py:231
  75.3 13.0 %collective-permute-start.24 = (f32[128,512]{1,0:T(8,128)S(1)}, f32[128,512]{1,0:T(8,128)S(1)}, u32[]{:S(2)}, u32[]{:S(2)}) collective-permute-start(f32[128,512]{1,0:T(8,128)S(1)} %add_add_fusion.1), channel_id=1, source_target_pairs={{0,192},{16,208},{32,224},{48,240},{64,0},{80,16},{96,32},{112,48}... | collective-permute-start | bytes 786440 | tf_op jit(solution)/shard_map/ppermute | solution.py:231
  88.4 13.4 %collective-permute-start.29 = (f32[128,512]{1,0:T(8,128)S(1)}, f32[128,512]{1,0:T(8,128)S(1)}, u32[]{:S(2)}, u32[]{:S(2)}) collective-permute-start(f32[128,512]{1,0:T(8,128)S(1)} %add_add_fusion.refs_4_), channel_id=1, source_target_pairs={{0,32},{16,48},{32,0},{48,16},{64,96},{80,112},{96,64},{112,80},{1... | collective-permute-start | bytes 786440 | tf_op jit(solution)/shard_map/ppermute | solution.py:231
  90.0 13.8 %collective-permute-start.28 = (f32[128,512]{1,0:T(8,128)S(1)}, f32[128,512]{1,0:T(8,128)S(1)}, u32[]{:S(2)}, u32[]{:S(2)}) collective-permute-start(f32[128,512]{1,0:T(8,128)S(1)} %add_add_fusion.refs_4_), channel_id=1, source_target_pairs={{0,16},{16,32},{32,48},{48,0},{64,80},{80,96},{96,112},{112,64},{1... | collective-permute-start | bytes 786440 | tf_op jit(solution)/shard_map/ppermute | solution.py:231
  90.0 13.8 %collective-permute-start.27 = (f32[128,512]{1,0:T(8,128)S(1)}, f32[128,512]{1,0:T(8,128)S(1)}, u32[]{:S(2)}, u32[]{:S(2)}) collective-permute-start(f32[128,512]{1,0:T(8,128)S(1)} %add_add_fusion.refs_4_), channel_id=1, source_target_pairs={{0,48},{16,0},{32,16},{48,32},{64,112},{80,64},{96,80},{112,96},{1... | collective-permute-start | bytes 786440 | tf_op jit(solution)/shard_map/ppermute | solution.py:231
  92.7 11.1 %copy-start = (f32[2048,512]{1,0:T(8,128)S(1)}, f32[2048,512]{1,0:T(8,128)}, u32[]{:S(2)}) copy-start(f32[2048,512]{1,0:T(8,128)} %refs_12_.1) | copy-start | bytes 12582916
  92.7 11.1 %copy-start.1 = (bf16[2048,384]{1,0:T(8,128)(2,1)S(1)}, bf16[2048,384]{1,0:T(8,128)(2,1)}, u32[]{:S(2)}) copy-start(bf16[2048,384]{1,0:T(8,128)(2,1)} %get-tuple-element.55.refs_8_) | copy-start | bytes 4718596
  92.7 11.1 %copy-start.2 = (bf16[2048,384]{1,0:T(8,128)(2,1)S(1)}, bf16[2048,384]{1,0:T(8,128)(2,1)}, u32[]{:S(2)}) copy-start(bf16[2048,384]{1,0:T(8,128)(2,1)} %get-tuple-element.57.refs_10_) | copy-start | bytes 4718596
  92.7 11.1 %copy-start.3 = (bf16[2048,128]{1,0:T(8,128)(2,1)S(1)}, bf16[2048,128]{1,0:T(8,128)(2,1)}, u32[]{:S(2)}) copy-start(bf16[2048,128]{1,0:T(8,128)(2,1)} %get-tuple-element.56.refs_9_) | copy-start | bytes 1572868
  92.7 11.1 %copy-start.4 = (bf16[2048,128]{1,0:T(8,128)(2,1)S(1)}, bf16[2048,128]{1,0:T(8,128)(2,1)}, u32[]{:S(2)}) copy-start(bf16[2048,128]{1,0:T(8,128)(2,1)} %get-tuple-element.58.refs_11_) | copy-start | bytes 1572868

commit v6 on v5

--- a/solution.py
+++ b/solution.py
@@ -464,15 +464,15 @@
         second.append(send(second[-1]))
         blocks += [first[s], second[s], exchange(second[s]), exchange(first[s])]
     first.append(send(first[-1]))
-    early = blocks[: 4 * far - 4]
+    early = blocks[: 2 * far]
     mixed, near, high, low = mix(early, trailing, 512)
     first[far], mixed = lax.optimization_barrier((first[far], mixed))
 
     received = [first[s] if core == 0 else second[s] for s in range(1, far) for core in range(2)] + [first[far]]
     part = gram_part(near, second[0], received)
     pieces = sent_along(part, False, STEPS)
-    late = blocks[4 * far - 4 :] + [first[far], exchange(first[far])]
-    late[0], part = lax.optimization_barrier((late[0], part))
+    last, part = lax.optimization_barrier((first[far], part))
+    late = blocks[2 * far :] + [last, exchange(last)]
     *quarters, late_high, late_low = mix_last(mixed, late, trailing, 512)
     *pieces, quarters[0] = lax.optimization_barrier((*pieces, quarters[0]))
     part = sum(pieces, part)

time: 110 us -> 110 us (level)
    ppermute x7, starting transfers between devices: 16.9 us -> 14.8 us  [send(): return lax.ppermute(value, 'col', ring)]
    ppermute x7, waiting for transfers between devices: 2.78 us -> 4.45 us  [send(): return lax.ppermute(value, 'col', ring)]
    ppermute x8, starting transfers between devices: 10.6 us -> 11.7 us  [exchange(): return lax.ppermute(value, 'col', swap)]
where the time goes in v6:
time: 110 us
  starting transfers between devices  46.4 us (42%)
  Pallas kernels  34 us (31%)
  blocking collectives  19.6 us (18%)
  waiting for transfers between devices  8.49 us (8%)
    all_gather x1, blocking collectives, on_device(): parts = lax.all_gather(part, 'col', axis=0, tiled=True)  19.6 us
    ppermute x12, starting transfers between devices, sent_along(): lax.ppermute(value, 'row', shifted(k, 0) if along_y else shifted(0, k))  16 us
    ppermute x7, starting transfers between devices, send(): return lax.ppermute(value, 'col', ring)  14.8 us
    ppermute x8, starting transfers between devices, exchange(): return lax.ppermute(value, 'col', swap)  11.7 us
    pallas_call x1, Pallas kernels, factor_first(): pl.pallas_call(functools.partial(first_kernel, steps), out_shape=[jax.Sha...  9.45 us
    pallas_call x1, Pallas kernels, factor_second(): pl.pallas_call(functools.partial(second_kernel, begin), out_shape=[whole,...  9.06 us
    pallas_call x1, Pallas kernels, finish(): pl.pallas_call(functools.partial(last_kernel, tile), out_shape=[jax.Shape...  6.26 us
    ppermute x7, waiting for transfers between devices, send(): return lax.ppermute(value, 'col', ring)  4.45 us
  transfers between devices with their start and end apart: 30, of which 7 were waited for; matrix products, arithmetic and copies ran while one was open for 0% of the time, Pallas kernels for 25%

profile of v6, /device:TPU:1, one launch (start us, length us, event | category | flops | bytes accessed | tf_op | source)
XLA Modules:
  0.0 109.8 jit_solution(189421120254803044)
XLA Ops:
  0.6 3.3 %collective-permute-start.4 = (f32[32,2048]{1,0:T(8,128)}, f32[32,2048]{1,0:T(8,128)S(1)}, u32[]{:S(2)}, u32[]{:S(2)}) collective-permute-start(f32[32,2048]{1,0:T(8,128)} %bitcast.20), channel_id=1, source_target_pairs={{0,1},{1,0},{2,3},{3,2},{4,5},{5,4},{6,7},{7,6},{8,9},{9,8},{10,11... | collective-permute-start | bytes 786440 | tf_op jit(solution)/shard_map/ppermute | solution.py:458
  4.0 3.8 %collective-permute-start = (f32[32,2048]{1,0:T(8,128)}, f32[32,2048]{1,0:T(8,128)S(1)}, u32[]{:S(2)}, u32[]{:S(2)}) collective-permute-start(f32[32,2048]{1,0:T(8,128)} %bitcast.21), channel_id=1, source_target_pairs={{0,2},{1,15},{2,4},{3,1},{4,6},{5,3},{6,8},{7,5},{8,10},{9,7},{10,... | collective-permute-start | bytes 786440 | tf_op jit(solution)/shard_map/ppermute | solution.py:455
  7.8 0.0 collective-permute-done.4.refs_0_.other_ref
  7.8 1.4 %collective-permute-start.5 = (f32[32,2048]{1,0:T(8,128)S(1)}, f32[32,2048]{1,0:T(8,128)S(1)}, u32[]{:S(2)}, u32[]{:S(2)}) collective-permute-start(f32[32,2048]{1,0:T(8,128)S(1)} %collective-permute-done.4.refs_0_.other_ref), channel_id=1, source_target_pairs={{0,2},{1,15},{2,4},{3,1},{4,6},{5,3},{6,8},{7,5},{8,10},{9,7},{10,... | collective-permute-start | bytes 786440 | tf_op jit(solution)/shard_map/ppermute | solution.py:455
  9.2 2.3 %collective-permute-done.refs_1_.refs_0_ = f32[32,2048]{1,0:T(8,128)S(1)} collective-permute-done((f32[32,2048]{1,0:T(8,128)}, f32[32,2048]{1,0:T(8,128)S(1)}, u32[]{:S(2)}, u32[]{:S(2)}) %collective-permute-start) | collective-permute-done | bytes 262176 | tf_op jit(solution)/shard_map/ppermute | solution.py:455
  11.4 3.0 %collective-permute-start.1 = (f32[32,2048]{1,0:T(8,128)S(1)}, f32[32,2048]{1,0:T(8,128)S(1)}, u32[]{:S(2)}, u32[]{:S(2)}) collective-permute-start(f32[32,2048]{1,0:T(8,128)S(1)} %collective-permute-done.refs_1_.refs_0_), channel_id=1, source_target_pairs={{0,2},{1,15},{2,4},{3,1},{4,6},{5,3},{6,8},{7,5},{8,10},{9,7},{10,... | collective-permute-start | bytes 786440 | tf_op jit(solution)/shard_map/ppermute | solution.py:455
  14.4 2.8 %collective-permute-start.8 = (f32[32,2048]{1,0:T(8,128)S(1)}, f32[32,2048]{1,0:T(8,128)S(1)}, u32[]{:S(2)}, u32[]{:S(2)}) collective-permute-start(f32[32,2048]{1,0:T(8,128)S(1)} %collective-permute-done.5.refs_2_.refs_1_), channel_id=1, source_target_pairs={{0,2},{1,15},{2,4},{3,1},{4,6},{5,3},{6,8},{7,5},{8,10},{9,7},{10,... | collective-permute-start | bytes 786440 | tf_op jit(solution)/shard_map/ppermute | solution.py:455
  17.3 0.5 collective-permute-done.1.refs_5_.refs_2_
  17.8 3.1 %collective-permute-start.2 = (f32[32,2048]{1,0:T(8,128)S(1)}, f32[32,2048]{1,0:T(8,128)S(1)}, u32[]{:S(2)}, u32[]{:S(2)}) collective-permute-start(f32[32,2048]{1,0:T(8,128)S(1)} %collective-permute-done.1.refs_5_.refs_2_), channel_id=1, source_target_pairs={{0,2},{1,15},{2,4},{3,1},{4,6},{5,3},{6,8},{7,5},{8,10},{9,7},{10,... | collective-permute-start | bytes 786440 | tf_op jit(solution)/shard_map/ppermute | solution.py:455
  20.9 0.5 collective-permute-start.14
  21.4 0.0 collective-permute-done.8.refs_6_.refs_3_
  21.4 1.7 %collective-permute-start.13 = (f32[32,2048]{1,0:T(8,128)S(1)}, f32[32,2048]{1,0:T(8,128)S(1)}, u32[]{:S(2)}, u32[]{:S(2)}) collective-permute-start(f32[32,2048]{1,0:T(8,128)S(1)} %collective-permute-done.8.refs_6_.refs_3_), channel_id=1, source_target_pairs={{0,1},{1,0},{2,3},{3,2},{4,5},{5,4},{6,7},{7,6},{8,9},{9,8},{10,11... | collective-permute-start | bytes 786440 | tf_op jit(solution)/shard_map/ppermute | solution.py:458
  23.1 0.0 collective-permute-done.7.refs_4_
  23.1 0.7 collective-permute-start.9
  23.8 0.4 collective-permute-done.2.refs_4_.refs_2_
  24.2 3.7 %collective-permute-start.16 = (f32[32,2048]{1,0:T(8,128)S(1)}, f32[32,2048]{1,0:T(8,128)S(1)}, u32[]{:S(2)}, u32[]{:S(2)}) collective-permute-start(f32[32,2048]{1,0:T(8,128)S(1)} %collective-permute-done.2.refs_4_.refs_2_), channel_id=1, source_target_pairs={{0,1},{1,0},{2,3},{3,2},{4,5},{5,4},{6,7},{7,6},{8,9},{9,8},{10,11... | collective-permute-start | bytes 786440 | tf_op jit(solution)/shard_map/ppermute | solution.py:458
  27.9 4.2 %mixed.1 = (f32[256,512]{1,0:T(8,128)}, f32[32,2048]{1,0:T(8,128)S(1)}, bf16[2048,256]{1,0:T(8,128)(2,1)}, bf16[2048,256]{1,0:T(8,128)(2,1)}) custom-call(f32[32,2048]{1,0:T(8,128)} %bitcast.22, f32[32,2048]{1,0:T(8,128)S(1)} %collective-permute-done.4.refs_0_.other_ref, f32[32,2048]{1,0:T(8,128)S(1)} %collective-permute-done.refs_1_.refs_0_, ...), custom_call_target="tpu_custom_call" | custom-call | flops 3000000000 | bytes 1048576 | tf_op jit(solution)/shard_map/mixed/pallas_call | solution.py:356
  32.1 1.3 %collective-permute-done.3.refs_6_ = f32[32,2048]{1,0:T(8,128)S(1)} collective-permute-done((f32[32,2048]{1,0:T(8,128)S(1)}, f32[32,2048]{1,0:T(8,128)S(1)}, u32[]{:S(2)}, u32[]{:S(2)}) %collective-permute-start.3) | collective-permute-done | bytes 262176 | tf_op jit(solution)/shard_map/ppermute | solution.py:455
  33.4 1.4 %gram_part.1 = f32[96,128]{1,0:T(8,128)S(1)} custom-call(s32[1]{0:T(128)} %bitcast.18.core_ref, f32[32,2048]{1,0:T(8,128)S(1)} %get-tuple-element.34.own_ref, f32[32,2048]{1,0:T(8,128)S(1)} %collective-permute-done.4.refs_0_.other_ref, f32[32,2048]{1,0:T(8,128)S(1)} %collective-permute-done.refs_1_.refs_0_, ...), custom_call_target="tpu_custom_call" | custom-call | flops 2000000000 | bytes 1048576 | tf_op jit(solution)/shard_map/gram_part/pallas_call | solution.py:269
  34.8 2.3 %collective-permute-start.15 = (f32[32,2048]{1,0:T(8,128)S(1)}, f32[32,2048]{1,0:T(8,128)S(1)}, u32[]{:S(2)}, u32[]{:S(2)}) collective-permute-start(f32[32,2048]{1,0:T(8,128)S(1)} %collective-permute-done.9.refs_5_.refs_3_), channel_id=1, source_target_pairs={{0,1},{1,0},{2,3},{3,2},{4,5},{5,4},{6,7},{7,6},{8,9},{9,8},{10,11... | collective-permute-start | bytes 786440 | tf_op jit(solution)/shard_map/ppermute | solution.py:458
  37.1 0.1 collective-permute-start.17
  37.2 2.5 %collective-permute-start.12 = (f32[96,128]{1,0:T(8,128)S(1)}, f32[96,128]{1,0:T(8,128)S(1)}, u32[]{:S(2)}, u32[]{:S(2)}) collective-permute-start(f32[96,128]{1,0:T(8,128)S(1)} %gram_part.1), channel_id=1, source_target_pairs={{0,48},{16,0},{32,16},{48,32},{64,112},{80,64},{96,80},{112,96},{1... | collective-permute-start | bytes 147464 | tf_op jit(solution)/shard_map/ppermute | solution.py:231
  39.7 0.5 collective-permute-start.11
  40.2 0.6 collective-permute-start.10
  40.9 3.6 %mixed_last.1 = (f32[128,512]{1,0:T(8,128)S(1)}, f32[128,512]{1,0:T(8,128)S(1)}, f32[128,512]{1,0:T(8,128)S(1)}, f32[128,512]{1,0:T(8,128)S(1)}, bf16[2048,256]{1,0:T(8,128)(2,1)}, /*index=5*/bf16[2048,256]{1,0:T(8,128)(2,1)}) custom-call(s32[1]{0:T(128)} %bitcast.16.place_ref, f32[256,512]{1,0:T(8,128)} %get-tuple-element.36.done_ref, ...), custom_call_target="tpu_custom_call" | custom-call | flops 3000000000 | bytes 1048576 | tf_op jit(solution)/shard_map/mixed_last/pallas_call | solution.py:377
  44.5 0.2 collective-permute-done.10
  44.7 2.8 %collective-permute-start.20 = (f32[96,128]{1,0:T(8,128)S(1)}, f32[96,128]{1,0:T(8,128)S(1)}, u32[]{:S(2)}, u32[]{:S(2)}) collective-permute-start(f32[96,128]{1,0:T(8,128)S(1)} %add_add_fusion.3), channel_id=1, source_target_pairs={{0,192},{16,208},{32,224},{48,240},{64,0},{80,16},{96,32},{112,48}... | collective-permute-start | bytes 147464 | tf_op jit(solution)/shard_map/ppermute | solution.py:231
  47.5 0.3 collective-permute-start.19
  47.9 0.7 collective-permute-start.18
  48.6 0.1 stack.71.place_ref
  48.7 1.4 %collective-permute-start.21 = (f32[128,512]{1,0:T(8,128)S(1)}, f32[128,512]{1,0:T(8,128)S(1)}, u32[]{:S(2)}, u32[]{:S(2)}) collective-permute-start(f32[128,512]{1,0:T(8,128)S(1)} %get-tuple-element.52), channel_id=1, source_target_pairs={{0,16},{16,32},{32,48},{48,0},{64,80},{80,96},{96,112},{112,64},{1... | collective-permute-start | bytes 786440 | tf_op jit(solution)/shard_map/ppermute | solution.py:479
  50.1 1.7 %collective-permute-start.22 = (f32[128,512]{1,0:T(8,128)S(1)}, f32[128,512]{1,0:T(8,128)S(1)}, u32[]{:S(2)}, u32[]{:S(2)}) collective-permute-start(f32[128,512]{1,0:T(8,128)S(1)} %get-tuple-element.53), channel_id=1, source_target_pairs={{0,32},{16,48},{32,0},{48,16},{64,96},{80,112},{96,64},{112,80},{1... | collective-permute-start | bytes 786440 | tf_op jit(solution)/shard_map/ppermute | solution.py:479
  51.8 0.8 collective-permute-start.23
  52.6 19.6 %all_gather.3.part_ref = f32[1536,128]{1,0:T(8,128)S(1)} all-gather(f32[96,128]{1,0:T(8,128)S(1)} %add_add_fusion.2), channel_id=1, replica_groups=mesh['row'=16,'col'=16] {'col'}, dimensions={0}, use_global_device_ids=true | all-gather | bytes 835584 | tf_op jit(solution)/shard_map/all_gather | solution.py:483
  72.3 0.1 add_add_fusion.1
  72.4 1.5 %collective-permute-start.26 = (f32[128,512]{1,0:T(8,128)S(1)}, f32[128,512]{1,0:T(8,128)S(1)}, u32[]{:S(2)}, u32[]{:S(2)}) collective-permute-start(f32[128,512]{1,0:T(8,128)S(1)} %add_add_fusion.1), channel_id=1, source_target_pairs={{0,128},{16,144},{32,160},{48,176},{64,192},{80,208},{96,224},{112... | collective-permute-start | bytes 786440 | tf_op jit(solution)/shard_map/ppermute | solution.py:231
  73.9 0.9 collective-permute-start.25
  74.8 1.8 %collective-permute-start.24 = (f32[128,512]{1,0:T(8,128)S(1)}, f32[128,512]{1,0:T(8,128)S(1)}, u32[]{:S(2)}, u32[]{:S(2)}) collective-permute-start(f32[128,512]{1,0:T(8,128)S(1)} %add_add_fusion.1), channel_id=1, source_target_pairs={{0,192},{16,208},{32,224},{48,240},{64,0},{80,16},{96,32},{112,48}... | collective-permute-start | bytes 786440 | tf_op jit(solution)/shard_map/ppermute | solution.py:231
  76.6 9.5 %factor_first.1 = (f32[512,512]{1,0:T(8,128)S(1)}, f32[512,512]{1,0:T(8,128)S(1)}) custom-call(f32[1536,128]{1,0:T(8,128)S(1)} %all_gather.3.part_ref), custom_call_target="tpu_custom_call" | custom-call | flops 10000000000 | bytes 1048576 | tf_op jit(solution)/shard_map/factor_first/pallas_call | solution.py:198
  86.0 1.8 %collective-permute-done.25 = f32[128,512]{1,0:T(8,128)S(1)} collective-permute-done((f32[128,512]{1,0:T(8,128)S(1)}, f32[128,512]{1,0:T(8,128)S(1)}, u32[]{:S(2)}, u32[]{:S(2)}) %collective-permute-start.25) | collective-permute-done | bytes 262176 | tf_op jit(solution)/shard_map/ppermute | solution.py:231
  87.8 0.1 add_add_fusion.refs_4_
  87.9 1.6 %collective-permute-start.29 = (f32[128,512]{1,0:T(8,128)S(1)}, f32[128,512]{1,0:T(8,128)S(1)}, u32[]{:S(2)}, u32[]{:S(2)}) collective-permute-start(f32[128,512]{1,0:T(8,128)S(1)} %add_add_fusion.refs_4_), channel_id=1, source_target_pairs={{0,32},{16,48},{32,0},{48,16},{64,96},{80,112},{96,64},{112,80},{1... | collective-permute-start | bytes 786440 | tf_op jit(solution)/shard_map/ppermute | solution.py:231
  89.5 0.3 collective-permute-start.28
  89.9 2.3 %collective-permute-start.27 = (f32[128,512]{1,0:T(8,128)S(1)}, f32[128,512]{1,0:T(8,128)S(1)}, u32[]{:S(2)}, u32[]{:S(2)}) collective-permute-start(f32[128,512]{1,0:T(8,128)S(1)} %add_add_fusion.refs_4_), channel_id=1, source_target_pairs={{0,48},{16,0},{32,16},{48,32},{64,112},{80,64},{96,80},{112,96},{1... | collective-permute-start | bytes 786440 | tf_op jit(solution)/shard_map/ppermute | solution.py:231
  92.2 0.0 copy-start.4
  92.2 9.1 %factor_second.1 = (f32[512,512]{1,0:T(8,128)S(1)}, f32[512,512]{1,0:T(8,128)S(1)}, f32[32,512]{1,0:T(8,128)}, bf16[512,512]{1,0:T(8,128)(2,1)S(1)}, bf16[512,51...) custom-call(s32[17]{0:T(128)S(1)} %stack.71.place_ref, ...), custom_call_target="tpu_custom_call", output_to_operand_aliasing={{0}: (1, {}), {1}: (2, {})} | custom-call | flops 8000000000 | bytes 1048576 | tf_op jit(solution)/shard_map/factor_second/pallas_call | solution.py:212
  101.3 2.0 %collective-permute-done.28.refs_6_ = f32[128,512]{1,0:T(8,128)S(1)} collective-permute-done((f32[128,512]{1,0:T(8,128)S(1)}, f32[128,512]{1,0:T(8,128)S(1)}, u32[]{:S(2)}, u32[]{:S(2)}) %collective-permute-start.28) | collective-permute-done | bytes 262176 | tf_op jit(solution)/shard_map/ppermute | solution.py:231
  103.4 6.3 %finish.1 = (f32[512,512]{1,0:T(8,128)}, f32[2048,512]{1,0:T(8,128)}) custom-call(bf16[512,512]{1,0:T(8,128)(2,1)S(1)} %get-tuple-element.47.refs_0_, bf16[512,512]{1,0:T(8,128)(2,1)S(1)} %get-tuple-element.48.refs_1_, bf16[512,512]{1,0:T(8,128)(2,1)S(1)} %get-tuple-element.49.refs_2_, bf16[512,512]{1,0:T(8,128)(2,1)S(1)} %get-tuple-element.50.refs_3_, ...), custom_call_target="tpu_custom_call" | custom-call | flops 8000000000 | bytes 1048576 | tf_op jit(solution)/shard_map/finish/pallas_call | solution.py:421
  (34 shorter events, 0.1 us)
Async XLA Ops:
  0.6 7.2 %collective-permute-start.4 = (f32[32,2048]{1,0:T(8,128)}, f32[32,2048]{1,0:T(8,128)S(1)}, u32[]{:S(2)}, u32[]{:S(2)}) collective-permute-start(f32[32,2048]{1,0:T(8,128)} %bitcast.20), channel_id=1, source_target_pairs={{0,1},{1,0},{2,3},{3,2},{4,5},{5,4},{6,7},{7,6},{8,9},{9,8},{10,11... | collective-permute-start | bytes 786440 | tf_op jit(solution)/shard_map/ppermute | solution.py:458
  4.0 7.5 %collective-permute-start = (f32[32,2048]{1,0:T(8,128)}, f32[32,2048]{1,0:T(8,128)S(1)}, u32[]{:S(2)}, u32[]{:S(2)}) collective-permute-start(f32[32,2048]{1,0:T(8,128)} %bitcast.21), channel_id=1, source_target_pairs={{0,2},{1,15},{2,4},{3,1},{4,6},{5,3},{6,8},{7,5},{8,10},{9,7},{10,... | collective-permute-start | bytes 786440 | tf_op jit(solution)/shard_map/ppermute | solution.py:455
  7.8 6.6 %collective-permute-start.5 = (f32[32,2048]{1,0:T(8,128)S(1)}, f32[32,2048]{1,0:T(8,128)S(1)}, u32[]{:S(2)}, u32[]{:S(2)}) collective-permute-start(f32[32,2048]{1,0:T(8,128)S(1)} %collective-permute-done.4.refs_0_.other_ref), channel_id=1, source_target_pairs={{0,2},{1,15},{2,4},{3,1},{4,6},{5,3},{6,8},{7,5},{8,10},{9,7},{10,... | collective-permute-start | bytes 786440 | tf_op jit(solution)/shard_map/ppermute | solution.py:455
  11.4 6.3 %collective-permute-start.1 = (f32[32,2048]{1,0:T(8,128)S(1)}, f32[32,2048]{1,0:T(8,128)S(1)}, u32[]{:S(2)}, u32[]{:S(2)}) collective-permute-start(f32[32,2048]{1,0:T(8,128)S(1)} %collective-permute-done.refs_1_.refs_0_), channel_id=1, source_target_pairs={{0,2},{1,15},{2,4},{3,1},{4,6},{5,3},{6,8},{7,5},{8,10},{9,7},{10,... | collective-permute-start | bytes 786440 | tf_op jit(solution)/shard_map/ppermute | solution.py:455
  14.4 6.9 %collective-permute-start.8 = (f32[32,2048]{1,0:T(8,128)S(1)}, f32[32,2048]{1,0:T(8,128)S(1)}, u32[]{:S(2)}, u32[]{:S(2)}) collective-permute-start(f32[32,2048]{1,0:T(8,128)S(1)} %collective-permute-done.5.refs_2_.refs_1_), channel_id=1, source_target_pairs={{0,2},{1,15},{2,4},{3,1},{4,6},{5,3},{6,8},{7,5},{8,10},{9,7},{10,... | collective-permute-start | bytes 786440 | tf_op jit(solution)/shard_map/ppermute | solution.py:455
  17.3 5.9 %collective-permute-start.7 = (f32[32,2048]{1,0:T(8,128)S(1)}, f32[32,2048]{1,0:T(8,128)S(1)}, u32[]{:S(2)}, u32[]{:S(2)}) collective-permute-start(f32[32,2048]{1,0:T(8,128)S(1)} %collective-permute-done.refs_1_.refs_0_), channel_id=1, source_target_pairs={{0,1},{1,0},{2,3},{3,2},{4,5},{5,4},{6,7},{7,6},{8,9},{9,8},{10,11... | collective-permute-start | bytes 786440 | tf_op jit(solution)/shard_map/ppermute | solution.py:458
  17.8 6.4 %collective-permute-start.2 = (f32[32,2048]{1,0:T(8,128)S(1)}, f32[32,2048]{1,0:T(8,128)S(1)}, u32[]{:S(2)}, u32[]{:S(2)}) collective-permute-start(f32[32,2048]{1,0:T(8,128)S(1)} %collective-permute-done.1.refs_5_.refs_2_), channel_id=1, source_target_pairs={{0,2},{1,15},{2,4},{3,1},{4,6},{5,3},{6,8},{7,5},{8,10},{9,7},{10,... | collective-permute-start | bytes 786440 | tf_op jit(solution)/shard_map/ppermute | solution.py:455
  20.9 7.0 %collective-permute-start.6 = (f32[32,2048]{1,0:T(8,128)S(1)}, f32[32,2048]{1,0:T(8,128)S(1)}, u32[]{:S(2)}, u32[]{:S(2)}) collective-permute-start(f32[32,2048]{1,0:T(8,128)S(1)} %collective-permute-done.5.refs_2_.refs_1_), channel_id=1, source_target_pairs={{0,1},{1,0},{2,3},{3,2},{4,5},{5,4},{6,7},{7,6},{8,9},{9,8},{10,11... | collective-permute-start | bytes 786440 | tf_op jit(solution)/shard_map/ppermute | solution.py:458
  20.9 16.4 %collective-permute-start.14 = (f32[32,2048]{1,0:T(8,128)S(1)}, f32[32,2048]{1,0:T(8,128)S(1)}, u32[]{:S(2)}, u32[]{:S(2)}) collective-permute-start(f32[32,2048]{1,0:T(8,128)S(1)} %collective-permute-done.1.refs_5_.refs_2_), channel_id=1, source_target_pairs={{0,1},{1,0},{2,3},{3,2},{4,5},{5,4},{6,7},{7,6},{8,9},{9,8},{10,11... | collective-permute-start | bytes 786440 | tf_op jit(solution)/shard_map/ppermute | solution.py:458
  21.4 18.3 %collective-permute-start.13 = (f32[32,2048]{1,0:T(8,128)S(1)}, f32[32,2048]{1,0:T(8,128)S(1)}, u32[]{:S(2)}, u32[]{:S(2)}) collective-permute-start(f32[32,2048]{1,0:T(8,128)S(1)} %collective-permute-done.8.refs_6_.refs_3_), channel_id=1, source_target_pairs={{0,1},{1,0},{2,3},{3,2},{4,5},{5,4},{6,7},{7,6},{8,9},{9,8},{10,11... | collective-permute-start | bytes 786440 | tf_op jit(solution)/shard_map/ppermute | solution.py:458
  23.1 10.3 %collective-permute-start.9 = (f32[32,2048]{1,0:T(8,128)S(1)}, f32[32,2048]{1,0:T(8,128)S(1)}, u32[]{:S(2)}, u32[]{:S(2)}) collective-permute-start(f32[32,2048]{1,0:T(8,128)S(1)} %collective-permute-done.8.refs_6_.refs_3_), channel_id=1, source_target_pairs={{0,2},{1,15},{2,4},{3,1},{4,6},{5,3},{6,8},{7,5},{8,10},{9,7},{10,... | collective-permute-start | bytes 786440 | tf_op jit(solution)/shard_map/ppermute | solution.py:455
  24.2 16.0 %collective-permute-start.16 = (f32[32,2048]{1,0:T(8,128)S(1)}, f32[32,2048]{1,0:T(8,128)S(1)}, u32[]{:S(2)}, u32[]{:S(2)}) collective-permute-start(f32[32,2048]{1,0:T(8,128)S(1)} %collective-permute-done.2.refs_4_.refs_2_), channel_id=1, source_target_pairs={{0,1},{1,0},{2,3},{3,2},{4,5},{5,4},{6,7},{7,6},{8,9},{9,8},{10,11... | collective-permute-start | bytes 786440 | tf_op jit(solution)/shard_map/ppermute | solution.py:458
  27.9 5.5 %collective-permute-start.3 = (f32[32,2048]{1,0:T(8,128)S(1)}, f32[32,2048]{1,0:T(8,128)S(1)}, u32[]{:S(2)}, u32[]{:S(2)}) collective-permute-start(f32[32,2048]{1,0:T(8,128)S(1)} %collective-permute-done.2.refs_4_.refs_2_), channel_id=1, source_target_pairs={{0,2},{1,15},{2,4},{3,1},{4,6},{5,3},{6,8},{7,5},{8,10},{9,7},{10,... | collective-permute-start | bytes 786440 | tf_op jit(solution)/shard_map/ppermute | solution.py:455
  34.8 6.1 %collective-permute-start.15 = (f32[32,2048]{1,0:T(8,128)S(1)}, f32[32,2048]{1,0:T(8,128)S(1)}, u32[]{:S(2)}, u32[]{:S(2)}) collective-permute-start(f32[32,2048]{1,0:T(8,128)S(1)} %collective-permute-done.9.refs_5_.refs_3_), channel_id=1, source_target_pairs={{0,1},{1,0},{2,3},{3,2},{4,5},{5,4},{6,7},{7,6},{8,9},{9,8},{10,11... | collective-permute-start | bytes 786440 | tf_op jit(solution)/shard_map/ppermute | solution.py:458
  37.1 3.7 %collective-permute-start.17 = (f32[32,2048]{1,0:T(8,128)S(1)}, f32[32,2048]{1,0:T(8,128)S(1)}, u32[]{:S(2)}, u32[]{:S(2)}) collective-permute-start(f32[32,2048]{1,0:T(8,128)S(1)} %collective-permute-done.3.refs_6_), channel_id=1, source_target_pairs={{0,1},{1,0},{2,3},{3,2},{4,5},{5,4},{6,7},{7,6},{8,9},{9,8},{10,11... | collective-permute-start | bytes 786440 | tf_op jit(solution)/shard_map/ppermute | solution.py:458
  37.2 7.2 %collective-permute-start.12 = (f32[96,128]{1,0:T(8,128)S(1)}, f32[96,128]{1,0:T(8,128)S(1)}, u32[]{:S(2)}, u32[]{:S(2)}) collective-permute-start(f32[96,128]{1,0:T(8,128)S(1)} %gram_part.1), channel_id=1, source_target_pairs={{0,48},{16,0},{32,16},{48,32},{64,112},{80,64},{96,80},{112,96},{1... | collective-permute-start | bytes 147464 | tf_op jit(solution)/shard_map/ppermute | solution.py:231
  39.7 4.8 %collective-permute-start.11 = (f32[96,128]{1,0:T(8,128)S(1)}, f32[96,128]{1,0:T(8,128)S(1)}, u32[]{:S(2)}, u32[]{:S(2)}) collective-permute-start(f32[96,128]{1,0:T(8,128)S(1)} %gram_part.1), channel_id=1, source_target_pairs={{0,32},{16,48},{32,0},{48,16},{64,96},{80,112},{96,64},{112,80},{1... | collective-permute-start | bytes 147464 | tf_op jit(solution)/shard_map/ppermute | solution.py:231
  40.2 4.5 %collective-permute-start.10 = (f32[96,128]{1,0:T(8,128)S(1)}, f32[96,128]{1,0:T(8,128)S(1)}, u32[]{:S(2)}, u32[]{:S(2)}) collective-permute-start(f32[96,128]{1,0:T(8,128)S(1)} %gram_part.1), channel_id=1, source_target_pairs={{0,16},{16,32},{32,48},{48,0},{64,80},{80,96},{96,112},{112,64},{1... | collective-permute-start | bytes 147464 | tf_op jit(solution)/shard_map/ppermute | solution.py:231
  44.7 7.1 %collective-permute-start.20 = (f32[96,128]{1,0:T(8,128)S(1)}, f32[96,128]{1,0:T(8,128)S(1)}, u32[]{:S(2)}, u32[]{:S(2)}) collective-permute-start(f32[96,128]{1,0:T(8,128)S(1)} %add_add_fusion.3), channel_id=1, source_target_pairs={{0,192},{16,208},{32,224},{48,240},{64,0},{80,16},{96,32},{112,48}... | collective-permute-start | bytes 147464 | tf_op jit(solution)/shard_map/ppermute | solution.py:231
  47.5 5.1 %collective-permute-start.19 = (f32[96,128]{1,0:T(8,128)S(1)}, f32[96,128]{1,0:T(8,128)S(1)}, u32[]{:S(2)}, u32[]{:S(2)}) collective-permute-start(f32[96,128]{1,0:T(8,128)S(1)} %add_add_fusion.3), channel_id=1, source_target_pairs={{0,128},{16,144},{32,160},{48,176},{64,192},{80,208},{96,224},{112... | collective-permute-start | bytes 147464 | tf_op jit(solution)/shard_map/ppermute | solution.py:231
  47.9 4.7 %collective-permute-start.18 = (f32[96,128]{1,0:T(8,128)S(1)}, f32[96,128]{1,0:T(8,128)S(1)}, u32[]{:S(2)}, u32[]{:S(2)}) collective-permute-start(f32[96,128]{1,0:T(8,128)S(1)} %add_add_fusion.3), channel_id=1, source_target_pairs={{0,64},{16,80},{32,96},{48,112},{64,128},{80,144},{96,160},{112,17... | collective-permute-start | bytes 147464 | tf_op jit(solution)/shard_map/ppermute | solution.py:231
  48.7 23.6 %collective-permute-start.21 = (f32[128,512]{1,0:T(8,128)S(1)}, f32[128,512]{1,0:T(8,128)S(1)}, u32[]{:S(2)}, u32[]{:S(2)}) collective-permute-start(f32[128,512]{1,0:T(8,128)S(1)} %get-tuple-element.52), channel_id=1, source_target_pairs={{0,16},{16,32},{32,48},{48,0},{64,80},{80,96},{96,112},{112,64},{1... | collective-permute-start | bytes 786440 | tf_op jit(solution)/shard_map/ppermute | solution.py:479
  50.1 22.2 %collective-permute-start.22 = (f32[128,512]{1,0:T(8,128)S(1)}, f32[128,512]{1,0:T(8,128)S(1)}, u32[]{:S(2)}, u32[]{:S(2)}) collective-permute-start(f32[128,512]{1,0:T(8,128)S(1)} %get-tuple-element.53), channel_id=1, source_target_pairs={{0,32},{16,48},{32,0},{48,16},{64,96},{80,112},{96,64},{112,80},{1... | collective-permute-start | bytes 786440 | tf_op jit(solution)/shard_map/ppermute | solution.py:479
  51.8 20.4 %collective-permute-start.23 = (f32[128,512]{1,0:T(8,128)S(1)}, f32[128,512]{1,0:T(8,128)S(1)}, u32[]{:S(2)}, u32[]{:S(2)}) collective-permute-start(f32[128,512]{1,0:T(8,128)S(1)} %get-tuple-element.54), channel_id=1, source_target_pairs={{0,48},{16,0},{32,16},{48,32},{64,112},{80,64},{96,80},{112,96},{1... | collective-permute-start | bytes 786440 | tf_op jit(solution)/shard_map/ppermute | solution.py:479
  72.4 13.7 %collective-permute-start.26 = (f32[128,512]{1,0:T(8,128)S(1)}, f32[128,512]{1,0:T(8,128)S(1)}, u32[]{:S(2)}, u32[]{:S(2)}) collective-permute-start(f32[128,512]{1,0:T(8,128)S(1)} %add_add_fusion.1), channel_id=1, source_target_pairs={{0,128},{16,144},{32,160},{48,176},{64,192},{80,208},{96,224},{112... | collective-permute-start | bytes 786440 | tf_op jit(solution)/shard_map/ppermute | solution.py:231
  73.9 13.9 %collective-permute-start.25 = (f32[128,512]{1,0:T(8,128)S(1)}, f32[128,512]{1,0:T(8,128)S(1)}, u32[]{:S(2)}, u32[]{:S(2)}) collective-permute-start(f32[128,512]{1,0:T(8,128)S(1)} %add_add_fusion.1), channel_id=1, source_target_pairs={{0,64},{16,80},{32,96},{48,112},{64,128},{80,144},{96,160},{112,17... | collective-permute-start | bytes 786440 | tf_op jit(solution)/shard_map/ppermute | solution.py:231
  74.8 13.0 %collective-permute-start.24 = (f32[128,512]{1,0:T(8,128)S(1)}, f32[128,512]{1,0:T(8,128)S(1)}, u32[]{:S(2)}, u32[]{:S(2)}) collective-permute-start(f32[128,512]{1,0:T(8,128)S(1)} %add_add_fusion.1), channel_id=1, source_target_pairs={{0,192},{16,208},{32,224},{48,240},{64,0},{80,16},{96,32},{112,48}... | collective-permute-start | bytes 786440 | tf_op jit(solution)/shard_map/ppermute | solution.py:231
  87.9 13.4 %collective-permute-start.29 = (f32[128,512]{1,0:T(8,128)S(1)}, f32[128,512]{1,0:T(8,128)S(1)}, u32[]{:S(2)}, u32[]{:S(2)}) collective-permute-start(f32[128,512]{1,0:T(8,128)S(1)} %add_add_fusion.refs_4_), channel_id=1, source_target_pairs={{0,32},{16,48},{32,0},{48,16},{64,96},{80,112},{96,64},{112,80},{1... | collective-permute-start | bytes 786440 | tf_op jit(solution)/shard_map/ppermute | solution.py:231
  89.5 13.8 %collective-permute-start.28 = (f32[128,512]{1,0:T(8,128)S(1)}, f32[128,512]{1,0:T(8,128)S(1)}, u32[]{:S(2)}, u32[]{:S(2)}) collective-permute-start(f32[128,512]{1,0:T(8,128)S(1)} %add_add_fusion.refs_4_), channel_id=1, source_target_pairs={{0,16},{16,32},{32,48},{48,0},{64,80},{80,96},{96,112},{112,64},{1... | collective-permute-start | bytes 786440 | tf_op jit(solution)/shard_map/ppermute | solution.py:231
  89.9 13.5 %collective-permute-start.27 = (f32[128,512]{1,0:T(8,128)S(1)}, f32[128,512]{1,0:T(8,128)S(1)}, u32[]{:S(2)}, u32[]{:S(2)}) collective-permute-start(f32[128,512]{1,0:T(8,128)S(1)} %add_add_fusion.refs_4_), channel_id=1, source_target_pairs={{0,48},{16,0},{32,16},{48,32},{64,112},{80,64},{96,80},{112,96},{1... | collective-permute-start | bytes 786440 | tf_op jit(solution)/shard_map/ppermute | solution.py:231
  92.2 11.1 %copy-start = (f32[2048,512]{1,0:T(8,128)S(1)}, f32[2048,512]{1,0:T(8,128)}, u32[]{:S(2)}) copy-start(f32[2048,512]{1,0:T(8,128)} %refs_12_.1) | copy-start | bytes 12582916
  92.2 11.1 %copy-start.1 = (bf16[2048,256]{1,0:T(8,128)(2,1)S(1)}, bf16[2048,256]{1,0:T(8,128)(2,1)}, u32[]{:S(2)}) copy-start(bf16[2048,256]{1,0:T(8,128)(2,1)} %get-tuple-element.56.refs_9_) | copy-start | bytes 3145732
  92.2 11.1 %copy-start.2 = (bf16[2048,256]{1,0:T(8,128)(2,1)S(1)}, bf16[2048,256]{1,0:T(8,128)(2,1)}, u32[]{:S(2)}) copy-start(bf16[2048,256]{1,0:T(8,128)(2,1)} %get-tuple-element.58.refs_11_) | copy-start | bytes 3145732
  92.2 11.1 %copy-start.3 = (bf16[2048,256]{1,0:T(8,128)(2,1)S(1)}, bf16[2048,256]{1,0:T(8,128)(2,1)}, u32[]{:S(2)}) copy-start(bf16[2048,256]{1,0:T(8,128)(2,1)} %get-tuple-element.55.refs_8_) | copy-start | bytes 3145732
  92.2 11.1 %copy-start.4 = (bf16[2048,256]{1,0:T(8,128)(2,1)S(1)}, bf16[2048,256]{1,0:T(8,128)(2,1)}, u32[]{:S(2)}) copy-start(bf16[2048,256]{1,0:T(8,128)(2,1)} %get-tuple-element.57.refs_10_) | copy-start | bytes 3145732
